TPU v7x, 32 devices: a whole 2x2x4 slice. The times are simulated.
32 devices in a mesh: groups: 2 (over y), elem: 4 (over z), sub: 2 (over x), col: 2 (over core).
Axes of the slice: x: 2, y: 2, z: 4, core: 2. Of those that a mesh axis runs over, the one named last changes fastest.
Arguments:
- jacobian: bfloat16 [1536, 20480], P(('groups', 'elem', 'sub')), parts along dimension 0, may hold values from -0.75 to 0.75
- prolong: bfloat16 [64, 98304], P('col', ('groups', 'elem', 'sub')), parts along dimension 1, may hold values from -5 to 5
- face_pattern: int32 [1536, 4], P(('groups', 'elem', 'sub')), parts along dimension 0, may hold values from -1 to 767, as said below
- owner: int32 [1536, 1], P(('groups', 'elem', 'sub')), parts along dimension 0, may hold values from 0 to 7; in each aligned block of 96 rows (0 to 95, 96 to 191, ...) at most 24 rows name the same one
- member: int32 [1536], P(('groups', 'elem', 'sub')), parts along dimension 0, may hold values from 0 to 11
- coarse_slot: int32 [1536, 5], P(('groups', 'elem', 'sub')), parts along dimension 0, may hold values from 0 to 8
Outputs:
- coarse: float32 [64, 192, 576], P('col', ('groups', 'elem', 'sub')), parts along dimension 1
There are 2 independent parts, one for each index of `groups`. A program takes and returns all parts, laid end to end along the dimension named above; each array names one. Nothing has to cross between parts.
Inputs may be any that keep to these rules, and one draw needn't show every extreme that they name: `face_pattern`: face 0 of each of the first 24 elements of a device names one of the last 24 elements of the previous device (-1 on the first device); face 1 of each of the last 24 names one of the first 24 elements of the next device (-1 on the last); every other face names another element of the same device. Among the 96 elements of one device, at most 24 name the same owner.
All inputs are finite; a program needn't handle non-finite values.
Results may differ from a plain program's by a relative error of at most 0.0029.
Values may be sent and summed in bfloat16 or wider, within the bound.
No kernel may reach another device: no remote copies, remote signals or barrier semaphores. Data moves between devices by JAX's collectives and lax.ppermute only.
A program may use at most 128 MiB of HBM per device.

v0:
```python
import functools

import jax
import jax.numpy as jnp
from jax import lax
from jax.experimental import pallas as pl
from jax.experimental.pallas import tpu as pltpu
from jax.sharding import PartitionSpec as P

B = 64
CB = 64
FACES = 4
CS = 9
AGG_DEV = 12
BLOCKS = AGG_DEV * CS
PAIRS = BLOCKS // 2
STEP = 16
UNROLL = 8
VMEM = pl.BlockSpec(memory_space=pltpu.VMEM)
SMEM = pl.BlockSpec(memory_space=pltpu.SMEM)
NT = (((1,), (1,)), ((), ()))


def params(mib=16):
    return pltpu.CompilerParams(vmem_limit_bytes=mib * 1024 * 1024)


def halo(cells, width):
    axes = ("elem", "sub")
    count = lax.axis_size(axes)
    up = [(i, i + 1) for i in range(count - 1)]
    down = [(i + 1, i) for i in range(count - 1)]
    return (
        lax.ppermute(cells[:, -width:], axes, up),
        lax.ppermute(cells[:, :width], axes, down),
    )


def halo_swaps(cells, width):
    axes = ("elem", "sub")
    count = lax.axis_size(axes)
    even = lax.axis_index(axes) % 2 == 0
    tail, head = cells[:, -width:], cells[:, :width]

    def swap(block, first):
        pairs = [(i, i + 1) for i in range(first, count - 1, 2)]
        return lax.ppermute(block, axes, pairs + [(j, i) for i, j in pairs])

    return swap(jnp.where(even, tail, head), 0), swap(jnp.where(even, head, tail), 1)


MEMBER, SLOT, FACE = 1, 2, 3 + FACES


def place_of(z, dest):
    return 3 - (z ^ dest)


def call_plan(count):
    sent = [(p, 0) for p in range(count)]
    kept = [(p, 1) for p in range(count)]
    return [sent[:1], sent[1:] + kept]


def group_lists(elems, count, ints_ref, list_ref, count_ref, call_ref):
    me = lax.axis_index("sub")
    z = lax.axis_index("elem")
    plan = call_plan(count)
    code = {table: (c, t) for c, tables in enumerate(plan) for t, table in enumerate(tables)}
    for d in range(count):
        for x in range(2):
            values = [0, 0]
            for y in range(count):
                for mine in range(2):
                    here = (z == y) & ((me == x) if mine else (me != x))
                    for i in range(2):
                        values[i] = jnp.where(here, code[place_of(y, d), mine][i], values[i])
            call_ref[0, 2 * d + x] = values[0]
            call_ref[1, 2 * d + x] = values[1]
    for call in range(len(plan)):
        count_ref[call] = 0

    def put(e, carry):
        owner = ints_ref[0, e]
        call = call_ref[0, owner]
        at = count_ref[call]
        list_ref[call, at] = 8 * e + call_ref[1, owner]
        count_ref[call] = at + 1
        return carry

    lax.fori_loop(0, elems, put, 0, unroll=4)


def near_kernel(elems, count, ints_ref, cells_ref, other_ref, near_ref, weight_ref, list_ref, count_ref, call_ref):
    group_lists(elems, count, ints_ref, list_ref, count_ref, call_ref)
    near_blocks(near_ref, 0, cells_ref)
    col = lax.axis_index("col")
    own_weights(weight_ref, col, cells_ref)
    own_weights(weight_ref, 1 - col, other_ref)


def rows_kernel(jac_ref, after_ref, rows_ref):
    width = 2048

    def step(i, carry):
        at = pl.ds(pl.multiple_of(i * STEP, STEP), STEP)
        for q in range(jac_ref.shape[1] // width):
            part = jac_ref[at, q * width:(q + 1) * width]
            rows_ref[at, q * 16:(q + 1) * 16] = pltpu.einshape("a(bc)->abc", part, b=16, c=128)
        return carry

    lax.fori_loop(0, jac_ref.shape[0] // STEP, step, 0)


def accumulate(call, trash, rim, ints_ref, list_ref, count_ref, rows_ref, near_ref, weight_ref, total):
    low = lax.broadcasted_iota(jnp.int32, (32, 128), 1) < B
    high = jnp.where(low, 0, 1)
    number = count_ref[call]
    device = lax.axis_index("elem") * lax.axis_size("sub") + lax.axis_index("sub")
    first_row = device * 4 * rim - rim
    absent = near_ref.shape[0] - 1
    total[...] = jnp.zeros_like(total)

    def body(it, carry):
        items = []
        for u in range(UNROLL):
            at = it * UNROLL + u
            valid = at < number
            entry = jnp.where(valid, list_ref[call, at], 0)
            e = entry >> 3
            items.append((valid, e, ints_ref[MEMBER, e] * CS + (entry & (7)) * BLOCKS))
        products = []
        for valid, e, base in items:
            parts = []
            for j in range(FACES + 1):
                if j == 0:
                    cell = e + rim
                else:
                    face = ints_ref[FACE + j - 1, e]
                    cell = jnp.where(face >= 0, face - first_row, absent)
                block = rows_ref[e, j * 32:(j + 1) * 32, :]
                zero = jnp.zeros_like(block)
                weights = jnp.concatenate([jnp.where(low, block, zero), jnp.where(low, zero, block)], axis=0)
                parts.append(lax.dot_general(near_ref[cell], weights, NT, preferred_element_type=jnp.float32))
            products.append(jnp.concatenate(parts, axis=0).astype(jnp.bfloat16))
        results = []
        for (valid, e, base), product in zip(items, products):
            own = weight_ref[e]
            own = jnp.concatenate([own, own], axis=0)
            results.append(lax.dot_general(product, own, NT, preferred_element_type=jnp.float32))
        for (valid, e, base), result in zip(items, results):
            for j in range(FACES + 1):
                target = jnp.where(valid, base + ints_ref[SLOT + j, e], 2 * trash)
                part = result[j * 32:(j + 1) * 32, :]
                total[target >> 1] += jnp.where(high == (target & 1), part, 0.0)
        return carry

    lax.fori_loop(0, (number + UNROLL - 1) // UNROLL, body, 0)


def near_blocks(near_ref, base, cells_ref):
    low = lax.broadcasted_iota(jnp.int32, (32, 128), 1) < B
    for p in range(cells_ref.shape[1] // 128):
        pair = cells_ref[:, p * 128:(p + 1) * 128].astype(jnp.float32)
        turned = pltpu.roll(pair, B, 1)
        near_ref[base + 2 * p] = jnp.where(low, pair, turned).astype(jnp.bfloat16)
        near_ref[base + 2 * p + 1] = jnp.where(low, turned, pair).astype(jnp.bfloat16)


def own_weights(weight_ref, side, cells_ref):
    row = lax.broadcasted_iota(jnp.int32, (128, B), 0)
    col = lax.broadcasted_iota(jnp.int32, (128, B), 1)
    source = 2 * (col % 32) + col // 32
    picks = [jnp.where(row == source + h * B, 1.0, 0.0).astype(jnp.bfloat16) for h in range(2)]
    at = pl.ds(pl.multiple_of(side * 32, 32), 32)
    for p in range(cells_ref.shape[1] // 128):
        pair = cells_ref[:, p * 128:(p + 1) * 128]
        for h in range(2):
            moved = jnp.dot(pair, picks[h], preferred_element_type=jnp.float32)
            weight_ref[2 * p + h, at, :] = moved.astype(jnp.bfloat16)


def first_kernel(elems, ints_ref, list_ref, count_ref, rows_ref, own_ref, weight_ref, one_ref, two_ref,
                 sent_ref, near_ref, total):
    rim = elems // 4
    device = lax.axis_index("elem") * lax.axis_size("sub") + lax.axis_index("sub")
    even = device % 2 == 0
    near_ref[rim:rim + elems] = own_ref[...]
    near_blocks(near_ref, jnp.where(even, rim + elems, 0), one_ref)
    near_blocks(near_ref, jnp.where(even, 0, rim + elems), two_ref)
    near_ref[near_ref.shape[0] - 1] = jnp.zeros((32, 128), jnp.bfloat16)
    accumulate(0, PAIRS, rim, ints_ref, list_ref, count_ref, rows_ref, near_ref, weight_ref, total)
    sent_ref[...] = total[:PAIRS].astype(jnp.bfloat16)


def next_kernel(elems, call, ints_ref, list_ref, count_ref, rows_ref, near_ref, weight_ref, after_ref, *rest):
    outs, total = rest[:-1], rest[-1]
    accumulate(call, len(outs) * PAIRS, elems // 4, ints_ref, list_ref, count_ref, rows_ref, near_ref, weight_ref, total)
    for k, out in enumerate(outs):
        out[...] = total[k * PAIRS:(k + 1) * PAIRS].astype(out.dtype)


def last_kernel(own_ref, across_ref, *rest):
    parts, out_ref, total = rest[:-2], rest[-2], rest[-1]
    total[...] = own_ref[...] + across_ref[...].astype(jnp.float32)
    at = 0
    for part in parts:
        total[at:at + part.shape[0]] += part[...].astype(jnp.float32)
        at = (at + part.shape[0]) % PAIRS
    low = lax.broadcasted_iota(jnp.int32, (32, 128), 1) < B
    for a in range(AGG_DEV):
        first = a * CS // 2
        for q in range(CS // 2):
            if a % 2 == 0:
                out_ref[a, :, q * 128:(q + 1) * 128] = total[first + q]
            else:
                out_ref[a, :, q * 128:(q + 1) * 128] = jnp.where(
                    low, pltpu.roll(total[first + q], B, 1), pltpu.roll(total[first + q + 1], B, 1))
        last = total[first + CS // 2]
        if a % 2 == 1:
            last = pltpu.roll(last, B, 1)
        out_ref[a, :, (CS // 2) * 128:] = last[:, :B]


def dense(jacobian, prolong, face_pattern, owner, member, coarse_slot):
    elems = jacobian.shape[0]
    half = prolong.shape[0]
    count = lax.axis_size("elem")
    rim = elems // 4
    tiles = jacobian.shape[1] // 128
    plan = call_plan(count)
    cost = pl.CostEstimate(flops=1000, bytes_accessed=1000, transcendentals=0)

    other = lax.ppermute(prolong, "col", [(0, 1), (1, 0)])
    one, two = halo_swaps(prolong, rim * B)
    ints = jnp.concatenate([owner.T, member[None], coarse_slot.T, face_pattern.T], axis=0)

    long = pl.CostEstimate(flops=20_000_000_000, bytes_accessed=1000, transcendentals=0)
    own_near, weights, lists, counts = pl.pallas_call(
        functools.partial(near_kernel, elems, count),
        in_specs=[SMEM, VMEM, VMEM],
        out_specs=[VMEM, VMEM, SMEM, SMEM],
        out_shape=[
            jax.ShapeDtypeStruct((elems, half, 2 * B), jnp.bfloat16),
            jax.ShapeDtypeStruct((elems, CB, B), jnp.bfloat16),
            jax.ShapeDtypeStruct((len(plan), elems + UNROLL), jnp.int32),
            jax.ShapeDtypeStruct((len(plan),), jnp.int32),
        ],
        scratch_shapes=[pltpu.SMEM((2, 2 * count), jnp.int32)],
        compiler_params=params(),
        cost_estimate=long,
        name="near",
    )(ints, prolong, other)
    rows = pl.pallas_call(
        rows_kernel,
        in_specs=[VMEM, pl.BlockSpec(memory_space=pl.ANY)],
        out_specs=VMEM,
        out_shape=jax.ShapeDtypeStruct((elems, tiles, 128), jnp.bfloat16),
        compiler_params=params(),
        cost_estimate=cost,
        name="rows",
    )(jacobian, own_near)

    table = (PAIRS, half, 2 * B)
    sent, near = pl.pallas_call(
        functools.partial(first_kernel, elems),
        in_specs=[SMEM] * 3 + [VMEM] * 5,
        out_specs=[VMEM] * 2,
        out_shape=[
            jax.ShapeDtypeStruct(table, jnp.bfloat16),
            jax.ShapeDtypeStruct((elems + 2 * rim + 1, half, 2 * B), jnp.bfloat16),
        ],
        scratch_shapes=[pltpu.VMEM((PAIRS + 1, half, 2 * B), jnp.float32)],
        compiler_params=params(),
        cost_estimate=cost,
        name="first",
    )(ints, lists, counts, rows, own_near, weights, one, two)
    arrived = [lax.ppermute(sent, "sub", [(0, 1), (1, 0)])]

    def summed(p, at, more=None):
        value = kept[p][at] + arrived[p][at].astype(jnp.float32)
        if more is not None:
            value = value + more.astype(jnp.float32)
        return value.astype(jnp.bfloat16)

    def swapped(block, bit):
        return lax.ppermute(block, "elem", [(y, y ^ bit) for y in range(count)])

    halves = [slice(0, PAIRS // 2), slice(PAIRS // 2, PAIRS)]
    kept = {}
    for call in range(1, len(plan)):
        shapes = [jax.ShapeDtypeStruct(table, jnp.float32 if mine else jnp.bfloat16) for p, mine in plan[call]]
        outs = pl.pallas_call(
            functools.partial(next_kernel, elems, call),
            in_specs=[SMEM] * 3 + [VMEM] * 3 + [pl.BlockSpec(memory_space=pl.ANY)],
            out_specs=[VMEM] * len(shapes),
            out_shape=shapes,
            scratch_shapes=[pltpu.VMEM((len(shapes) * PAIRS + 1, half, 2 * B), jnp.float32)],
            compiler_params=params(),
            cost_estimate=long,
            name="next_%d" % call,
        )(ints, lists, counts, rows, near, weights, sent)
        for (p, mine), out in zip(plan[call], outs):
            if mine:
                kept[p] = out
        for (p, mine), out in zip(plan[call], outs):
            if not mine:
                if p > 1:
                    out = lax.optimization_barrier((out, arrived[0]))[0]
                if p > 2:
                    first = [summed(0, at) for at in halves]
                    out = lax.optimization_barrier((out, *first))[0]
                arrived.append(lax.ppermute(out, "sub", [(0, 1), (1, 0)]))

    near_sums = [swapped(block, 1) for block in first]
    second = [summed(1, at, more) for at, more in zip(halves, near_sums)]
    arrived[2] = lax.optimization_barrier((arrived[2], *second))[0]
    far_sums = [swapped(block, 2) for block in second]
    pieces = [slice(i * PAIRS // 3, (i + 1) * PAIRS // 3) for i in range(3)]
    next_sums = [swapped(summed(2, at), 1) for at in pieces]

    coarse = pl.pallas_call(
        last_kernel,
        in_specs=[VMEM] * (4 + len(pieces)),
        out_specs=VMEM,
        out_shape=jax.ShapeDtypeStruct((AGG_DEV, half, CS * CB), jnp.float32),
        scratch_shapes=[pltpu.VMEM(table, jnp.float32)],
        compiler_params=params(),
        cost_estimate=cost,
        name="last",
    )(kept[count - 1], arrived[count - 1], *next_sums, *far_sums)
    return coarse.transpose(1, 0, 2)


def direct(jacobian, prolong, face_pattern, owner, member, coarse_slot):
    elems = jacobian.shape[0]
    owners = lax.axis_size(("elem", "sub"))
    capacity = max(2, 2 * elems // owners)
    device = lax.axis_index(("elem", "sub"))
    half = prolong.shape[0]
    rim = elems // 4
    before, after = halo(prolong, rim * B)
    ghosts = jnp.concatenate([before, prolong, after], axis=1).reshape(half, elems + 2 * rim, B)
    whole = lax.all_gather(prolong, "col", axis=0, tiled=True).reshape(CB, elems, B)
    first_row = device * elems - rim
    selfcol = jnp.arange(elems, dtype=jnp.int32)[:, None] + rim
    remote = jnp.where(face_pattern >= 0, face_pattern - first_row, 0)
    columns = jnp.concatenate([selfcol, remote], axis=1)
    present = jnp.concatenate([jnp.ones((elems, 1), jnp.bool_), face_pattern >= 0], axis=1)
    neighbour_rows = ghosts[:, columns, :] * present[None, :, :, None].astype(jnp.bfloat16)
    blocks = jacobian.reshape(elems, FACES + 1, B, B)
    product = jnp.einsum(
        "ejik,cejk->ejic", blocks, neighbour_rows, preferred_element_type=jnp.float32
    ).astype(jnp.bfloat16)
    owner_flat = owner[:, 0]
    marks = (owner_flat[:, None] == jnp.arange(owners, dtype=jnp.int32)[None, :]).astype(jnp.int32)
    ranking = jnp.sum(jnp.cumsum(marks, axis=0) * marks, axis=1) - 1
    place = owner_flat * capacity + ranking
    target = member[:, None] * CS + coarse_slot
    slots = owners * capacity
    labels = jnp.full((slots, FACES + 1), -1, jnp.int32).at[place].set(target)
    contribution = jnp.einsum("rei,ejic->ejcr", whole, product, preferred_element_type=jnp.float32)
    payload = jnp.zeros((slots, FACES + 1, half, CB), jnp.float32).at[place].set(contribution)
    axes = ("elem", "sub")
    arrived = lax.all_to_all(payload, axes, split_axis=0, concat_axis=0, tiled=True)
    arrived_labels = lax.all_to_all(labels, axes, split_axis=0, concat_axis=0, tiled=True)
    items = slots * (FACES + 1)
    values = arrived.reshape(items, half * CB)
    flat_labels = arrived_labels.reshape(items)
    destination = jnp.where(flat_labels >= 0, flat_labels, BLOCKS).astype(jnp.int32)
    summed = jnp.zeros((BLOCKS, half * CB), jnp.float32).at[destination].add(values, mode="drop")
    summed = summed.reshape(AGG_DEV, CS, half, CB).transpose(2, 0, 1, 3)
    return summed.reshape(half, AGG_DEV, CS * CB)


def shards(jacobian, *rest):
    elems = jacobian.shape[0]
    owners = lax.axis_size(("elem", "sub"))
    capacity = max(2, 2 * elems // owners)
    if lax.axis_size("sub") == 2 and lax.axis_size("elem") == 4 and BLOCKS <= capacity * (FACES + 1):
        return dense(jacobian, *rest)
    return direct(jacobian, *rest)


def solution(mesh):
    in_specs = (
        P(("groups", "elem", "sub"), None),
        P("col", ("groups", "elem", "sub")),
        P(("groups", "elem", "sub"), None),
        P(("groups", "elem", "sub"), None),
        P(("groups", "elem", "sub")),
        P(("groups", "elem", "sub"), None),
    )
    out_specs = P("col", ("groups", "elem", "sub"), None)
    return jax.shard_map(shards, mesh=mesh, in_specs=in_specs, out_specs=out_specs, check_vma=False)
```

profile of v0, /device:TPU:0, one launch (start us, length us, event | category | flops | bytes accessed | tf_op | source)
XLA Modules:
  0.0 69.4 jit_solution(1610716747915826866)
XLA Ops:
  0.5 1.0 %broadcast_select_fusion = (bf16[32,1536]{1,0:T(8,128)(2,1)S(1)}, bf16[32,1536]{1,0:T(8,128)(2,1)S(1)}) fusion(pred[]{:T(512)S(6)} %eq.5, bf16[32,6144]{1,0:T(8,128)(2,1)} %cells_ref.1), kind=kLoop, calls=%fused_computation.7 | loop fusion | flops 98304 | bytes 393217 | tf_op jit(solution)/shard_map/jit(_where)/select_n | solution.py:49
  1.4 0.7 collective-permute-start.2
  2.1 5.3 %collective-permute-start.1 = (bf16[32,1536]{1,0:T(8,128)(2,1)S(1)}, bf16[32,1536]{1,0:T(8,128)(2,1)S(1)}, u32[]{:S(2)}, u32[]{:S(2)}) collective-permute-start(bf16[32,1536]{1,0:T(8,128)(2,1)S(1)} %get-tuple-element.47), channel_id=1, source_target_pairs={{0,2},{4,6},{8,10},{12,14},{2,0},{6,4},{10,8},{14,12},{1,3},{5,7},... | collective-permute-start | bytes 294920 | tf_op jit(solution)/shard_map/ppermute | solution.py:47
  7.4 0.7 %pad_add_fusion.ints_ref = s32[11,96]{1,0:T(8,128)S(1)} fusion(s32[4,96]{1,0:T(4,128)} %bitcast.6, s32[5,96]{1,0:T(8,128)} %bitcast.5, s32[1,96]{1,0:T(1,128)} %bitcast.7, s32[1,96]{1,0:T(1,128)} %bitcast.8), kind=kLoop, calls=%fused_computation.9 | loop fusion | flops 3168 | bytes 8448 | tf_op jit(solution)/shard_map/concatenate | solution.py:236
  8.2 1.1 %copy-done.1 = bf16[32,6144]{1,0:T(8,128)(2,1)S(1)} copy-done((bf16[32,6144]{1,0:T(8,128)(2,1)S(1)}, bf16[32,6144]{1,0:T(8,128)(2,1)}, u32[]{:S(2)}) %copy-start.1) | copy-done | bytes 393240
  9.3 3.6 %near.1 = (bf16[96,32,128]{2,1,0:T(8,128)(2,1)S(1)}, bf16[96,64,64]{2,1,0:T(8,128)(2,1)S(1)}, s32[2,104]{1,0:T(2,128)S(1)}, s32[2]{0:T(128)S(1)}) custom-call(s32[11,96]{1,0:T(8,128)S(1)} %pad_add_fusion.ints_ref, bf16[32,6144]{1,0:T(8,128)(2,1)S(1)} %copy-done.1, bf16[32,6144]{1,0:T(8,128)(2,1)S(1)} %collective-permute-done.other_ref), custom_call_target="tpu_custom_call" | custom-call | flops 20000000000 | bytes 1000 | tf_op jit(solution)/shard_map/near/pallas_call | solution.py:239
  12.9 1.3 %rows.1.rows_ref = bf16[96,160,128]{2,1,0:T(8,128)(2,1)S(1)} custom-call(bf16[96,20480]{1,0:T(8,128)(2,1)S(1)} %copy-done, bf16[96,32,128]{2,1,0:T(8,128)(2,1)S(1)} %get-tuple-element.24.after_ref.own_ref), custom_call_target="tpu_custom_call" | custom-call | flops 1000 | bytes 1000 | tf_op jit(solution)/shard_map/rows/pallas_call | solution.py:254
  14.3 3.2 %first.1 = (bf16[54,32,128]{2,1,0:T(8,128)(2,1)S(1)}, bf16[145,32,128]{2,1,0:T(8,128)(2,1)S(1)}) custom-call(s32[11,96]{1,0:T(8,128)S(1)} %pad_add_fusion.ints_ref, s32[2,104]{1,0:T(2,128)S(1)} %get-tuple-element.22.list_ref, s32[2]{0:T(128)S(1)} %get-tuple-element.23.count_ref, bf16[96,160,128]{2,1,0:T(8,128)(2,1)S(1)} %rows.1.rows_ref, ...), custom_call_target="tpu_custom_call" | custom-call | flops 1000 | bytes 1000 | tf_op jit(solution)/shard_map/first/pallas_call | solution.py:265
  17.5 8.1 %next_1.1 = (bf16[54,32,128]{2,1,0:T(8,128)(2,1)S(1)}, bf16[54,32,128]{2,1,0:T(8,128)(2,1)S(1)}, bf16[54,32,128]{2,1,0:T(8,128)(2,1)S(1)}, f32[54,32,128]{2,1,0:...) custom-call(s32[11,96]{1,0:T(8,128)S(1)} %pad_add_fusion.ints_ref, ...), custom_call_target="tpu_custom_call" | custom-call | flops 20000000000 | bytes 1000 | tf_op jit(solution)/shard_map/next_1/pallas_call | solution.py:293
  25.6 3.6 %collective-permute-start.6 = (bf16[54,32,128]{2,1,0:T(8,128)(2,1)S(1)}, bf16[54,32,128]{2,1,0:T(8,128)(2,1)S(1)}, u32[]{:S(2)}, u32[]{:S(2)}) collective-permute-start(bf16[54,32,128]{2,1,0:T(8,128)(2,1)S(1)} %get-tuple-element.37), channel_id=1, source_target_pairs={{0,2},{2,0},{1,3},{3,1},{4,6},{6,4},{5,7},{7,5},{8,10},{10,8},{9,1... | collective-permute-start | bytes 1327112 | tf_op jit(solution)/shard_map/ppermute | solution.py:313
  29.7 1.4 %collective-permute-start.8 = (bf16[27,32,128]{2,1,0:T(8,128)(2,1)S(1)}, bf16[27,32,128]{2,1,0:T(8,128)(2,1)S(1)}, u32[]{:S(2)}, u32[]{:S(2)}) collective-permute-start(bf16[27,32,128]{2,1,0:T(8,128)(2,1)S(1)} %get-tuple-element.44), channel_id=1, source_target_pairs={{0,4},{4,0},{8,12},{12,8},{1,5},{5,1},{9,13},{13,9},{2,6},{6,2},{1... | collective-permute-start | bytes 663560 | tf_op jit(solution)/shard_map/ppermute | solution.py:287
  31.1 0.7 collective-permute-start.7
  32.0 1.7 %collective-permute-start.4 = (bf16[54,32,128]{2,1,0:T(8,128)(2,1)S(1)}, bf16[54,32,128]{2,1,0:T(8,128)(2,1)S(1)}, u32[]{:S(2)}, u32[]{:S(2)}) collective-permute-start(bf16[54,32,128]{2,1,0:T(8,128)(2,1)S(1)} %get-tuple-element.32), channel_id=1, source_target_pairs={{0,2},{2,0},{1,3},{3,1},{4,6},{6,4},{5,7},{7,5},{8,10},{10,8},{9,1... | collective-permute-start | bytes 1327112 | tf_op jit(solution)/shard_map/ppermute | solution.py:313
  33.8 6.4 %collective-permute-done.6 = bf16[54,32,128]{2,1,0:T(8,128)(2,1)S(1)} collective-permute-done((bf16[54,32,128]{2,1,0:T(8,128)(2,1)S(1)}, bf16[54,32,128]{2,1,0:T(8,128)(2,1)S(1)}, u32[]{:S(2)}, u32[]{:S(2)}) %collective-permute-start.6) | collective-permute-done | bytes 442400 | tf_op jit(solution)/shard_map/ppermute | solution.py:313
  40.2 0.7 collective-permute-done.7
  41.1 2.7 %collective-permute-start.13 = (bf16[27,32,128]{2,1,0:T(8,128)(2,1)S(1)}, bf16[27,32,128]{2,1,0:T(8,128)(2,1)S(1)}, u32[]{:S(2)}, u32[]{:S(2)}) collective-permute-start(bf16[27,32,128]{2,1,0:T(8,128)(2,1)S(1)} %get-tuple-element.42), channel_id=1, source_target_pairs={{0,8},{4,12},{8,0},{12,4},{1,9},{5,13},{9,1},{13,5},{2,10},{6,14},... | collective-permute-start | bytes 663560 | tf_op jit(solution)/shard_map/ppermute | solution.py:287
  44.1 5.6 %collective-permute-done.5 = bf16[54,32,128]{2,1,0:T(8,128)(2,1)S(1)} collective-permute-done((bf16[54,32,128]{2,1,0:T(8,128)(2,1)S(1)}, bf16[54,32,128]{2,1,0:T(8,128)(2,1)S(1)}, u32[]{:S(2)}, u32[]{:S(2)}) %collective-permute-start.5) | collective-permute-done | bytes 442400 | tf_op jit(solution)/shard_map/ppermute | solution.py:313
  49.8 1.7 %collective-permute-start.11 = (bf16[18,32,128]{2,1,0:T(8,128)(2,1)S(1)}, bf16[18,32,128]{2,1,0:T(8,128)(2,1)S(1)}, u32[]{:S(2)}, u32[]{:S(2)}) collective-permute-start(bf16[18,32,128]{2,1,0:T(8,128)(2,1)S(1)} %get-tuple-element.39), channel_id=1, source_target_pairs={{0,4},{4,0},{8,12},{12,8},{1,5},{5,1},{9,13},{13,9},{2,6},{6,2},{1... | collective-permute-start | bytes 442376 | tf_op jit(solution)/shard_map/ppermute | solution.py:287
  51.9 6.7 %collective-permute-done.13.rest_4_ = bf16[27,32,128]{2,1,0:T(8,128)(2,1)S(1)} collective-permute-done((bf16[27,32,128]{2,1,0:T(8,128)(2,1)S(1)}, bf16[27,32,128]{2,1,0:T(8,128)(2,1)S(1)}, u32[]{:S(2)}, u32[]{:S(2)}) %collective-permute-start.13) | collective-permute-done | bytes 221216 | tf_op jit(solution)/shard_map/ppermute | solution.py:287
  58.6 3.2 %collective-permute-done.12.rest_3_ = bf16[27,32,128]{2,1,0:T(8,128)(2,1)S(1)} collective-permute-done((bf16[27,32,128]{2,1,0:T(8,128)(2,1)S(1)}, bf16[27,32,128]{2,1,0:T(8,128)(2,1)S(1)}, u32[]{:S(2)}, u32[]{:S(2)}) %collective-permute-start.12) | collective-permute-done | bytes 221216 | tf_op jit(solution)/shard_map/ppermute | solution.py:287
  61.9 2.5 %collective-permute-done.11.rest_2_ = bf16[18,32,128]{2,1,0:T(8,128)(2,1)S(1)} collective-permute-done((bf16[18,32,128]{2,1,0:T(8,128)(2,1)S(1)}, bf16[18,32,128]{2,1,0:T(8,128)(2,1)S(1)}, u32[]{:S(2)}, u32[]{:S(2)}) %collective-permute-start.11) | collective-permute-done | bytes 147488 | tf_op jit(solution)/shard_map/ppermute | solution.py:287
  64.4 2.1 %collective-permute-done.10.rest_1_ = bf16[18,32,128]{2,1,0:T(8,128)(2,1)S(1)} collective-permute-done((bf16[18,32,128]{2,1,0:T(8,128)(2,1)S(1)}, bf16[18,32,128]{2,1,0:T(8,128)(2,1)S(1)}, u32[]{:S(2)}, u32[]{:S(2)}) %collective-permute-start.10) | collective-permute-done | bytes 147488 | tf_op jit(solution)/shard_map/ppermute | solution.py:287
  66.5 1.6 %collective-permute-done.9.rest_0_ = bf16[18,32,128]{2,1,0:T(8,128)(2,1)S(1)} collective-permute-done((bf16[18,32,128]{2,1,0:T(8,128)(2,1)S(1)}, bf16[18,32,128]{2,1,0:T(8,128)(2,1)S(1)}, u32[]{:S(2)}, u32[]{:S(2)}) %collective-permute-start.9) | collective-permute-done | bytes 147488 | tf_op jit(solution)/shard_map/ppermute | solution.py:287
  68.1 1.3 %last.1 = f32[12,32,576]{2,1,0:T(8,128)} custom-call(f32[54,32,128]{2,1,0:T(8,128)S(1)} %get-tuple-element.28.own_ref, bf16[54,32,128]{2,1,0:T(8,128)(2,1)S(1)} %collective-permute-done.4.across_ref, bf16[18,32,128]{2,1,0:T(8,128)(2,1)S(1)} %collective-permute-done.9.rest_0_, bf16[18,32,128]{2,1,0:T(8,128)(2,1)S(1)} %collective-permute-done.10.rest_1_, ...), custom_call_target="tpu_custom_call" | custom-call | flops 1000 | bytes 1000 | tf_op jit(solution)/shard_map/last/pallas_call | solution.py:322
  (18 shorter events, 2.3 us)
Async XLA Ops:
  0.0 8.2 %collective-permute-start = (bf16[32,6144]{1,0:T(8,128)(2,1)}, bf16[32,6144]{1,0:T(8,128)(2,1)S(1)}, u32[]{:S(2)}, u32[]{:S(2)}) collective-permute-start(bf16[32,6144]{1,0:T(8,128)(2,1)} %cells_ref.1), channel_id=1, source_target_pairs={{0,1},{1,0},{2,3},{3,2},{4,5},{5,4},{6,7},{7,6},{8,9},{9,8},{10,11... | collective-permute-start | bytes 1179656 | tf_op jit(solution)/shard_map/ppermute | solution.py:234
  1.4 12.8 %collective-permute-start.2 = (bf16[32,1536]{1,0:T(8,128)(2,1)S(1)}, bf16[32,1536]{1,0:T(8,128)(2,1)S(1)}, u32[]{:S(2)}, u32[]{:S(2)}) collective-permute-start(bf16[32,1536]{1,0:T(8,128)(2,1)S(1)} %get-tuple-element.46), channel_id=1, source_target_pairs={{2,4},{6,8},{10,12},{4,2},{8,6},{12,10},{3,5},{7,9},{11,13},{5,3},... | collective-permute-start | bytes 294920 | tf_op jit(solution)/shard_map/ppermute | solution.py:47
  2.1 12.2 %collective-permute-start.1 = (bf16[32,1536]{1,0:T(8,128)(2,1)S(1)}, bf16[32,1536]{1,0:T(8,128)(2,1)S(1)}, u32[]{:S(2)}, u32[]{:S(2)}) collective-permute-start(bf16[32,1536]{1,0:T(8,128)(2,1)S(1)} %get-tuple-element.47), channel_id=1, source_target_pairs={{0,2},{4,6},{8,10},{12,14},{2,0},{6,4},{10,8},{14,12},{1,3},{5,7},... | collective-permute-start | bytes 294920 | tf_op jit(solution)/shard_map/ppermute | solution.py:47
  8.2 4.8 %copy-start = (bf16[96,20480]{1,0:T(8,128)(2,1)S(1)}, bf16[96,20480]{1,0:T(8,128)(2,1)}, u32[]{:S(2)}) copy-start(bf16[96,20480]{1,0:T(8,128)(2,1)} %jac_ref.1) | copy-start | bytes 11796484
  8.2 1.1 %copy-start.1 = (bf16[32,6144]{1,0:T(8,128)(2,1)S(1)}, bf16[32,6144]{1,0:T(8,128)(2,1)}, u32[]{:S(2)}) copy-start(bf16[32,6144]{1,0:T(8,128)(2,1)} %cells_ref.1) | copy-start | bytes 1179652
  17.4 12.1 %collective-permute-start.3 = (bf16[54,32,128]{2,1,0:T(8,128)(2,1)S(1)}, bf16[54,32,128]{2,1,0:T(8,128)(2,1)S(1)}, u32[]{:S(2)}, u32[]{:S(2)}) collective-permute-start(bf16[54,32,128]{2,1,0:T(8,128)(2,1)S(1)} %get-tuple-element.27.after_ref), channel_id=1, source_target_pairs={{0,2},{2,0},{1,3},{3,1},{4,6},{6,4},{5,7},{7,5},{8,10},{10,8},{9,1... | collective-permute-start | bytes 1327112 | tf_op jit(solution)/shard_map/ppermute | solution.py:278
  25.6 14.6 %collective-permute-start.6 = (bf16[54,32,128]{2,1,0:T(8,128)(2,1)S(1)}, bf16[54,32,128]{2,1,0:T(8,128)(2,1)S(1)}, u32[]{:S(2)}, u32[]{:S(2)}) collective-permute-start(bf16[54,32,128]{2,1,0:T(8,128)(2,1)S(1)} %get-tuple-element.37), channel_id=1, source_target_pairs={{0,2},{2,0},{1,3},{3,1},{4,6},{6,4},{5,7},{7,5},{8,10},{10,8},{9,1... | collective-permute-start | bytes 1327112 | tf_op jit(solution)/shard_map/ppermute | solution.py:313
  29.7 10.6 %collective-permute-start.8 = (bf16[27,32,128]{2,1,0:T(8,128)(2,1)S(1)}, bf16[27,32,128]{2,1,0:T(8,128)(2,1)S(1)}, u32[]{:S(2)}, u32[]{:S(2)}) collective-permute-start(bf16[27,32,128]{2,1,0:T(8,128)(2,1)S(1)} %get-tuple-element.44), channel_id=1, source_target_pairs={{0,4},{4,0},{8,12},{12,8},{1,5},{5,1},{9,13},{13,9},{2,6},{6,2},{1... | collective-permute-start | bytes 663560 | tf_op jit(solution)/shard_map/ppermute | solution.py:287
  31.1 9.8 %collective-permute-start.7 = (bf16[27,32,128]{2,1,0:T(8,128)(2,1)S(1)}, bf16[27,32,128]{2,1,0:T(8,128)(2,1)S(1)}, u32[]{:S(2)}, u32[]{:S(2)}) collective-permute-start(bf16[27,32,128]{2,1,0:T(8,128)(2,1)S(1)} %get-tuple-element.45), channel_id=1, source_target_pairs={{0,4},{4,0},{8,12},{12,8},{1,5},{5,1},{9,13},{13,9},{2,6},{6,2},{1... | collective-permute-start | bytes 663560 | tf_op jit(solution)/shard_map/ppermute | solution.py:287
  31.8 17.9 %collective-permute-start.5 = (bf16[54,32,128]{2,1,0:T(8,128)(2,1)S(1)}, bf16[54,32,128]{2,1,0:T(8,128)(2,1)S(1)}, u32[]{:S(2)}, u32[]{:S(2)}) collective-permute-start(bf16[54,32,128]{2,1,0:T(8,128)(2,1)S(1)} %get-tuple-element.35), channel_id=1, source_target_pairs={{0,2},{2,0},{1,3},{3,1},{4,6},{6,4},{5,7},{7,5},{8,10},{10,8},{9,1... | collective-permute-start | bytes 1327112 | tf_op jit(solution)/shard_map/ppermute | solution.py:313
  32.0 29.8 %collective-permute-start.4 = (bf16[54,32,128]{2,1,0:T(8,128)(2,1)S(1)}, bf16[54,32,128]{2,1,0:T(8,128)(2,1)S(1)}, u32[]{:S(2)}, u32[]{:S(2)}) collective-permute-start(bf16[54,32,128]{2,1,0:T(8,128)(2,1)S(1)} %get-tuple-element.32), channel_id=1, source_target_pairs={{0,2},{2,0},{1,3},{3,1},{4,6},{6,4},{5,7},{7,5},{8,10},{10,8},{9,1... | collective-permute-start | bytes 1327112 | tf_op jit(solution)/shard_map/ppermute | solution.py:313
  41.1 17.6 %collective-permute-start.13 = (bf16[27,32,128]{2,1,0:T(8,128)(2,1)S(1)}, bf16[27,32,128]{2,1,0:T(8,128)(2,1)S(1)}, u32[]{:S(2)}, u32[]{:S(2)}) collective-permute-start(bf16[27,32,128]{2,1,0:T(8,128)(2,1)S(1)} %get-tuple-element.42), channel_id=1, source_target_pairs={{0,8},{4,12},{8,0},{12,4},{1,9},{5,13},{9,1},{13,5},{2,10},{6,14},... | collective-permute-start | bytes 663560 | tf_op jit(solution)/shard_map/ppermute | solution.py:287
  43.8 18.1 %collective-permute-start.12 = (bf16[27,32,128]{2,1,0:T(8,128)(2,1)S(1)}, bf16[27,32,128]{2,1,0:T(8,128)(2,1)S(1)}, u32[]{:S(2)}, u32[]{:S(2)}) collective-permute-start(bf16[27,32,128]{2,1,0:T(8,128)(2,1)S(1)} %get-tuple-element.43), channel_id=1, source_target_pairs={{0,8},{4,12},{8,0},{12,4},{1,9},{5,13},{9,1},{13,5},{2,10},{6,14},... | collective-permute-start | bytes 663560 | tf_op jit(solution)/shard_map/ppermute | solution.py:287
  49.8 14.5 %collective-permute-start.11 = (bf16[18,32,128]{2,1,0:T(8,128)(2,1)S(1)}, bf16[18,32,128]{2,1,0:T(8,128)(2,1)S(1)}, u32[]{:S(2)}, u32[]{:S(2)}) collective-permute-start(bf16[18,32,128]{2,1,0:T(8,128)(2,1)S(1)} %get-tuple-element.39), channel_id=1, source_target_pairs={{0,4},{4,0},{8,12},{12,8},{1,5},{5,1},{9,13},{13,9},{2,6},{6,2},{1... | collective-permute-start | bytes 442376 | tf_op jit(solution)/shard_map/ppermute | solution.py:287
  51.6 14.9 %collective-permute-start.10 = (bf16[18,32,128]{2,1,0:T(8,128)(2,1)S(1)}, bf16[18,32,128]{2,1,0:T(8,128)(2,1)S(1)}, u32[]{:S(2)}, u32[]{:S(2)}) collective-permute-start(bf16[18,32,128]{2,1,0:T(8,128)(2,1)S(1)} %get-tuple-element.40), channel_id=1, source_target_pairs={{0,4},{4,0},{8,12},{12,8},{1,5},{5,1},{9,13},{13,9},{2,6},{6,2},{1... | collective-permute-start | bytes 442376 | tf_op jit(solution)/shard_map/ppermute | solution.py:287
  58.6 9.4 %collective-permute-start.9 = (bf16[18,32,128]{2,1,0:T(8,128)(2,1)S(1)}, bf16[18,32,128]{2,1,0:T(8,128)(2,1)S(1)}, u32[]{:S(2)}, u32[]{:S(2)}) collective-permute-start(bf16[18,32,128]{2,1,0:T(8,128)(2,1)S(1)} %get-tuple-element.41), channel_id=1, source_target_pairs={{0,4},{4,0},{8,12},{12,8},{1,5},{5,1},{9,13},{13,9},{2,6},{6,2},{1... | collective-permute-start | bytes 442376 | tf_op jit(solution)/shard_map/ppermute | solution.py:287
where the time goes:
time: 69.8 us; the launch traced here: 69.4 us
  waiting for transfers between devices  29.2 us (42%)
  starting transfers between devices  19.3 us (28%)
  Pallas kernels  17.5 us (25%)
  other arithmetic  2.11 us (3%)
  local copies, waits for them, and re-layouts  1.15 us (2%)
    ppermute x7, waiting for transfers between devices, swapped(): return lax.ppermute(block, 'elem', [(y, y ^ bit) for y in range(count)])  16.8 us
    ppermute x3, waiting for transfers between devices, dense(): arrived.append(lax.ppermute(out, 'sub', [(0, 1), (1, 0)]))  12.1 us
    pallas_call x1, Pallas kernels, dense(): pl.pallas_call(functools.partial(next_kernel, elems, call), in_specs=[SME...  8.12 us
    ppermute x7, starting transfers between devices, swapped(): return lax.ppermute(block, 'elem', [(y, y ^ bit) for y in range(count)])  7.17 us
    ppermute x2, starting transfers between devices, swap(): return lax.ppermute(block, axes, pairs + [(j, i) for i, j in pairs])  6.01 us
    ppermute x3, starting transfers between devices, dense(): arrived.append(lax.ppermute(out, 'sub', [(0, 1), (1, 0)]))  5.58 us
    pallas_call x1, Pallas kernels, dense(): pl.pallas_call(functools.partial(near_kernel, elems, count), in_specs=[SM...  3.6 us
    pallas_call x1, Pallas kernels, dense(): pl.pallas_call(functools.partial(first_kernel, elems), in_specs=[SMEM] *...  3.17 us
  transfers between devices with their start and end apart: 14, of which 9 were waited for; matrix products, arithmetic and copies ran while one was open for 3% of the time, Pallas kernels for 19%

commit v1 on v0

--- a/solution.py
+++ b/solution.py
@@ -50,23 +50,30 @@
 
 
 MEMBER, SLOT, FACE = 1, 2, 3 + FACES
+CELL, TARGET = 0, FACES
+LANES = 128
+
+
+ROUNDS = ([(0, 2), (1, 0), (2, 3), (3, 1)], [(0, 1), (1, 3), (2, 0), (3, 2)])
 
 
 def place_of(z, dest):
-    return 3 - (z ^ dest)
+    if dest in (z, z ^ 3):
+        return 3 if dest == z else 0
+    return 1 if (z, dest) in ROUNDS[0] else 2
 
 
 def call_plan(count):
     sent = [(p, 0) for p in range(count)]
     kept = [(p, 1) for p in range(count)]
-    return [sent[:1], sent[1:] + kept]
+    return [sent[:2], sent[2:] + kept]
 
 
 def group_lists(elems, count, ints_ref, list_ref, count_ref, call_ref):
     me = lax.axis_index("sub")
     z = lax.axis_index("elem")
     plan = call_plan(count)
-    code = {table: (c, t) for c, tables in enumerate(plan) for t, table in enumerate(tables)}
+    code = {table: (c, 2 + t * BLOCKS) for c, tables in enumerate(plan) for t, table in enumerate(tables)}
     for d in range(count):
         for x in range(2):
             values = [0, 0]
@@ -76,7 +83,7 @@
                     for i in range(2):
                         values[i] = jnp.where(here, code[place_of(y, d), mine][i], values[i])
             call_ref[0, 2 * d + x] = values[0]
-            call_ref[1, 2 * d + x] = values[1]
+            call_ref[1, 2 * d + x] = LANES * values[1]
     for call in range(len(plan)):
         count_ref[call] = 0
 
@@ -84,14 +91,25 @@
         owner = ints_ref[0, e]
         call = call_ref[0, owner]
         at = count_ref[call]
-        list_ref[call, at] = 8 * e + call_ref[1, owner]
+        list_ref[call, at] = e + call_ref[1, owner]
         count_ref[call] = at + 1
         return carry
 
-    lax.fori_loop(0, elems, put, 0, unroll=4)
-
-
-def near_kernel(elems, count, ints_ref, cells_ref, other_ref, near_ref, weight_ref, list_ref, count_ref, call_ref):
+    lax.fori_loop(0, elems, put, 0, unroll=8)
+    for call in range(len(plan)):
+        for u in range(UNROLL):
+            list_ref[call, count_ref[call] + u] = elems
+
+
+def near_kernel(elems, count, ints_ref, again_ref, cells_ref, other_ref,
+                near_ref, weight_ref, code_ref, list_ref, count_ref, call_ref):
+    device = lax.axis_index("elem") * lax.axis_size("sub") + lax.axis_index("sub")
+    rim = elems // 4
+    faces = again_ref[FACE:FACE + FACES, :]
+    code_ref[...] = jnp.zeros_like(code_ref)
+    code_ref[CELL:CELL + FACES, :elems] = jnp.where(faces >= 0, faces - (device * elems - rim), elems + 2 * rim)
+    code_ref[TARGET:TARGET + FACES + 1, :elems] = (
+        again_ref[MEMBER:MEMBER + 1, :] * CS + again_ref[SLOT:SLOT + FACES + 1, :])
     group_lists(elems, count, ints_ref, list_ref, count_ref, call_ref)
     near_blocks(near_ref, 0, cells_ref)
     col = lax.axis_index("col")
@@ -112,50 +130,41 @@
     lax.fori_loop(0, jac_ref.shape[0] // STEP, step, 0)
 
 
-def accumulate(call, trash, rim, ints_ref, list_ref, count_ref, rows_ref, near_ref, weight_ref, total):
+def accumulate(call, elems, code_ref, list_ref, count_ref, rows_ref, near_ref, weight_ref, total):
     low = lax.broadcasted_iota(jnp.int32, (32, 128), 1) < B
     high = jnp.where(low, 0, 1)
-    number = count_ref[call]
-    device = lax.axis_index("elem") * lax.axis_size("sub") + lax.axis_index("sub")
-    first_row = device * 4 * rim - rim
-    absent = near_ref.shape[0] - 1
     total[...] = jnp.zeros_like(total)
 
     def body(it, carry):
         items = []
         for u in range(UNROLL):
-            at = it * UNROLL + u
-            valid = at < number
-            entry = jnp.where(valid, list_ref[call, at], 0)
-            e = entry >> 3
-            items.append((valid, e, ints_ref[MEMBER, e] * CS + (entry & (7)) * BLOCKS))
+            entry = list_ref[call, it * UNROLL + u]
+            at = entry & (LANES - 1)
+            items.append((at, jnp.minimum(at, elems - 1), entry >> 7))
         products = []
-        for valid, e, base in items:
+        for at, e, base in items:
             parts = []
             for j in range(FACES + 1):
-                if j == 0:
-                    cell = e + rim
-                else:
-                    face = ints_ref[FACE + j - 1, e]
-                    cell = jnp.where(face >= 0, face - first_row, absent)
+                cell = near_ref[e + elems // 4 if j == 0 else code_ref[CELL + j - 1, at]]
+                zero = jnp.zeros_like(cell)
+                both = jnp.concatenate([jnp.where(low, cell, zero), jnp.where(low, zero, cell)], axis=0)
                 block = rows_ref[e, j * 32:(j + 1) * 32, :]
-                zero = jnp.zeros_like(block)
-                weights = jnp.concatenate([jnp.where(low, block, zero), jnp.where(low, zero, block)], axis=0)
-                parts.append(lax.dot_general(near_ref[cell], weights, NT, preferred_element_type=jnp.float32))
+                part = lax.dot_general(both, block, NT, preferred_element_type=jnp.float32)
+                parts.append(jnp.concatenate([part[:32], part[32:]], axis=1))
             products.append(jnp.concatenate(parts, axis=0).astype(jnp.bfloat16))
         results = []
-        for (valid, e, base), product in zip(items, products):
+        for (at, e, base), product in zip(items, products):
             own = weight_ref[e]
             own = jnp.concatenate([own, own], axis=0)
             results.append(lax.dot_general(product, own, NT, preferred_element_type=jnp.float32))
-        for (valid, e, base), result in zip(items, results):
+        for (at, e, base), result in zip(items, results):
             for j in range(FACES + 1):
-                target = jnp.where(valid, base + ints_ref[SLOT + j, e], 2 * trash)
+                target = base + code_ref[TARGET + j, at]
                 part = result[j * 32:(j + 1) * 32, :]
                 total[target >> 1] += jnp.where(high == (target & 1), part, 0.0)
         return carry
 
-    lax.fori_loop(0, (number + UNROLL - 1) // UNROLL, body, 0)
+    lax.fori_loop(0, (count_ref[call] + UNROLL - 1) // UNROLL, body, 0)
 
 
 def near_blocks(near_ref, base, cells_ref):
@@ -180,8 +189,8 @@
             weight_ref[2 * p + h, at, :] = moved.astype(jnp.bfloat16)
 
 
-def first_kernel(elems, ints_ref, list_ref, count_ref, rows_ref, own_ref, weight_ref, one_ref, two_ref,
-                 sent_ref, near_ref, total):
+def first_kernel(elems, code_ref, list_ref, count_ref, rows_ref, own_ref, weight_ref, one_ref, two_ref, *rest):
+    outs, near_ref, total = rest[:-2], rest[-2], rest[-1]
     rim = elems // 4
     device = lax.axis_index("elem") * lax.axis_size("sub") + lax.axis_index("sub")
     even = device % 2 == 0
@@ -189,15 +198,16 @@
     near_blocks(near_ref, jnp.where(even, rim + elems, 0), one_ref)
     near_blocks(near_ref, jnp.where(even, 0, rim + elems), two_ref)
     near_ref[near_ref.shape[0] - 1] = jnp.zeros((32, 128), jnp.bfloat16)
-    accumulate(0, PAIRS, rim, ints_ref, list_ref, count_ref, rows_ref, near_ref, weight_ref, total)
-    sent_ref[...] = total[:PAIRS].astype(jnp.bfloat16)
-
-
-def next_kernel(elems, call, ints_ref, list_ref, count_ref, rows_ref, near_ref, weight_ref, after_ref, *rest):
+    accumulate(0, elems, code_ref, list_ref, count_ref, rows_ref, near_ref, weight_ref, total)
+    for k, out in enumerate(outs):
+        out[...] = total[1 + k * PAIRS:1 + (k + 1) * PAIRS].astype(out.dtype)
+
+
+def next_kernel(elems, call, code_ref, list_ref, count_ref, rows_ref, near_ref, weight_ref, *rest):
     outs, total = rest[:-1], rest[-1]
-    accumulate(call, len(outs) * PAIRS, elems // 4, ints_ref, list_ref, count_ref, rows_ref, near_ref, weight_ref, total)
+    accumulate(call, elems, code_ref, list_ref, count_ref, rows_ref, near_ref, weight_ref, total)
     for k, out in enumerate(outs):
-        out[...] = total[k * PAIRS:(k + 1) * PAIRS].astype(out.dtype)
+        out[...] = total[1 + k * PAIRS:1 + (k + 1) * PAIRS].astype(out.dtype)
 
 
 def last_kernel(own_ref, across_ref, *rest):
@@ -236,13 +246,14 @@
     ints = jnp.concatenate([owner.T, member[None], coarse_slot.T, face_pattern.T], axis=0)
 
     long = pl.CostEstimate(flops=20_000_000_000, bytes_accessed=1000, transcendentals=0)
-    own_near, weights, lists, counts = pl.pallas_call(
+    own_near, weights, codes, lists, counts = pl.pallas_call(
         functools.partial(near_kernel, elems, count),
-        in_specs=[SMEM, VMEM, VMEM],
-        out_specs=[VMEM, VMEM, SMEM, SMEM],
+        in_specs=[SMEM, VMEM, VMEM, VMEM],
+        out_specs=[VMEM, VMEM, VMEM, SMEM, SMEM],
         out_shape=[
             jax.ShapeDtypeStruct((elems, half, 2 * B), jnp.bfloat16),
             jax.ShapeDtypeStruct((elems, CB, B), jnp.bfloat16),
+            jax.ShapeDtypeStruct((16, LANES), jnp.int32),
             jax.ShapeDtypeStruct((len(plan), elems + UNROLL), jnp.int32),
             jax.ShapeDtypeStruct((len(plan),), jnp.int32),
         ],
@@ -250,7 +261,7 @@
         compiler_params=params(),
         cost_estimate=long,
         name="near",
-    )(ints, prolong, other)
+    )(ints, ints, prolong, other)
     rows = pl.pallas_call(
         rows_kernel,
         in_specs=[VMEM, pl.BlockSpec(memory_space=pl.ANY)],
@@ -262,73 +273,66 @@
     )(jacobian, own_near)
 
     table = (PAIRS, half, 2 * B)
-    sent, near = pl.pallas_call(
+    *sent, near = pl.pallas_call(
         functools.partial(first_kernel, elems),
         in_specs=[SMEM] * 3 + [VMEM] * 5,
-        out_specs=[VMEM] * 2,
-        out_shape=[
-            jax.ShapeDtypeStruct(table, jnp.bfloat16),
+        out_specs=[VMEM] * 3,
+        out_shape=[jax.ShapeDtypeStruct(table, jnp.bfloat16)] * 2 + [
             jax.ShapeDtypeStruct((elems + 2 * rim + 1, half, 2 * B), jnp.bfloat16),
         ],
-        scratch_shapes=[pltpu.VMEM((PAIRS + 1, half, 2 * B), jnp.float32)],
+        scratch_shapes=[pltpu.VMEM((1 + 2 * PAIRS, half, 2 * B), jnp.float32)],
         compiler_params=params(),
         cost_estimate=cost,
         name="first",
-    )(ints, lists, counts, rows, own_near, weights, one, two)
-    arrived = [lax.ppermute(sent, "sub", [(0, 1), (1, 0)])]
-
-    def summed(p, at, more=None):
+    )(codes, lists, counts, rows, own_near, weights, one, two)
+    arrived = [lax.ppermute(block, "sub", [(0, 1), (1, 0)]) for block in sent]
+
+    outer = (lax.axis_index("elem") + 1) % 4 < 2
+
+    def summed(p, at, more=None, adds=None):
         value = kept[p][at] + arrived[p][at].astype(jnp.float32)
         if more is not None:
-            value = value + more.astype(jnp.float32)
+            value = value + jnp.where(adds, more.astype(jnp.float32), 0.0)
         return value.astype(jnp.bfloat16)
 
-    def swapped(block, bit):
-        return lax.ppermute(block, "elem", [(y, y ^ bit) for y in range(count)])
+    def sent_to(block, pairs):
+        return lax.ppermute(block, "elem", pairs)
 
     halves = [slice(0, PAIRS // 2), slice(PAIRS // 2, PAIRS)]
-    kept = {}
-    for call in range(1, len(plan)):
-        shapes = [jax.ShapeDtypeStruct(table, jnp.float32 if mine else jnp.bfloat16) for p, mine in plan[call]]
-        outs = pl.pallas_call(
-            functools.partial(next_kernel, elems, call),
-            in_specs=[SMEM] * 3 + [VMEM] * 3 + [pl.BlockSpec(memory_space=pl.ANY)],
-            out_specs=[VMEM] * len(shapes),
-            out_shape=shapes,
-            scratch_shapes=[pltpu.VMEM((len(shapes) * PAIRS + 1, half, 2 * B), jnp.float32)],
-            compiler_params=params(),
-            cost_estimate=long,
-            name="next_%d" % call,
-        )(ints, lists, counts, rows, near, weights, sent)
-        for (p, mine), out in zip(plan[call], outs):
-            if mine:
-                kept[p] = out
-        for (p, mine), out in zip(plan[call], outs):
-            if not mine:
-                if p > 1:
-                    out = lax.optimization_barrier((out, arrived[0]))[0]
-                if p > 2:
-                    first = [summed(0, at) for at in halves]
-                    out = lax.optimization_barrier((out, *first))[0]
-                arrived.append(lax.ppermute(out, "sub", [(0, 1), (1, 0)]))
-
-    near_sums = [swapped(block, 1) for block in first]
-    second = [summed(1, at, more) for at, more in zip(halves, near_sums)]
-    arrived[2] = lax.optimization_barrier((arrived[2], *second))[0]
-    far_sums = [swapped(block, 2) for block in second]
-    pieces = [slice(i * PAIRS // 3, (i + 1) * PAIRS // 3) for i in range(3)]
-    next_sums = [swapped(summed(2, at), 1) for at in pieces]
+    shapes = [jax.ShapeDtypeStruct(table, jnp.float32 if mine else jnp.bfloat16) for p, mine in plan[1]]
+    outs = pl.pallas_call(
+        functools.partial(next_kernel, elems, 1),
+        in_specs=[SMEM] * 3 + [VMEM] * 3,
+        out_specs=[VMEM] * len(shapes),
+        out_shape=shapes,
+        scratch_shapes=[pltpu.VMEM((1 + len(shapes) * PAIRS, half, 2 * B), jnp.float32)],
+        compiler_params=params(),
+        cost_estimate=long,
+        name="next",
+    )(codes, lists, counts, rows, near, weights)
+    sent, kept = outs[:count - 2], outs[count - 2:]
+    first = [summed(0, at) for at in halves]
+    for block in sent:
+        block = lax.optimization_barrier((block, *first))[0]
+        arrived.append(lax.ppermute(block, "sub", [(0, 1), (1, 0)]))
+
+    near_sums = [sent_to(block, [(y, y ^ 1) for y in range(count)]) for block in first]
+    near_sums = jnp.concatenate(near_sums, axis=0)
+    second = summed(1, slice(None), near_sums, outer)
+    arrived[2] = lax.optimization_barrier((arrived[2], second))[0]
+    parts = [sent_to(second, ROUNDS[0])]
+    parts += [sent_to(summed(2, at, near_sums[at], ~outer), ROUNDS[1]) for at in halves]
 
     coarse = pl.pallas_call(
         last_kernel,
-        in_specs=[VMEM] * (4 + len(pieces)),
+        in_specs=[VMEM] * 5,
         out_specs=VMEM,
         out_shape=jax.ShapeDtypeStruct((AGG_DEV, half, CS * CB), jnp.float32),
         scratch_shapes=[pltpu.VMEM(table, jnp.float32)],
         compiler_params=params(),
         cost_estimate=cost,
         name="last",
-    )(kept[count - 1], arrived[count - 1], *next_sums, *far_sums)
+    )(kept[count - 1], arrived[count - 1], *parts)
     return coarse.transpose(1, 0, 2)
 
 

time: 69.8 us -> 67.1 us (0.961)
  waiting for transfers between devices: 29.2 us -> 25.3 us
  other arithmetic: 2.11 us -> 5.4 us
  starting transfers between devices: 19.3 us -> 18 us
  Pallas kernels: 17.5 us -> 16.8 us
    ppermute x11 -> x9, waiting for transfers between devices: 29.2 us -> 25.3 us  [the longest x5 8.73 us: sent_to(): return lax.ppermute(block, 'elem', pairs)]
    convert_element_type x3, other arithmetic: 0.44 us -> 3.73 us  [summed(): return value.astype(jnp.bfloat16)]
    ppermute x2, starting transfers between devices: 6.01 us -> 3.21 us  [swap(): return lax.ppermute(block, axes, pairs + [(j, i) for i, j in pairs])]
    ppermute x11 -> x9, starting transfers between devices: 12.8 us -> 14.3 us  [the longest x5 6.55 us: sent_to(): return lax.ppermute(block, 'elem', pairs)]
    pallas_call x2, Pallas kernels: 9.43 us -> 8.43 us  [the longest x1 7.13 us: dense(): pl.pallas_call(functools.partial(next_kernel, elems, 1), in_specs=[SMEM]...]
  transfers between devices with their start and end apart: 14 -> 12, of which waited for: 9 -> 7; matrix products, arithmetic and copies ran while one was open for 3% -> 8% of each run, Pallas kernels for 19% -> 18%
where the time goes in v1:
time: 67.1 us; the launch traced here: 66.8 us
  waiting for transfers between devices  25.3 us (38%)
  starting transfers between devices  18 us (27%)
  Pallas kernels  16.8 us (25%)
  other arithmetic  5.4 us (8%)
  local copies, waits for them, and re-layouts  1.15 us (2%)
    ppermute x5, waiting for transfers between devices, sent_to(): return lax.ppermute(block, 'elem', pairs)  8.73 us
    ppermute x2, waiting for transfers between devices, dense(): arrived.append(lax.ppermute(block, 'sub', [(0, 1), (1, 0)]))  8.38 us
    ppermute x2, waiting for transfers between devices, dense(): arrived = [lax.ppermute(block, 'sub', [(0, 1), (1, 0)]) for block in sent]  8.23 us
    pallas_call x1, Pallas kernels, dense(): pl.pallas_call(functools.partial(next_kernel, elems, 1), in_specs=[SMEM]...  7.13 us
    ppermute x5, starting transfers between devices, sent_to(): return lax.ppermute(block, 'elem', pairs)  6.55 us
    ppermute x2, starting transfers between devices, dense(): arrived = [lax.ppermute(block, 'sub', [(0, 1), (1, 0)]) for block in sent]  5.53 us
    convert_element_type x3, other arithmetic, summed(): return value.astype(jnp.bfloat16)  3.73 us
    pallas_call x1, Pallas kernels, dense(): pl.pallas_call(functools.partial(near_kernel, elems, count), in_specs=[SM...  3.62 us
  transfers between devices with their start and end apart: 12, of which 7 were waited for; matrix products, arithmetic and copies ran while one was open for 8% of the time, Pallas kernels for 18%

profile of v1, /device:TPU:0, one launch (start us, length us, event | category | flops | bytes accessed | tf_op | source)
XLA Modules:
  0.0 66.8 jit_solution(5111048494178377945)
XLA Ops:
  0.5 1.0 %broadcast_select_fusion = (bf16[32,1536]{1,0:T(8,128)(2,1)S(1)}, bf16[32,1536]{1,0:T(8,128)(2,1)S(1)}) fusion(pred[]{:T(512)S(6)} %eq.6, bf16[32,6144]{1,0:T(8,128)(2,1)} %cells_ref.1), kind=kLoop, calls=%fused_computation.5 | loop fusion | flops 98304 | bytes 393217 | tf_op jit(solution)/shard_map/jit(_where)/select_n | solution.py:49
  1.4 2.6 %collective-permute-start.1 = (bf16[32,1536]{1,0:T(8,128)(2,1)S(1)}, bf16[32,1536]{1,0:T(8,128)(2,1)S(1)}, u32[]{:S(2)}, u32[]{:S(2)}) collective-permute-start(bf16[32,1536]{1,0:T(8,128)(2,1)S(1)} %get-tuple-element.44), channel_id=1, source_target_pairs={{0,2},{4,6},{8,10},{12,14},{2,0},{6,4},{10,8},{14,12},{1,3},{5,7},... | collective-permute-start | bytes 294920 | tf_op jit(solution)/shard_map/ppermute | solution.py:47
  5.4 1.1 %copy-done.1 = bf16[32,6144]{1,0:T(8,128)(2,1)S(1)} copy-done((bf16[32,6144]{1,0:T(8,128)(2,1)S(1)}, bf16[32,6144]{1,0:T(8,128)(2,1)}, u32[]{:S(2)}) %copy-start.1) | copy-done | bytes 393240
  6.5 3.6 %near.1 = (bf16[96,32,128]{2,1,0:T(8,128)(2,1)S(1)}, bf16[96,64,64]{2,1,0:T(8,128)(2,1)S(1)}, s32[16,128]{1,0:T(8,128)S(1)}, s32[2,104]{1,0:T(2,128)S(1)}, s32[2]{0:T(128)S(1)}) custom-call(s32[11,96]{1,0:T(8,128)S(1)} %pad_add_fusion.ints_ref.again_ref, s32[11,96]{1,0:T(8,128)S(1)} %pad_add_fusion.ints_ref.again_ref, bf16[32,6144]{1,0:T(8,128)(2,1)S(1)} %copy-done.1, ...), custom_call_target="tpu_custom_call" | custom-call | flops 20000000000 | bytes 1000 | tf_op jit(solution)/shard_map/near/pallas_call | solution.py:249
  10.2 1.3 %rows.1.rows_ref = bf16[96,160,128]{2,1,0:T(8,128)(2,1)S(1)} custom-call(bf16[96,20480]{1,0:T(8,128)(2,1)S(1)} %copy-done, bf16[96,32,128]{2,1,0:T(8,128)(2,1)S(1)} %get-tuple-element.25.after_ref.own_ref), custom_call_target="tpu_custom_call" | custom-call | flops 1000 | bytes 1000 | tf_op jit(solution)/shard_map/rows/pallas_call | solution.py:265
  11.5 3.5 %first.1 = (bf16[54,32,128]{2,1,0:T(8,128)(2,1)S(1)}, bf16[54,32,128]{2,1,0:T(8,128)(2,1)}, bf16[145,32,128]{2,1,0:T(8,128)(2,1)S(1)}) custom-call(s32[16,128]{1,0:T(8,128)S(1)} %get-tuple-element.22.code_ref, s32[2,104]{1,0:T(2,128)S(1)} %get-tuple-element.23.list_ref, s32[2]{0:T(128)S(1)} %get-tuple-element.24.count_ref, ...), custom_call_target="tpu_custom_call" | custom-call | flops 1000 | bytes 1000 | tf_op jit(solution)/shard_map/first/pallas_call | solution.py:276
  15.0 5.5 %collective-permute-start.3 = (bf16[54,32,128]{2,1,0:T(8,128)(2,1)S(1)}, bf16[54,32,128]{2,1,0:T(8,128)(2,1)S(1)}, u32[]{:S(2)}, u32[]{:S(2)}) collective-permute-start(bf16[54,32,128]{2,1,0:T(8,128)(2,1)S(1)} %get-tuple-element.31), channel_id=1, source_target_pairs={{0,2},{2,0},{1,3},{3,1},{4,6},{6,4},{5,7},{7,5},{8,10},{10,8},{9,1... | collective-permute-start | bytes 1327112 | tf_op jit(solution)/shard_map/ppermute | solution.py:288
  20.4 7.1 %next.1 = (bf16[54,32,128]{2,1,0:T(8,128)(2,1)S(1)}, bf16[54,32,128]{2,1,0:T(8,128)(2,1)S(1)}, f32[54,32,128]{2,1,0:T(8,128)S(1)}, f32[54,32,128]{2,1,0:T(8,128)...) custom-call(s32[16,128]{1,0:T(8,128)S(1)} %get-tuple-element.22.code_ref, ...), custom_call_target="tpu_custom_call" | custom-call | flops 20000000000 | bytes 1000 | tf_op jit(solution)/shard_map/next/pallas_call | solution.py:303
  27.6 3.6 %collective-permute-done.3 = bf16[54,32,128]{2,1,0:T(8,128)(2,1)S(1)} collective-permute-done((bf16[54,32,128]{2,1,0:T(8,128)(2,1)S(1)}, bf16[54,32,128]{2,1,0:T(8,128)(2,1)S(1)}, u32[]{:S(2)}, u32[]{:S(2)}) %collective-permute-start.3) | collective-permute-done | bytes 442400 | tf_op jit(solution)/shard_map/ppermute | solution.py:288
  31.2 0.9 %add_convert_fusion.3 = (bf16[27,32,128]{2,1,0:T(8,128)(2,1)}, bf16[27,32,128]{2,1,0:T(8,128)(2,1)}) fusion(f32[54,32,128]{2,1,0:T(8,128)S(1)} %get-tuple-element.30, bf16[54,32,128]{2,1,0:T(8,128)(2,1)S(1)} %collective-permute-done.3), kind=kLoop, calls=%fused_computation.3 | loop fusion | flops 663552 | bytes 1769472 | tf_op jit(solution)/shard_map/convert_element_type | solution.py:296
  32.1 1.2 %collective-permute-start.6 = (bf16[27,32,128]{2,1,0:T(8,128)(2,1)}, bf16[27,32,128]{2,1,0:T(8,128)(2,1)}, u32[]{:S(2)}, u32[]{:S(2)}) collective-permute-start(bf16[27,32,128]{2,1,0:T(8,128)(2,1)} %get-tuple-element.42), channel_id=1, source_target_pairs={{0,4},{4,0},{8,12},{12,8},{1,5},{5,1},{9,13},{13,9},{2,6},{6,2},{1... | collective-permute-start | bytes 663560 | tf_op jit(solution)/shard_map/ppermute | solution.py:299
  34.2 2.2 %collective-permute-start.9 = (bf16[54,32,128]{2,1,0:T(8,128)(2,1)S(1)}, bf16[54,32,128]{2,1,0:T(8,128)(2,1)}, u32[]{:S(2)}, u32[]{:S(2)}) collective-permute-start(bf16[54,32,128]{2,1,0:T(8,128)(2,1)S(1)} %get-tuple-element.37), channel_id=1, source_target_pairs={{0,2},{2,0},{1,3},{3,1},{4,6},{6,4},{5,7},{7,5},{8,10},{10,8},{9,1... | collective-permute-start | bytes 1327112 | tf_op jit(solution)/shard_map/ppermute | solution.py:317
  36.4 4.6 %collective-permute-done.5 = bf16[54,32,128]{2,1,0:T(8,128)(2,1)} collective-permute-done((bf16[54,32,128]{2,1,0:T(8,128)(2,1)}, bf16[54,32,128]{2,1,0:T(8,128)(2,1)}, u32[]{:S(2)}, u32[]{:S(2)}) %collective-permute-start.5) | collective-permute-done | bytes 442400 | tf_op jit(solution)/shard_map/ppermute | solution.py:288
  41.0 2.4 %collective-permute-done.7 = bf16[27,32,128]{2,1,0:T(8,128)(2,1)} collective-permute-done((bf16[27,32,128]{2,1,0:T(8,128)(2,1)}, bf16[27,32,128]{2,1,0:T(8,128)(2,1)}, u32[]{:S(2)}, u32[]{:S(2)}) %collective-permute-start.7) | collective-permute-done | bytes 221216 | tf_op jit(solution)/shard_map/ppermute | solution.py:299
  43.4 1.4 %add_convert_fusion = bf16[54,32,128]{2,1,0:T(8,128)(2,1)S(1)} fusion(f32[54,32,128]{2,1,0:T(8,128)S(1)} %get-tuple-element.33, bf16[54,32,128]{2,1,0:T(8,128)(2,1)} %collective-permute-done.5, bf16[27,32,128]{2,1,0:T(8,128)(2,1)} %collective-permute-done.7, bf16[27,32,128]{2,1,0:T(8,128)(2,1)} %collective-permute-done.6, pred[]{:T(512)S(6)} %lt.15), kind=kLoop, calls=%fused_computation | loop fusion | flops 1548288 | bytes 2211841 | tf_op jit(solution)/shard_map/convert_element_type | solution.py:296
  44.8 1.5 %collective-permute-start.8 = (bf16[54,32,128]{2,1,0:T(8,128)(2,1)S(1)}, bf16[54,32,128]{2,1,0:T(8,128)(2,1)S(1)}, u32[]{:S(2)}, u32[]{:S(2)}) collective-permute-start(bf16[54,32,128]{2,1,0:T(8,128)(2,1)S(1)} %add_convert_fusion), channel_id=1, source_target_pairs={{0,8},{4,0},{8,12},{12,4},{1,9},{5,1},{9,13},{13,5},{2,10},{6,2},{... | collective-permute-start | bytes 1327112 | tf_op jit(solution)/shard_map/ppermute | solution.py:299
  46.3 4.2 %collective-permute-done.9 = bf16[54,32,128]{2,1,0:T(8,128)(2,1)} collective-permute-done((bf16[54,32,128]{2,1,0:T(8,128)(2,1)S(1)}, bf16[54,32,128]{2,1,0:T(8,128)(2,1)}, u32[]{:S(2)}, u32[]{:S(2)}) %collective-permute-start.9) | collective-permute-done | bytes 442400 | tf_op jit(solution)/shard_map/ppermute | solution.py:317
  50.5 1.5 %add_convert_fusion.1 = (bf16[27,32,128]{2,1,0:T(8,128)(2,1)S(1)}, bf16[27,32,128]{2,1,0:T(8,128)(2,1)S(1)}) fusion(bf16[27,32,128]{2,1,0:T(8,128)(2,1)} %collective-permute-done.7, f32[54,32,128]{2,1,0:T(8,128)S(1)} %get-tuple-element.35, bf16[54,32,128]{2,1,0:T(8,128)(2,1)} %collective-permute-done.9, pred[]{:T(512)S(6)} %not.4, ...), kind=kLoop, calls=%fused_computation.1 | loop fusion | flops 1327104 | bytes 2211841 | tf_op jit(solution)/shard_map/convert_element_type | solution.py:296
  52.0 1.0 %collective-permute-start.10 = (bf16[27,32,128]{2,1,0:T(8,128)(2,1)S(1)}, bf16[27,32,128]{2,1,0:T(8,128)(2,1)S(1)}, u32[]{:S(2)}, u32[]{:S(2)}) collective-permute-start(bf16[27,32,128]{2,1,0:T(8,128)(2,1)S(1)} %get-tuple-element.40), channel_id=1, source_target_pairs={{0,4},{4,12},{8,0},{12,8},{1,5},{5,13},{9,1},{13,9},{2,6},{6,14},{... | collective-permute-start | bytes 663560 | tf_op jit(solution)/shard_map/ppermute | solution.py:299
  53.0 2.0 %collective-permute-start.11 = (bf16[27,32,128]{2,1,0:T(8,128)(2,1)S(1)}, bf16[27,32,128]{2,1,0:T(8,128)(2,1)S(1)}, u32[]{:S(2)}, u32[]{:S(2)}) collective-permute-start(bf16[27,32,128]{2,1,0:T(8,128)(2,1)S(1)} %get-tuple-element.39), channel_id=1, source_target_pairs={{0,4},{4,12},{8,0},{12,8},{1,5},{5,13},{9,1},{13,9},{2,6},{6,14},{... | collective-permute-start | bytes 663560 | tf_op jit(solution)/shard_map/ppermute | solution.py:299
  55.0 4.2 %collective-permute-done.4.across_ref = bf16[54,32,128]{2,1,0:T(8,128)(2,1)S(1)} collective-permute-done((bf16[54,32,128]{2,1,0:T(8,128)(2,1)S(1)}, bf16[54,32,128]{2,1,0:T(8,128)(2,1)S(1)}, u32[]{:S(2)}, u32[]{:S(2)}) %collective-permute-start.4) | collective-permute-done | bytes 442400 | tf_op jit(solution)/shard_map/ppermute | solution.py:317
  59.1 2.8 %collective-permute-done.10.rest_1_ = bf16[27,32,128]{2,1,0:T(8,128)(2,1)S(1)} collective-permute-done((bf16[27,32,128]{2,1,0:T(8,128)(2,1)S(1)}, bf16[27,32,128]{2,1,0:T(8,128)(2,1)S(1)}, u32[]{:S(2)}, u32[]{:S(2)}) %collective-permute-start.10) | collective-permute-done | bytes 221216 | tf_op jit(solution)/shard_map/ppermute | solution.py:299
  61.9 3.5 %collective-permute-done.11.rest_2_ = bf16[27,32,128]{2,1,0:T(8,128)(2,1)S(1)} collective-permute-done((bf16[27,32,128]{2,1,0:T(8,128)(2,1)S(1)}, bf16[27,32,128]{2,1,0:T(8,128)(2,1)S(1)}, u32[]{:S(2)}, u32[]{:S(2)}) %collective-permute-start.11) | collective-permute-done | bytes 221216 | tf_op jit(solution)/shard_map/ppermute | solution.py:299
  65.5 1.3 %last.1 = f32[12,32,576]{2,1,0:T(8,128)} custom-call(f32[54,32,128]{2,1,0:T(8,128)S(1)} %get-tuple-element.28.own_ref, bf16[54,32,128]{2,1,0:T(8,128)(2,1)S(1)} %collective-permute-done.4.across_ref, bf16[54,32,128]{2,1,0:T(8,128)(2,1)S(1)} %collective-permute-done.8.rest_0_, bf16[27,32,128]{2,1,0:T(8,128)(2,1)S(1)} %collective-permute-done.10.rest_1_, ...), custom_call_target="tpu_custom_call" | custom-call | flops 1000 | bytes 1000 | tf_op jit(solution)/shard_map/last/pallas_call | solution.py:326
  (14 shorter events, 2.8 us)
Async XLA Ops:
  0.0 5.4 %collective-permute-start = (bf16[32,6144]{1,0:T(8,128)(2,1)}, bf16[32,6144]{1,0:T(8,128)(2,1)S(1)}, u32[]{:S(2)}, u32[]{:S(2)}) collective-permute-start(bf16[32,6144]{1,0:T(8,128)(2,1)} %cells_ref.1), channel_id=1, source_target_pairs={{0,1},{1,0},{2,3},{3,2},{4,5},{5,4},{6,7},{7,6},{8,9},{9,8},{10,11... | collective-permute-start | bytes 1179656 | tf_op jit(solution)/shard_map/ppermute | solution.py:244
  1.4 10.1 %collective-permute-start.1 = (bf16[32,1536]{1,0:T(8,128)(2,1)S(1)}, bf16[32,1536]{1,0:T(8,128)(2,1)S(1)}, u32[]{:S(2)}, u32[]{:S(2)}) collective-permute-start(bf16[32,1536]{1,0:T(8,128)(2,1)S(1)} %get-tuple-element.44), channel_id=1, source_target_pairs={{0,2},{4,6},{8,10},{12,14},{2,0},{6,4},{10,8},{14,12},{1,3},{5,7},... | collective-permute-start | bytes 294920 | tf_op jit(solution)/shard_map/ppermute | solution.py:47
  4.0 7.5 %collective-permute-start.2 = (bf16[32,1536]{1,0:T(8,128)(2,1)S(1)}, bf16[32,1536]{1,0:T(8,128)(2,1)S(1)}, u32[]{:S(2)}, u32[]{:S(2)}) collective-permute-start(bf16[32,1536]{1,0:T(8,128)(2,1)S(1)} %get-tuple-element.43), channel_id=1, source_target_pairs={{2,4},{6,8},{10,12},{4,2},{8,6},{12,10},{3,5},{7,9},{11,13},{5,3},... | collective-permute-start | bytes 294920 | tf_op jit(solution)/shard_map/ppermute | solution.py:47
  5.4 4.8 %copy-start = (bf16[96,20480]{1,0:T(8,128)(2,1)S(1)}, bf16[96,20480]{1,0:T(8,128)(2,1)}, u32[]{:S(2)}) copy-start(bf16[96,20480]{1,0:T(8,128)(2,1)} %jac_ref.1) | copy-start | bytes 11796484
  5.4 1.1 %copy-start.1 = (bf16[32,6144]{1,0:T(8,128)(2,1)S(1)}, bf16[32,6144]{1,0:T(8,128)(2,1)}, u32[]{:S(2)}) copy-start(bf16[32,6144]{1,0:T(8,128)(2,1)} %cells_ref.1) | copy-start | bytes 1179652
  15.0 16.3 %collective-permute-start.3 = (bf16[54,32,128]{2,1,0:T(8,128)(2,1)S(1)}, bf16[54,32,128]{2,1,0:T(8,128)(2,1)S(1)}, u32[]{:S(2)}, u32[]{:S(2)}) collective-permute-start(bf16[54,32,128]{2,1,0:T(8,128)(2,1)S(1)} %get-tuple-element.31), channel_id=1, source_target_pairs={{0,2},{2,0},{1,3},{3,1},{4,6},{6,4},{5,7},{7,5},{8,10},{10,8},{9,1... | collective-permute-start | bytes 1327112 | tf_op jit(solution)/shard_map/ppermute | solution.py:288
  27.5 13.5 %collective-permute-start.5 = (bf16[54,32,128]{2,1,0:T(8,128)(2,1)}, bf16[54,32,128]{2,1,0:T(8,128)(2,1)}, u32[]{:S(2)}, u32[]{:S(2)}) collective-permute-start(bf16[54,32,128]{2,1,0:T(8,128)(2,1)} %get-tuple-element.34), channel_id=1, source_target_pairs={{0,2},{2,0},{1,3},{3,1},{4,6},{6,4},{5,7},{7,5},{8,10},{10,8},{9,1... | collective-permute-start | bytes 1327112 | tf_op jit(solution)/shard_map/ppermute | solution.py:288
  32.1 8.9 %collective-permute-start.6 = (bf16[27,32,128]{2,1,0:T(8,128)(2,1)}, bf16[27,32,128]{2,1,0:T(8,128)(2,1)}, u32[]{:S(2)}, u32[]{:S(2)}) collective-permute-start(bf16[27,32,128]{2,1,0:T(8,128)(2,1)} %get-tuple-element.42), channel_id=1, source_target_pairs={{0,4},{4,0},{8,12},{12,8},{1,5},{5,1},{9,13},{13,9},{2,6},{6,2},{1... | collective-permute-start | bytes 663560 | tf_op jit(solution)/shard_map/ppermute | solution.py:299
  33.3 10.1 %collective-permute-start.7 = (bf16[27,32,128]{2,1,0:T(8,128)(2,1)}, bf16[27,32,128]{2,1,0:T(8,128)(2,1)}, u32[]{:S(2)}, u32[]{:S(2)}) collective-permute-start(bf16[27,32,128]{2,1,0:T(8,128)(2,1)} %get-tuple-element.41), channel_id=1, source_target_pairs={{0,4},{4,0},{8,12},{12,8},{1,5},{5,1},{9,13},{13,9},{2,6},{6,2},{1... | collective-permute-start | bytes 663560 | tf_op jit(solution)/shard_map/ppermute | solution.py:299
  34.2 16.3 %collective-permute-start.9 = (bf16[54,32,128]{2,1,0:T(8,128)(2,1)S(1)}, bf16[54,32,128]{2,1,0:T(8,128)(2,1)}, u32[]{:S(2)}, u32[]{:S(2)}) collective-permute-start(bf16[54,32,128]{2,1,0:T(8,128)(2,1)S(1)} %get-tuple-element.37), channel_id=1, source_target_pairs={{0,2},{2,0},{1,3},{3,1},{4,6},{6,4},{5,7},{7,5},{8,10},{10,8},{9,1... | collective-permute-start | bytes 1327112 | tf_op jit(solution)/shard_map/ppermute | solution.py:317
  36.4 22.8 %collective-permute-start.4 = (bf16[54,32,128]{2,1,0:T(8,128)(2,1)S(1)}, bf16[54,32,128]{2,1,0:T(8,128)(2,1)S(1)}, u32[]{:S(2)}, u32[]{:S(2)}) collective-permute-start(bf16[54,32,128]{2,1,0:T(8,128)(2,1)S(1)} %get-tuple-element.32), channel_id=1, source_target_pairs={{0,2},{2,0},{1,3},{3,1},{4,6},{6,4},{5,7},{7,5},{8,10},{10,8},{9,1... | collective-permute-start | bytes 1327112 | tf_op jit(solution)/shard_map/ppermute | solution.py:317
  44.8 20.7 %collective-permute-start.8 = (bf16[54,32,128]{2,1,0:T(8,128)(2,1)S(1)}, bf16[54,32,128]{2,1,0:T(8,128)(2,1)S(1)}, u32[]{:S(2)}, u32[]{:S(2)}) collective-permute-start(bf16[54,32,128]{2,1,0:T(8,128)(2,1)S(1)} %add_convert_fusion), channel_id=1, source_target_pairs={{0,8},{4,0},{8,12},{12,4},{1,9},{5,1},{9,13},{13,5},{2,10},{6,2},{... | collective-permute-start | bytes 1327112 | tf_op jit(solution)/shard_map/ppermute | solution.py:299
  52.0 10.0 %collective-permute-start.10 = (bf16[27,32,128]{2,1,0:T(8,128)(2,1)S(1)}, bf16[27,32,128]{2,1,0:T(8,128)(2,1)S(1)}, u32[]{:S(2)}, u32[]{:S(2)}) collective-permute-start(bf16[27,32,128]{2,1,0:T(8,128)(2,1)S(1)} %get-tuple-element.40), channel_id=1, source_target_pairs={{0,4},{4,12},{8,0},{12,8},{1,5},{5,13},{9,1},{13,9},{2,6},{6,14},{... | collective-permute-start | bytes 663560 | tf_op jit(solution)/shard_map/ppermute | solution.py:299
  53.0 12.5 %collective-permute-start.11 = (bf16[27,32,128]{2,1,0:T(8,128)(2,1)S(1)}, bf16[27,32,128]{2,1,0:T(8,128)(2,1)S(1)}, u32[]{:S(2)}, u32[]{:S(2)}) collective-permute-start(bf16[27,32,128]{2,1,0:T(8,128)(2,1)S(1)} %get-tuple-element.39), channel_id=1, source_target_pairs={{0,4},{4,12},{8,0},{12,8},{1,5},{5,13},{9,1},{13,9},{2,6},{6,14},{... | collective-permute-start | bytes 663560 | tf_op jit(solution)/shard_map/ppermute | solution.py:299

commit v2 on v1

--- a/solution.py
+++ b/solution.py
@@ -66,14 +66,15 @@
 def call_plan(count):
     sent = [(p, 0) for p in range(count)]
     kept = [(p, 1) for p in range(count)]
-    return [sent[:2], sent[2:] + kept]
-
-
-def group_lists(elems, count, ints_ref, list_ref, count_ref, call_ref):
+    return [sent[:1], sent[1:] + kept]
+
+
+def lists_kernel(elems, count, ints_ref, again_ref, code_ref, list_ref, count_ref):
     me = lax.axis_index("sub")
     z = lax.axis_index("elem")
     plan = call_plan(count)
-    code = {table: (c, 2 + t * BLOCKS) for c, tables in enumerate(plan) for t, table in enumerate(tables)}
+    code = {table: (c, t) for c, tables in enumerate(plan) for t, table in enumerate(tables)}
+    numbers, calls = 0, 0
     for d in range(count):
         for x in range(2):
             values = [0, 0]
@@ -82,39 +83,34 @@
                     here = (z == y) & ((me == x) if mine else (me != x))
                     for i in range(2):
                         values[i] = jnp.where(here, code[place_of(y, d), mine][i], values[i])
-            call_ref[0, 2 * d + x] = values[0]
-            call_ref[1, 2 * d + x] = LANES * values[1]
-    for call in range(len(plan)):
-        count_ref[call] = 0
-
-    def put(e, carry):
-        owner = ints_ref[0, e]
-        call = call_ref[0, owner]
-        at = count_ref[call]
-        list_ref[call, at] = e + call_ref[1, owner]
-        count_ref[call] = at + 1
-        return carry
-
-    lax.fori_loop(0, elems, put, 0, unroll=8)
-    for call in range(len(plan)):
-        for u in range(UNROLL):
-            list_ref[call, count_ref[call] + u] = elems
-
-
-def near_kernel(elems, count, ints_ref, again_ref, cells_ref, other_ref,
-                near_ref, weight_ref, code_ref, list_ref, count_ref, call_ref):
-    device = lax.axis_index("elem") * lax.axis_size("sub") + lax.axis_index("sub")
+            calls += values[0] << (2 * d + x)
+            numbers += values[1] << (3 * (2 * d + x))
+
+    device = z * lax.axis_size("sub") + me
     rim = elems // 4
     faces = again_ref[FACE:FACE + FACES, :]
     code_ref[...] = jnp.zeros_like(code_ref)
     code_ref[CELL:CELL + FACES, :elems] = jnp.where(faces >= 0, faces - (device * elems - rim), elems + 2 * rim)
     code_ref[TARGET:TARGET + FACES + 1, :elems] = (
         again_ref[MEMBER:MEMBER + 1, :] * CS + again_ref[SLOT:SLOT + FACES + 1, :])
-    group_lists(elems, count, ints_ref, list_ref, count_ref, call_ref)
+
+    zero, one = 0, 0
+    for start in range(0, elems, STEP):
+        owners = [ints_ref[0, e] for e in range(start, start + STEP)]
+        for e, owner in zip(range(start, start + STEP), owners):
+            call = (calls >> owner) & 1
+            number = (numbers >> (3 * owner)) & 7
+            list_ref[call, jnp.where(call == 0, zero, one)] = LANES * BLOCKS * number + (2 * LANES + e)
+            zero, one = zero + 1 - call, one + call
+    for call, number in enumerate((zero, one)):
+        count_ref[call] = number
+        for u in range(UNROLL):
+            list_ref[call, number + u] = elems
+
+
+def near_kernel(cells_ref, other_ref, after_ref, near_ref, weight_ref):
     near_blocks(near_ref, 0, cells_ref)
-    col = lax.axis_index("col")
-    own_weights(weight_ref, col, cells_ref)
-    own_weights(weight_ref, 1 - col, other_ref)
+    own_weights(weight_ref, cells_ref, other_ref)
 
 
 def rows_kernel(jac_ref, after_ref, rows_ref):
@@ -176,17 +172,23 @@
         near_ref[base + 2 * p + 1] = jnp.where(low, turned, pair).astype(jnp.bfloat16)
 
 
-def own_weights(weight_ref, side, cells_ref):
-    row = lax.broadcasted_iota(jnp.int32, (128, B), 0)
-    col = lax.broadcasted_iota(jnp.int32, (128, B), 1)
-    source = 2 * (col % 32) + col // 32
-    picks = [jnp.where(row == source + h * B, 1.0, 0.0).astype(jnp.bfloat16) for h in range(2)]
-    at = pl.ds(pl.multiple_of(side * 32, 32), 32)
-    for p in range(cells_ref.shape[1] // 128):
-        pair = cells_ref[:, p * 128:(p + 1) * 128]
-        for h in range(2):
-            moved = jnp.dot(pair, picks[h], preferred_element_type=jnp.float32)
-            weight_ref[2 * p + h, at, :] = moved.astype(jnp.bfloat16)
+def own_weights(weight_ref, cells_ref, other_ref):
+    row = lax.broadcasted_iota(jnp.int32, (128, 128), 0)
+    col = lax.broadcasted_iota(jnp.int32, (128, 128), 1)
+    source = (col // B) * B + 2 * (col % 32) + (col % B) // 32
+    pick = jnp.where(row == source, 1.0, 0.0).astype(jnp.bfloat16)
+    low_first = lax.axis_index("col") == 0
+    step = 8
+    for p in range(0, cells_ref.shape[1] // 128, step):
+        stacked = []
+        for q in range(p, p + step):
+            own, other = cells_ref[:, q * 128:(q + 1) * 128], other_ref[:, q * 128:(q + 1) * 128]
+            stacked += [jnp.where(low_first, own, other), jnp.where(low_first, other, own)]
+        moved = jnp.dot(jnp.concatenate(stacked, axis=0), pick, preferred_element_type=jnp.float32)
+        for q in range(step):
+            pair = moved[q * CB:(q + 1) * CB]
+            for h in range(2):
+                weight_ref[2 * (p + q) + h] = pair[:, h * B:(h + 1) * B].astype(jnp.bfloat16)
 
 
 def first_kernel(elems, code_ref, list_ref, count_ref, rows_ref, own_ref, weight_ref, one_ref, two_ref, *rest):
@@ -203,20 +205,35 @@
         out[...] = total[1 + k * PAIRS:1 + (k + 1) * PAIRS].astype(out.dtype)
 
 
-def next_kernel(elems, call, code_ref, list_ref, count_ref, rows_ref, near_ref, weight_ref, *rest):
+def next_kernel(elems, call, cuts, code_ref, list_ref, count_ref, rows_ref, near_ref, weight_ref, *rest):
     outs, total = rest[:-1], rest[-1]
     accumulate(call, elems, code_ref, list_ref, count_ref, rows_ref, near_ref, weight_ref, total)
-    for k, out in enumerate(outs):
-        out[...] = total[1 + k * PAIRS:1 + (k + 1) * PAIRS].astype(out.dtype)
-
-
-def last_kernel(own_ref, across_ref, *rest):
-    parts, out_ref, total = rest[:-2], rest[-2], rest[-1]
-    total[...] = own_ref[...] + across_ref[...].astype(jnp.float32)
+    for (t, at), out in zip(cuts, outs):
+        start = 1 + t * PAIRS
+        out[...] = total[start + at.start:start + at.stop].astype(out.dtype)
+
+
+def add_kernel(start, kept_ref, came_ref, *rest):
+    out_ref = rest[-1]
+    at = slice(start, start + out_ref.shape[0])
+    value = kept_ref[at] + came_ref[...].astype(jnp.float32)
+    for more_ref in rest[:-1]:
+        value = value + more_ref[at].astype(jnp.float32)
+    out_ref[...] = value.astype(out_ref.dtype)
+
+
+def gather_kernel(own_ref, *rest):
+    parts, total = rest[:-1], rest[-1]
+    total[...] = own_ref[...]
     at = 0
     for part in parts:
         total[at:at + part.shape[0]] += part[...].astype(jnp.float32)
         at = (at + part.shape[0]) % PAIRS
+
+
+def last_kernel(*rest):
+    out_ref, total = rest[-2], rest[-1]
+    gather_kernel(*rest[:-2], total)
     low = lax.broadcasted_iota(jnp.int32, (32, 128), 1) < B
     for a in range(AGG_DEV):
         first = a * CS // 2
@@ -246,22 +263,31 @@
     ints = jnp.concatenate([owner.T, member[None], coarse_slot.T, face_pattern.T], axis=0)
 
     long = pl.CostEstimate(flops=20_000_000_000, bytes_accessed=1000, transcendentals=0)
-    own_near, weights, codes, lists, counts = pl.pallas_call(
-        functools.partial(near_kernel, elems, count),
-        in_specs=[SMEM, VMEM, VMEM, VMEM],
-        out_specs=[VMEM, VMEM, VMEM, SMEM, SMEM],
+    codes, lists, counts = pl.pallas_call(
+        functools.partial(lists_kernel, elems, count),
+        in_specs=[SMEM, VMEM],
+        out_specs=[VMEM, SMEM, SMEM],
         out_shape=[
-            jax.ShapeDtypeStruct((elems, half, 2 * B), jnp.bfloat16),
-            jax.ShapeDtypeStruct((elems, CB, B), jnp.bfloat16),
             jax.ShapeDtypeStruct((16, LANES), jnp.int32),
             jax.ShapeDtypeStruct((len(plan), elems + UNROLL), jnp.int32),
             jax.ShapeDtypeStruct((len(plan),), jnp.int32),
         ],
-        scratch_shapes=[pltpu.SMEM((2, 2 * count), jnp.int32)],
         compiler_params=params(),
         cost_estimate=long,
+        name="lists",
+    )(ints, ints)
+    own_near, weights = pl.pallas_call(
+        near_kernel,
+        in_specs=[VMEM, VMEM, pl.BlockSpec(memory_space=pl.ANY)],
+        out_specs=[VMEM, VMEM],
+        out_shape=[
+            jax.ShapeDtypeStruct((elems, half, 2 * B), jnp.bfloat16),
+            jax.ShapeDtypeStruct((elems, CB, B), jnp.bfloat16),
+        ],
+        compiler_params=params(),
+        cost_estimate=cost,
         name="near",
-    )(ints, ints, prolong, other)
+    )(prolong, other, codes)
     rows = pl.pallas_call(
         rows_kernel,
         in_specs=[VMEM, pl.BlockSpec(memory_space=pl.ANY)],
@@ -273,66 +299,92 @@
     )(jacobian, own_near)
 
     table = (PAIRS, half, 2 * B)
-    *sent, near = pl.pallas_call(
+    sent, near = pl.pallas_call(
         functools.partial(first_kernel, elems),
         in_specs=[SMEM] * 3 + [VMEM] * 5,
-        out_specs=[VMEM] * 3,
-        out_shape=[jax.ShapeDtypeStruct(table, jnp.bfloat16)] * 2 + [
+        out_specs=[VMEM] * 2,
+        out_shape=[
+            jax.ShapeDtypeStruct(table, jnp.bfloat16),
             jax.ShapeDtypeStruct((elems + 2 * rim + 1, half, 2 * B), jnp.bfloat16),
         ],
-        scratch_shapes=[pltpu.VMEM((1 + 2 * PAIRS, half, 2 * B), jnp.float32)],
+        scratch_shapes=[pltpu.VMEM((1 + PAIRS, half, 2 * B), jnp.float32)],
         compiler_params=params(),
         cost_estimate=cost,
         name="first",
     )(codes, lists, counts, rows, own_near, weights, one, two)
-    arrived = [lax.ppermute(block, "sub", [(0, 1), (1, 0)]) for block in sent]
-
-    outer = (lax.axis_index("elem") + 1) % 4 < 2
-
-    def summed(p, at, more=None, adds=None):
-        value = kept[p][at] + arrived[p][at].astype(jnp.float32)
-        if more is not None:
-            value = value + jnp.where(adds, more.astype(jnp.float32), 0.0)
-        return value.astype(jnp.bfloat16)
-
-    def sent_to(block, pairs):
+
+    def across(block):
+        return lax.ppermute(block, "sub", [(0, 1), (1, 0)])
+
+    def along(block, pairs):
         return lax.ppermute(block, "elem", pairs)
 
-    halves = [slice(0, PAIRS // 2), slice(PAIRS // 2, PAIRS)]
-    shapes = [jax.ShapeDtypeStruct(table, jnp.float32 if mine else jnp.bfloat16) for p, mine in plan[1]]
+    def behind(block, *others):
+        return lax.optimization_barrier((block, *others))[0]
+
+    def summed(p, at, block, *more):
+        return pl.pallas_call(
+            functools.partial(add_kernel, at.start),
+            in_specs=[VMEM] * (2 + len(more)),
+            out_specs=VMEM,
+            out_shape=jax.ShapeDtypeStruct(block.shape, jnp.bfloat16),
+            compiler_params=params(),
+            cost_estimate=cost,
+            name="add_%d" % p,
+        )(kept[p], block, *more)
+
+    whole, halves = slice(0, PAIRS), [slice(0, PAIRS // 2), slice(PAIRS // 2, PAIRS)]
+    pieces = {p: halves if p < 3 else [whole] for p in range(1, count)}
+    cuts = [(t, at) for t, (p, mine) in enumerate(plan[1]) for at in ([whole] if mine else pieces[p])]
+    came = {0: [across(sent)]}
     outs = pl.pallas_call(
-        functools.partial(next_kernel, elems, 1),
+        functools.partial(next_kernel, elems, 1, cuts),
         in_specs=[SMEM] * 3 + [VMEM] * 3,
-        out_specs=[VMEM] * len(shapes),
-        out_shape=shapes,
-        scratch_shapes=[pltpu.VMEM((1 + len(shapes) * PAIRS, half, 2 * B), jnp.float32)],
+        out_specs=[VMEM] * len(cuts),
+        out_shape=[
+            jax.ShapeDtypeStruct((at.stop - at.start, half, 2 * B), jnp.float32 if plan[1][t][1] else jnp.bfloat16)
+            for t, at in cuts
+        ],
+        scratch_shapes=[pltpu.VMEM((1 + len(plan[1]) * PAIRS, half, 2 * B), jnp.float32)],
         compiler_params=params(),
         cost_estimate=long,
         name="next",
     )(codes, lists, counts, rows, near, weights)
-    sent, kept = outs[:count - 2], outs[count - 2:]
-    first = [summed(0, at) for at in halves]
-    for block in sent:
-        block = lax.optimization_barrier((block, *first))[0]
-        arrived.append(lax.ppermute(block, "sub", [(0, 1), (1, 0)]))
-
-    near_sums = [sent_to(block, [(y, y ^ 1) for y in range(count)]) for block in first]
-    near_sums = jnp.concatenate(near_sums, axis=0)
-    second = summed(1, slice(None), near_sums, outer)
-    arrived[2] = lax.optimization_barrier((arrived[2], second))[0]
-    parts = [sent_to(second, ROUNDS[0])]
-    parts += [sent_to(summed(2, at, near_sums[at], ~outer), ROUNDS[1]) for at in halves]
-
+    kept = outs[-count:]
+    first = summed(0, whole, came[0][0])
+    sent = outs[:-count]
+    straight = along(first, [(1, 2), (2, 1)])
+    joined = along(first, [(0, 1), (3, 2)])
+    came[1] = [across(sent[0]), across(behind(sent[1], first))]
+    ready1 = [summed(1, at, block) for at, block in zip(halves, came[1])]
+    round1 = [along(block, ROUNDS[0]) for block in ready1]
+    came[2] = [across(behind(sent[2], came[1][0])), across(behind(sent[3], came[1][1], straight, joined))]
+    came[2][1] = behind(came[2][1], *round1)
+    came[2][0] = behind(came[2][0], round1[0])
+    ready2 = [summed(2, at, block, joined) for at, block in zip(halves, came[2])]
+    round2 = [along(block, ROUNDS[1]) for block in ready2]
+    came[3] = [across(behind(sent[4], came[2][0]))]
+
+    total = pl.pallas_call(
+        gather_kernel,
+        in_specs=[VMEM] * 4,
+        out_specs=VMEM,
+        out_shape=jax.ShapeDtypeStruct(table, jnp.float32),
+        compiler_params=params(),
+        cost_estimate=pl.CostEstimate(flops=1_000_000_000, bytes_accessed=1000, transcendentals=0),
+        name="gather",
+    )(kept[count - 1], straight, *round1)
+    parts = round2 + came[count - 1]
     coarse = pl.pallas_call(
         last_kernel,
-        in_specs=[VMEM] * 5,
+        in_specs=[VMEM] * (1 + len(parts)),
         out_specs=VMEM,
         out_shape=jax.ShapeDtypeStruct((AGG_DEV, half, CS * CB), jnp.float32),
         scratch_shapes=[pltpu.VMEM(table, jnp.float32)],
         compiler_params=params(),
         cost_estimate=cost,
         name="last",
-    )(kept[count - 1], arrived[count - 1], *parts)
+    )(total, *parts)
     return coarse.transpose(1, 0, 2)
 
 

time: 67.1 us -> 64.4 us (0.960)
  starting transfers between devices: 18 us -> 23.5 us
  other arithmetic: 5.4 us -> 1.67 us
  waiting for transfers between devices: 25.3 us -> 23.3 us
  Pallas kernels: 16.8 us -> 15.5 us
  local copies, waits for them, and re-layouts: 1.15 us -> 0.01 us
    convert_element_type x3 -> x0, other arithmetic: 3.73 us -> none  [summed(): return value.astype(jnp.bfloat16)]
    ppermute x2, starting transfers between devices: 3.21 us -> 6.01 us  [swap(): return lax.ppermute(block, axes, pairs + [(j, i) for i, j in pairs])]
    ppermute x9 -> x12, starting transfers between devices: 14.3 us -> 17 us  [the longest x6 9.67 us: along(): return lax.ppermute(block, 'elem', pairs)]
    ppermute x9 -> x12, waiting for transfers between devices: 25.3 us -> 23.3 us  [the longest x6 11.9 us: across(): return lax.ppermute(block, 'sub', [(0, 1), (1, 0)])]
    unnamed x4, local copies, waits for them, and re-layouts: 1.15 us -> 0.01 us
    pallas_call x1, Pallas kernels: 3.47 us -> 2.71 us  [dense(): pl.pallas_call(functools.partial(first_kernel, elems), in_specs=[SMEM] *...]
    pallas_call x3 -> x10, Pallas kernels: 12 us -> 11.5 us  [the longest x1 7.16 us: dense(): pl.pallas_call(functools.partial(next_kernel, elems, 1, cuts), in_specs=[...]
  transfers between devices with their start and end apart: 12 -> 15, of which waited for: 7 -> 8; matrix products, arithmetic and copies ran while one was open for 8% -> 3% of each run, Pallas kernels for 18% -> 18%
where the time goes in v2:
time: 64.4 us; the launch traced here: 64.2 us
  starting transfers between devices  23.5 us (36%)
  waiting for transfers between devices  23.3 us (36%)
  Pallas kernels  15.5 us (24%)
  other arithmetic  1.67 us (3%)
    ppermute x6, waiting for transfers between devices, across(): return lax.ppermute(block, 'sub', [(0, 1), (1, 0)])  11.9 us
    ppermute x6, waiting for transfers between devices, along(): return lax.ppermute(block, 'elem', pairs)  11.4 us
    ppermute x6, starting transfers between devices, along(): return lax.ppermute(block, 'elem', pairs)  9.67 us
    ppermute x6, starting transfers between devices, across(): return lax.ppermute(block, 'sub', [(0, 1), (1, 0)])  7.36 us
    pallas_call x1, Pallas kernels, dense(): pl.pallas_call(functools.partial(next_kernel, elems, 1, cuts), in_specs=[...  7.16 us
    ppermute x2, starting transfers between devices, swap(): return lax.ppermute(block, axes, pairs + [(j, i) for i, j in pairs])  6.01 us
    pallas_call x1, Pallas kernels, dense(): pl.pallas_call(functools.partial(first_kernel, elems), in_specs=[SMEM] *...  2.71 us
    pallas_call x1, Pallas kernels, dense(): pl.pallas_call(functools.partial(lists_kernel, elems, count), in_specs=[S...  1.89 us
  transfers between devices with their start and end apart: 15, of which 8 were waited for; matrix products, arithmetic and copies ran while one was open for 3% of the time, Pallas kernels for 18%

profile of v2, /device:TPU:0, one launch (start us, length us, event | category | flops | bytes accessed | tf_op | source)
XLA Modules:
  0.0 64.2 jit_solution(359476787188261269)
XLA Ops:
  0.5 1.0 %broadcast_select_fusion = (bf16[32,1536]{1,0:T(8,128)(2,1)S(1)}, bf16[32,1536]{1,0:T(8,128)(2,1)S(1)}) fusion(pred[]{:T(512)S(6)} %eq.5, bf16[32,6144]{1,0:T(8,128)(2,1)} %cells_ref.1), kind=kLoop, calls=%fused_computation | loop fusion | flops 98304 | bytes 393217 | tf_op jit(solution)/shard_map/jit(_where)/select_n | solution.py:49
  2.1 5.3 %collective-permute-start.1 = (bf16[32,1536]{1,0:T(8,128)(2,1)S(1)}, bf16[32,1536]{1,0:T(8,128)(2,1)S(1)}, u32[]{:S(2)}, u32[]{:S(2)}) collective-permute-start(bf16[32,1536]{1,0:T(8,128)(2,1)S(1)} %get-tuple-element.50), channel_id=1, source_target_pairs={{0,2},{4,6},{8,10},{12,14},{2,0},{6,4},{10,8},{14,12},{1,3},{5,7},... | collective-permute-start | bytes 294920 | tf_op jit(solution)/shard_map/ppermute | solution.py:47
  7.4 0.7 %pad_add_fusion.ints_ref.again_ref = s32[11,96]{1,0:T(8,128)S(1)} fusion(s32[4,96]{1,0:T(4,128)} %bitcast.6, s32[5,96]{1,0:T(8,128)} %bitcast.5, s32[1,96]{1,0:T(1,128)} %bitcast.7, s32[1,96]{1,0:T(1,128)} %bitcast.8), kind=kLoop, calls=%fused_computation.2 | loop fusion | flops 3168 | bytes 8448 | tf_op jit(solution)/shard_map/concatenate | solution.py:263
  8.2 1.9 %lists.1 = (s32[16,128]{1,0:T(8,128)S(1)}, s32[2,104]{1,0:T(2,128)S(1)}, s32[2]{0:T(128)S(1)}) custom-call(s32[11,96]{1,0:T(8,128)S(1)} %pad_add_fusion.ints_ref.again_ref, s32[11,96]{1,0:T(8,128)S(1)} %pad_add_fusion.ints_ref.again_ref), custom_call_target="tpu_custom_call" | custom-call | flops 20000000000 | bytes 1000 | tf_op jit(solution)/shard_map/lists/pallas_call | solution.py:266
  10.8 1.3 %rows.1.rows_ref = bf16[96,160,128]{2,1,0:T(8,128)(2,1)S(1)} custom-call(bf16[96,20480]{1,0:T(8,128)(2,1)S(1)} %copy-done, bf16[96,32,128]{2,1,0:T(8,128)(2,1)S(1)} %get-tuple-element.30.after_ref.own_ref), custom_call_target="tpu_custom_call" | custom-call | flops 1000 | bytes 1000 | tf_op jit(solution)/shard_map/rows/pallas_call | solution.py:291
  12.1 2.7 %first.1 = (bf16[54,32,128]{2,1,0:T(8,128)(2,1)S(1)}, bf16[145,32,128]{2,1,0:T(8,128)(2,1)S(1)}) custom-call(s32[16,128]{1,0:T(8,128)S(1)} %get-tuple-element.27.after_ref.code_ref, s32[2,104]{1,0:T(2,128)S(1)} %get-tuple-element.28.list_ref, s32[2]{0:T(128)S(1)} %get-tuple-element.29.count_ref, bf16[96,160,128]{2,1,0:T(8,128)(2,1)S(1)} %rows.1.rows_ref, ...), custom_call_target="tpu_custom_call" | custom-call | flops 1000 | bytes 1000 | tf_op jit(solution)/shard_map/first/pallas_call | solution.py:302
  14.8 0.8 %collective-permute-start.3 = (bf16[54,32,128]{2,1,0:T(8,128)(2,1)S(1)}, bf16[54,32,128]{2,1,0:T(8,128)(2,1)S(1)}, u32[]{:S(2)}, u32[]{:S(2)}) collective-permute-start(bf16[54,32,128]{2,1,0:T(8,128)(2,1)S(1)} %get-tuple-element.35), channel_id=1, source_target_pairs={{0,2},{2,0},{1,3},{3,1},{4,6},{6,4},{5,7},{7,5},{8,10},{10,8},{9,1... | collective-permute-start | bytes 1327112 | tf_op jit(solution)/shard_map/ppermute | solution.py:317
  15.6 7.2 %next.1 = (bf16[27,32,128]{2,1,0:T(8,128)(2,1)S(1)}, bf16[27,32,128]{2,1,0:T(8,128)(2,1)S(1)}, bf16[27,32,128]{2,1,0:T(8,128)(2,1)S(1)}, bf16[27,32,128]{2,1,0:T...) custom-call(s32[16,128]{1,0:T(8,128)S(1)} %get-tuple-element.27.afte, ...), custom_call_target="tpu_custom_call" | custom-call | flops 20000000000 | bytes 1000 | tf_op jit(solution)/shard_map/next/pallas_call | solution.py:340
  22.8 2.5 %collective-permute-start.5 = (bf16[27,32,128]{2,1,0:T(8,128)(2,1)S(1)}, bf16[27,32,128]{2,1,0:T(8,128)(2,1)S(1)}, u32[]{:S(2)}, u32[]{:S(2)}) collective-permute-start(bf16[27,32,128]{2,1,0:T(8,128)(2,1)S(1)} %get-tuple-element.37), channel_id=1, source_target_pairs={{0,2},{2,0},{1,3},{3,1},{4,6},{6,4},{5,7},{7,5},{8,10},{10,8},{9,1... | collective-permute-start | bytes 663560 | tf_op jit(solution)/shard_map/ppermute | solution.py:317
  25.3 2.6 %collective-permute-done.3.came_ref = bf16[54,32,128]{2,1,0:T(8,128)(2,1)S(1)} collective-permute-done((bf16[54,32,128]{2,1,0:T(8,128)(2,1)S(1)}, bf16[54,32,128]{2,1,0:T(8,128)(2,1)S(1)}, u32[]{:S(2)}, u32[]{:S(2)}) %collective-permute-start.3) | collective-permute-done | bytes 442400 | tf_op jit(solution)/shard_map/ppermute | solution.py:317
  28.0 2.3 %collective-permute-start.10 = (bf16[54,32,128]{2,1,0:T(8,128)(2,1)S(1)}, bf16[54,32,128]{2,1,0:T(8,128)(2,1)S(1)}, u32[]{:S(2)}, u32[]{:S(2)}) collective-permute-start(bf16[54,32,128]{2,1,0:T(8,128)(2,1)S(1)} %add_0.1), channel_id=1, source_target_pairs={{0,4},{12,8},{1,5},{13,9},{2,6},{14,10},{3,7},{15,11},{16,20},{28,... | collective-permute-start | bytes 1327112 | tf_op jit(solution)/shard_map/ppermute | solution.py:320
  31.7 3.1 %collective-permute-start.6 = (bf16[27,32,128]{2,1,0:T(8,128)(2,1)S(1)}, bf16[27,32,128]{2,1,0:T(8,128)(2,1)S(1)}, u32[]{:S(2)}, u32[]{:S(2)}) collective-permute-start(bf16[27,32,128]{2,1,0:T(8,128)(2,1)S(1)} %add_1.2), channel_id=1, source_target_pairs={{0,8},{4,0},{8,12},{12,4},{1,9},{5,1},{9,13},{13,5},{2,10},{6,2},{... | collective-permute-start | bytes 663560 | tf_op jit(solution)/shard_map/ppermute | solution.py:320
  34.8 0.9 %collective-permute-start.9 = (bf16[27,32,128]{2,1,0:T(8,128)(2,1)S(1)}, bf16[27,32,128]{2,1,0:T(8,128)(2,1)S(1)}, u32[]{:S(2)}, u32[]{:S(2)}) collective-permute-start(bf16[27,32,128]{2,1,0:T(8,128)(2,1)S(1)} %get-tuple-element.42), channel_id=1, source_target_pairs={{0,2},{2,0},{1,3},{3,1},{4,6},{6,4},{5,7},{7,5},{8,10},{10,8},{9,1... | collective-permute-start | bytes 663560 | tf_op jit(solution)/shard_map/ppermute | solution.py:317
  35.7 1.1 %collective-permute-start.7 = (bf16[27,32,128]{2,1,0:T(8,128)(2,1)S(1)}, bf16[27,32,128]{2,1,0:T(8,128)(2,1)S(1)}, u32[]{:S(2)}, u32[]{:S(2)}) collective-permute-start(bf16[27,32,128]{2,1,0:T(8,128)(2,1)S(1)} %get-tuple-element.39), channel_id=1, source_target_pairs={{0,2},{2,0},{1,3},{3,1},{4,6},{6,4},{5,7},{7,5},{8,10},{10,8},{9,1... | collective-permute-start | bytes 663560 | tf_op jit(solution)/shard_map/ppermute | solution.py:317
  36.8 7.2 %collective-permute-done.6.rest_1_ = bf16[27,32,128]{2,1,0:T(8,128)(2,1)S(1)} collective-permute-done((bf16[27,32,128]{2,1,0:T(8,128)(2,1)S(1)}, bf16[27,32,128]{2,1,0:T(8,128)(2,1)S(1)}, u32[]{:S(2)}, u32[]{:S(2)}) %collective-permute-start.6) | collective-permute-done | bytes 221216 | tf_op jit(solution)/shard_map/ppermute | solution.py:320
  44.1 1.7 %collective-permute-done.7.came_ref = bf16[27,32,128]{2,1,0:T(8,128)(2,1)S(1)} collective-permute-done((bf16[27,32,128]{2,1,0:T(8,128)(2,1)S(1)}, bf16[27,32,128]{2,1,0:T(8,128)(2,1)S(1)}, u32[]{:S(2)}, u32[]{:S(2)}) %collective-permute-start.7) | collective-permute-done | bytes 221216 | tf_op jit(solution)/shard_map/ppermute | solution.py:317
  45.8 1.8 %collective-permute-start.8 = (bf16[27,32,128]{2,1,0:T(8,128)(2,1)S(1)}, bf16[27,32,128]{2,1,0:T(8,128)(2,1)S(1)}, u32[]{:S(2)}, u32[]{:S(2)}) collective-permute-start(bf16[27,32,128]{2,1,0:T(8,128)(2,1)S(1)} %add_1.3), channel_id=1, source_target_pairs={{0,8},{4,0},{8,12},{12,4},{1,9},{5,1},{9,13},{13,5},{2,10},{6,2},{... | collective-permute-start | bytes 663560 | tf_op jit(solution)/shard_map/ppermute | solution.py:320
  47.6 1.4 %collective-permute-start.12 = (bf16[27,32,128]{2,1,0:T(8,128)(2,1)S(1)}, bf16[27,32,128]{2,1,0:T(8,128)(2,1)S(1)}, u32[]{:S(2)}, u32[]{:S(2)}) collective-permute-start(bf16[27,32,128]{2,1,0:T(8,128)(2,1)S(1)} %get-tuple-element.45), channel_id=1, source_target_pairs={{0,2},{2,0},{1,3},{3,1},{4,6},{6,4},{5,7},{7,5},{8,10},{10,8},{9,1... | collective-permute-start | bytes 663560 | tf_op jit(solution)/shard_map/ppermute | solution.py:317
  49.7 0.7 %collective-permute-start.11 = (bf16[27,32,128]{2,1,0:T(8,128)(2,1)S(1)}, bf16[27,32,128]{2,1,0:T(8,128)(2,1)S(1)}, u32[]{:S(2)}, u32[]{:S(2)}) collective-permute-start(bf16[27,32,128]{2,1,0:T(8,128)(2,1)S(1)} %add_2.2), channel_id=1, source_target_pairs={{0,4},{4,12},{8,0},{12,8},{1,5},{5,13},{9,1},{13,9},{2,6},{6,14},{... | collective-permute-start | bytes 663560 | tf_op jit(solution)/shard_map/ppermute | solution.py:320
  50.4 3.7 %collective-permute-done.8.rest_2_ = bf16[27,32,128]{2,1,0:T(8,128)(2,1)S(1)} collective-permute-done((bf16[27,32,128]{2,1,0:T(8,128)(2,1)S(1)}, bf16[27,32,128]{2,1,0:T(8,128)(2,1)S(1)}, u32[]{:S(2)}, u32[]{:S(2)}) %collective-permute-start.8) | collective-permute-done | bytes 221216 | tf_op jit(solution)/shard_map/ppermute | solution.py:320
  54.2 1.8 %collective-permute-done.12.came_ref = bf16[27,32,128]{2,1,0:T(8,128)(2,1)S(1)} collective-permute-done((bf16[27,32,128]{2,1,0:T(8,128)(2,1)S(1)}, bf16[27,32,128]{2,1,0:T(8,128)(2,1)S(1)}, u32[]{:S(2)}, u32[]{:S(2)}) %collective-permute-start.12) | collective-permute-done | bytes 221216 | tf_op jit(solution)/shard_map/ppermute | solution.py:317
  56.1 1.1 %collective-permute-start.13 = (bf16[27,32,128]{2,1,0:T(8,128)(2,1)S(1)}, bf16[27,32,128]{2,1,0:T(8,128)(2,1)S(1)}, u32[]{:S(2)}, u32[]{:S(2)}) collective-permute-start(bf16[27,32,128]{2,1,0:T(8,128)(2,1)S(1)} %add_2.3), channel_id=1, source_target_pairs={{0,4},{4,12},{8,0},{12,8},{1,5},{5,13},{9,1},{13,9},{2,6},{6,14},{... | collective-permute-start | bytes 663560 | tf_op jit(solution)/shard_map/ppermute | solution.py:320
  57.3 5.2 %collective-permute-done.14.rest_3_ = bf16[54,32,128]{2,1,0:T(8,128)(2,1)S(1)} collective-permute-done((bf16[54,32,128]{2,1,0:T(8,128)(2,1)S(1)}, bf16[54,32,128]{2,1,0:T(8,128)(2,1)S(1)}, u32[]{:S(2)}, u32[]{:S(2)}) %collective-permute-start.14) | collective-permute-done | bytes 442400 | tf_op jit(solution)/shard_map/ppermute | solution.py:317
  63.0 1.3 %last.1 = f32[12,32,576]{2,1,0:T(8,128)} custom-call(f32[54,32,128]{2,1,0:T(8,128)S(1)} %gather.1.rest_0_, bf16[27,32,128]{2,1,0:T(8,128)(2,1)S(1)} %collective-permute-done.11.rest_1_, bf16[27,32,128]{2,1,0:T(8,128)(2,1)S(1)} %collective-permute-done.13.rest_2_, bf16[54,32,128]{2,1,0:T(8,128)(2,1)S(1)} %collective-permute-done.14.rest_3_), custom_call_target="tpu_custom_call" | custom-call | flops 1000 | bytes 1000 | tf_op jit(solution)/shard_map/last/pallas_call | solution.py:378
  (24 shorter events, 4.7 us)
Async XLA Ops:
  0.0 10.1 %collective-permute-start = (bf16[32,6144]{1,0:T(8,128)(2,1)}, bf16[32,6144]{1,0:T(8,128)(2,1)S(1)}, u32[]{:S(2)}, u32[]{:S(2)}) collective-permute-start(bf16[32,6144]{1,0:T(8,128)(2,1)} %cells_ref.1), channel_id=1, source_target_pairs={{0,1},{1,0},{2,3},{3,2},{4,5},{5,4},{6,7},{7,6},{8,9},{9,8},{10,11... | collective-permute-start | bytes 1179656 | tf_op jit(solution)/shard_map/ppermute | solution.py:261
  1.4 10.7 %collective-permute-start.2 = (bf16[32,1536]{1,0:T(8,128)(2,1)S(1)}, bf16[32,1536]{1,0:T(8,128)(2,1)S(1)}, u32[]{:S(2)}, u32[]{:S(2)}) collective-permute-start(bf16[32,1536]{1,0:T(8,128)(2,1)S(1)} %get-tuple-element.49), channel_id=1, source_target_pairs={{2,4},{6,8},{10,12},{4,2},{8,6},{12,10},{3,5},{7,9},{11,13},{5,3},... | collective-permute-start | bytes 294920 | tf_op jit(solution)/shard_map/ppermute | solution.py:47
  2.1 10.0 %collective-permute-start.1 = (bf16[32,1536]{1,0:T(8,128)(2,1)S(1)}, bf16[32,1536]{1,0:T(8,128)(2,1)S(1)}, u32[]{:S(2)}, u32[]{:S(2)}) collective-permute-start(bf16[32,1536]{1,0:T(8,128)(2,1)S(1)} %get-tuple-element.50), channel_id=1, source_target_pairs={{0,2},{4,6},{8,10},{12,14},{2,0},{6,4},{10,8},{14,12},{1,3},{5,7},... | collective-permute-start | bytes 294920 | tf_op jit(solution)/shard_map/ppermute | solution.py:47
  8.2 1.9 %copy-start.1 = (bf16[32,6144]{1,0:T(8,128)(2,1)S(1)}, bf16[32,6144]{1,0:T(8,128)(2,1)}, u32[]{:S(2)}) copy-start(bf16[32,6144]{1,0:T(8,128)(2,1)} %cells_ref.1) | copy-start | bytes 1179652
  8.2 2.6 %copy-start = (bf16[96,20480]{1,0:T(8,128)(2,1)S(1)}, bf16[96,20480]{1,0:T(8,128)(2,1)}, u32[]{:S(2)}) copy-start(bf16[96,20480]{1,0:T(8,128)(2,1)} %jac_ref.1) | copy-start | bytes 11796484
  14.8 13.1 %collective-permute-start.3 = (bf16[54,32,128]{2,1,0:T(8,128)(2,1)S(1)}, bf16[54,32,128]{2,1,0:T(8,128)(2,1)S(1)}, u32[]{:S(2)}, u32[]{:S(2)}) collective-permute-start(bf16[54,32,128]{2,1,0:T(8,128)(2,1)S(1)} %get-tuple-element.35), channel_id=1, source_target_pairs={{0,2},{2,0},{1,3},{3,1},{4,6},{6,4},{5,7},{7,5},{8,10},{10,8},{9,1... | collective-permute-start | bytes 1327112 | tf_op jit(solution)/shard_map/ppermute | solution.py:317
  22.8 8.8 %collective-permute-start.5 = (bf16[27,32,128]{2,1,0:T(8,128)(2,1)S(1)}, bf16[27,32,128]{2,1,0:T(8,128)(2,1)S(1)}, u32[]{:S(2)}, u32[]{:S(2)}) collective-permute-start(bf16[27,32,128]{2,1,0:T(8,128)(2,1)S(1)} %get-tuple-element.37), channel_id=1, source_target_pairs={{0,2},{2,0},{1,3},{3,1},{4,6},{6,4},{5,7},{7,5},{8,10},{10,8},{9,1... | collective-permute-start | bytes 663560 | tf_op jit(solution)/shard_map/ppermute | solution.py:317
  28.0 19.6 %collective-permute-start.10 = (bf16[54,32,128]{2,1,0:T(8,128)(2,1)S(1)}, bf16[54,32,128]{2,1,0:T(8,128)(2,1)S(1)}, u32[]{:S(2)}, u32[]{:S(2)}) collective-permute-start(bf16[54,32,128]{2,1,0:T(8,128)(2,1)S(1)} %add_0.1), channel_id=1, source_target_pairs={{0,4},{12,8},{1,5},{13,9},{2,6},{14,10},{3,7},{15,11},{16,20},{28,... | collective-permute-start | bytes 1327112 | tf_op jit(solution)/shard_map/ppermute | solution.py:320
  30.4 17.2 %collective-permute-start.4 = (bf16[54,32,128]{2,1,0:T(8,128)(2,1)S(1)}, bf16[54,32,128]{2,1,0:T(8,128)(2,1)S(1)}, u32[]{:S(2)}, u32[]{:S(2)}) collective-permute-start(bf16[54,32,128]{2,1,0:T(8,128)(2,1)S(1)} %add_0.1), channel_id=1, source_target_pairs={{4,8},{8,4},{5,9},{9,5},{6,10},{10,6},{7,11},{11,7},{20,24},{24,20... | collective-permute-start | bytes 1327112 | tf_op jit(solution)/shard_map/ppermute | solution.py:320
  31.7 12.4 %collective-permute-start.6 = (bf16[27,32,128]{2,1,0:T(8,128)(2,1)S(1)}, bf16[27,32,128]{2,1,0:T(8,128)(2,1)S(1)}, u32[]{:S(2)}, u32[]{:S(2)}) collective-permute-start(bf16[27,32,128]{2,1,0:T(8,128)(2,1)S(1)} %add_1.2), channel_id=1, source_target_pairs={{0,8},{4,0},{8,12},{12,4},{1,9},{5,1},{9,13},{13,5},{2,10},{6,2},{... | collective-permute-start | bytes 663560 | tf_op jit(solution)/shard_map/ppermute | solution.py:320
  34.8 9.3 %collective-permute-start.9 = (bf16[27,32,128]{2,1,0:T(8,128)(2,1)S(1)}, bf16[27,32,128]{2,1,0:T(8,128)(2,1)S(1)}, u32[]{:S(2)}, u32[]{:S(2)}) collective-permute-start(bf16[27,32,128]{2,1,0:T(8,128)(2,1)S(1)} %get-tuple-element.42), channel_id=1, source_target_pairs={{0,2},{2,0},{1,3},{3,1},{4,6},{6,4},{5,7},{7,5},{8,10},{10,8},{9,1... | collective-permute-start | bytes 663560 | tf_op jit(solution)/shard_map/ppermute | solution.py:317
  35.7 10.1 %collective-permute-start.7 = (bf16[27,32,128]{2,1,0:T(8,128)(2,1)S(1)}, bf16[27,32,128]{2,1,0:T(8,128)(2,1)S(1)}, u32[]{:S(2)}, u32[]{:S(2)}) collective-permute-start(bf16[27,32,128]{2,1,0:T(8,128)(2,1)S(1)} %get-tuple-element.39), channel_id=1, source_target_pairs={{0,2},{2,0},{1,3},{3,1},{4,6},{6,4},{5,7},{7,5},{8,10},{10,8},{9,1... | collective-permute-start | bytes 663560 | tf_op jit(solution)/shard_map/ppermute | solution.py:317
  45.8 8.3 %collective-permute-start.8 = (bf16[27,32,128]{2,1,0:T(8,128)(2,1)S(1)}, bf16[27,32,128]{2,1,0:T(8,128)(2,1)S(1)}, u32[]{:S(2)}, u32[]{:S(2)}) collective-permute-start(bf16[27,32,128]{2,1,0:T(8,128)(2,1)S(1)} %add_1.3), channel_id=1, source_target_pairs={{0,8},{4,0},{8,12},{12,4},{1,9},{5,1},{9,13},{13,5},{2,10},{6,2},{... | collective-permute-start | bytes 663560 | tf_op jit(solution)/shard_map/ppermute | solution.py:320
  47.6 8.4 %collective-permute-start.12 = (bf16[27,32,128]{2,1,0:T(8,128)(2,1)S(1)}, bf16[27,32,128]{2,1,0:T(8,128)(2,1)S(1)}, u32[]{:S(2)}, u32[]{:S(2)}) collective-permute-start(bf16[27,32,128]{2,1,0:T(8,128)(2,1)S(1)} %get-tuple-element.45), channel_id=1, source_target_pairs={{0,2},{2,0},{1,3},{3,1},{4,6},{6,4},{5,7},{7,5},{8,10},{10,8},{9,1... | collective-permute-start | bytes 663560 | tf_op jit(solution)/shard_map/ppermute | solution.py:317
  49.0 13.5 %collective-permute-start.14 = (bf16[54,32,128]{2,1,0:T(8,128)(2,1)S(1)}, bf16[54,32,128]{2,1,0:T(8,128)(2,1)S(1)}, u32[]{:S(2)}, u32[]{:S(2)}) collective-permute-start(bf16[54,32,128]{2,1,0:T(8,128)(2,1)S(1)} %get-tuple-element.48), channel_id=1, source_target_pairs={{0,2},{2,0},{1,3},{3,1},{4,6},{6,4},{5,7},{7,5},{8,10},{10,8},{9,1... | collective-permute-start | bytes 1327112 | tf_op jit(solution)/shard_map/ppermute | solution.py:317
  49.7 12.8 %collective-permute-start.11 = (bf16[27,32,128]{2,1,0:T(8,128)(2,1)S(1)}, bf16[27,32,128]{2,1,0:T(8,128)(2,1)S(1)}, u32[]{:S(2)}, u32[]{:S(2)}) collective-permute-start(bf16[27,32,128]{2,1,0:T(8,128)(2,1)S(1)} %add_2.2), channel_id=1, source_target_pairs={{0,4},{4,12},{8,0},{12,8},{1,5},{5,13},{9,1},{13,9},{2,6},{6,14},{... | collective-permute-start | bytes 663560 | tf_op jit(solution)/shard_map/ppermute | solution.py:320
  56.1 6.9 %collective-permute-start.13 = (bf16[27,32,128]{2,1,0:T(8,128)(2,1)S(1)}, bf16[27,32,128]{2,1,0:T(8,128)(2,1)S(1)}, u32[]{:S(2)}, u32[]{:S(2)}) collective-permute-start(bf16[27,32,128]{2,1,0:T(8,128)(2,1)S(1)} %add_2.3), channel_id=1, source_target_pairs={{0,4},{4,12},{8,0},{12,8},{1,5},{5,13},{9,1},{13,9},{2,6},{6,14},{... | collective-permute-start | bytes 663560 | tf_op jit(solution)/shard_map/ppermute | solution.py:320

commit v3 on v2

--- a/solution.py
+++ b/solution.py
@@ -202,7 +202,7 @@
     near_ref[near_ref.shape[0] - 1] = jnp.zeros((32, 128), jnp.bfloat16)
     accumulate(0, elems, code_ref, list_ref, count_ref, rows_ref, near_ref, weight_ref, total)
     for k, out in enumerate(outs):
-        out[...] = total[1 + k * PAIRS:1 + (k + 1) * PAIRS].astype(out.dtype)
+        out[...] = total[1 + k * PAIRS // 2:1 + (k + 1) * PAIRS // 2].astype(out.dtype)
 
 
 def next_kernel(elems, call, cuts, code_ref, list_ref, count_ref, rows_ref, near_ref, weight_ref, *rest):
@@ -213,12 +213,12 @@
         out[...] = total[start + at.start:start + at.stop].astype(out.dtype)
 
 
-def add_kernel(start, kept_ref, came_ref, *rest):
+def add_kernel(start, joins, kept_ref, came_ref, *rest):
     out_ref = rest[-1]
-    at = slice(start, start + out_ref.shape[0])
-    value = kept_ref[at] + came_ref[...].astype(jnp.float32)
-    for more_ref in rest[:-1]:
-        value = value + more_ref[at].astype(jnp.float32)
+    value = kept_ref[start:start + out_ref.shape[0]] + came_ref[...].astype(jnp.float32)
+    if joins is not None:
+        outer = (lax.axis_index("elem") + 1) % 4 < 2
+        value = value + jnp.where(outer == joins, rest[0][...].astype(jnp.float32), 0.0)
     out_ref[...] = value.astype(out_ref.dtype)
 
 
@@ -299,12 +299,11 @@
     )(jacobian, own_near)
 
     table = (PAIRS, half, 2 * B)
-    sent, near = pl.pallas_call(
+    *sent, near = pl.pallas_call(
         functools.partial(first_kernel, elems),
         in_specs=[SMEM] * 3 + [VMEM] * 5,
-        out_specs=[VMEM] * 2,
-        out_shape=[
-            jax.ShapeDtypeStruct(table, jnp.bfloat16),
+        out_specs=[VMEM] * 3,
+        out_shape=[jax.ShapeDtypeStruct((PAIRS // 2, half, 2 * B), jnp.bfloat16)] * 2 + [
             jax.ShapeDtypeStruct((elems + 2 * rim + 1, half, 2 * B), jnp.bfloat16),
         ],
         scratch_shapes=[pltpu.VMEM((1 + PAIRS, half, 2 * B), jnp.float32)],
@@ -322,9 +321,9 @@
     def behind(block, *others):
         return lax.optimization_barrier((block, *others))[0]
 
-    def summed(p, at, block, *more):
+    def summed(p, at, block, joins=None, *more):
         return pl.pallas_call(
-            functools.partial(add_kernel, at.start),
+            functools.partial(add_kernel, at.start, joins),
             in_specs=[VMEM] * (2 + len(more)),
             out_specs=VMEM,
             out_shape=jax.ShapeDtypeStruct(block.shape, jnp.bfloat16),
@@ -336,7 +335,7 @@
     whole, halves = slice(0, PAIRS), [slice(0, PAIRS // 2), slice(PAIRS // 2, PAIRS)]
     pieces = {p: halves if p < 3 else [whole] for p in range(1, count)}
     cuts = [(t, at) for t, (p, mine) in enumerate(plan[1]) for at in ([whole] if mine else pieces[p])]
-    came = {0: [across(sent)]}
+    came = {0: [across(block) for block in sent]}
     outs = pl.pallas_call(
         functools.partial(next_kernel, elems, 1, cuts),
         in_specs=[SMEM] * 3 + [VMEM] * 3,
@@ -351,29 +350,28 @@
         name="next",
     )(codes, lists, counts, rows, near, weights)
     kept = outs[-count:]
-    first = summed(0, whole, came[0][0])
     sent = outs[:-count]
-    straight = along(first, [(1, 2), (2, 1)])
-    joined = along(first, [(0, 1), (3, 2)])
-    came[1] = [across(sent[0]), across(behind(sent[1], first))]
-    ready1 = [summed(1, at, block) for at, block in zip(halves, came[1])]
+    ready0 = [summed(0, at, block) for at, block in zip(halves, came[0])]
+    joined = [along(block, [(y, y ^ 1) for y in range(count)]) for block in ready0]
+    came[1] = [across(sent[0]), across(behind(sent[1], came[0][1]))]
+    ready1 = [summed(1, at, block, True, more) for at, block, more in zip(halves, came[1], joined)]
     round1 = [along(block, ROUNDS[0]) for block in ready1]
-    came[2] = [across(behind(sent[2], came[1][0])), across(behind(sent[3], came[1][1], straight, joined))]
+    came[2] = [across(behind(sent[2], joined[0])), across(behind(sent[3], came[1][1]))]
+    came[2][0] = behind(came[2][0], round1[0])
     came[2][1] = behind(came[2][1], *round1)
-    came[2][0] = behind(came[2][0], round1[0])
-    ready2 = [summed(2, at, block, joined) for at, block in zip(halves, came[2])]
+    ready2 = [summed(2, at, block, False, more) for at, block, more in zip(halves, came[2], joined)]
     round2 = [along(block, ROUNDS[1]) for block in ready2]
     came[3] = [across(behind(sent[4], came[2][0]))]
 
     total = pl.pallas_call(
         gather_kernel,
-        in_specs=[VMEM] * 4,
+        in_specs=[VMEM] * 3,
         out_specs=VMEM,
         out_shape=jax.ShapeDtypeStruct(table, jnp.float32),
         compiler_params=params(),
         cost_estimate=pl.CostEstimate(flops=1_000_000_000, bytes_accessed=1000, transcendentals=0),
         name="gather",
-    )(kept[count - 1], straight, *round1)
+    )(kept[count - 1], *round1)
     parts = round2 + came[count - 1]
     coarse = pl.pallas_call(
         last_kernel,

time: 64.4 us -> 59.1 us (0.918)
  waiting for transfers between devices: 23.3 us -> 15.2 us
  starting transfers between devices: 23.5 us -> 25.8 us
    ppermute x6 -> x7, waiting for transfers between devices: 11.9 us -> 6.47 us  [across(): return lax.ppermute(block, 'sub', [(0, 1), (1, 0)])]
    ppermute x6, waiting for transfers between devices: 11.4 us -> 8.73 us  [along(): return lax.ppermute(block, 'elem', pairs)]
    ppermute x6, starting transfers between devices: 9.67 us -> 11.3 us  [along(): return lax.ppermute(block, 'elem', pairs)]
    ppermute x6 -> x7, starting transfers between devices: 7.36 us -> 7.97 us  [across(): return lax.ppermute(block, 'sub', [(0, 1), (1, 0)])]
  transfers between devices with their start and end apart: 15 -> 16, of which waited for: 8 -> 8; matrix products, arithmetic and copies ran while one was open for 3% -> 3% of each run, Pallas kernels for 18% -> 21%
where the time goes in v3:
time: 59.1 us; the launch traced here: 58.4 us
  starting transfers between devices  25.8 us (44%)
  Pallas kernels  15.6 us (26%)
  waiting for transfers between devices  15.2 us (26%)
  other arithmetic  1.67 us (3%)
    ppermute x6, starting transfers between devices, along(): return lax.ppermute(block, 'elem', pairs)  11.3 us
    ppermute x6, waiting for transfers between devices, along(): return lax.ppermute(block, 'elem', pairs)  8.73 us
    ppermute x7, starting transfers between devices, across(): return lax.ppermute(block, 'sub', [(0, 1), (1, 0)])  7.97 us
    pallas_call x1, Pallas kernels, dense(): pl.pallas_call(functools.partial(next_kernel, elems, 1, cuts), in_specs=[...  7.75 us
    ppermute x7, waiting for transfers between devices, across(): return lax.ppermute(block, 'sub', [(0, 1), (1, 0)])  6.47 us
    ppermute x2, starting transfers between devices, swap(): return lax.ppermute(block, axes, pairs + [(j, i) for i, j in pairs])  6.01 us
    pallas_call x1, Pallas kernels, dense(): pl.pallas_call(functools.partial(first_kernel, elems), in_specs=[SMEM] *...  2.13 us
    pallas_call x1, Pallas kernels, dense(): pl.pallas_call(functools.partial(lists_kernel, elems, count), in_specs=[S...  1.89 us
  transfers between devices with their start and end apart: 16, of which 8 were waited for; matrix products, arithmetic and copies ran while one was open for 3% of the time, Pallas kernels for 21%

profile of v3, /device:TPU:0, one launch (start us, length us, event | category | flops | bytes accessed | tf_op | source)
XLA Modules:
  0.0 58.4 jit_solution(17833890599725729694)
XLA Ops:
  0.5 1.0 %broadcast_select_fusion = (bf16[32,1536]{1,0:T(8,128)(2,1)S(1)}, bf16[32,1536]{1,0:T(8,128)(2,1)S(1)}) fusion(pred[]{:T(512)S(6)} %eq.5, bf16[32,6144]{1,0:T(8,128)(2,1)} %cells_ref.1), kind=kLoop, calls=%fused_computation | loop fusion | flops 98304 | bytes 393217 | tf_op jit(solution)/shard_map/jit(_where)/select_n | solution.py:49
  2.1 5.3 %collective-permute-start.1 = (bf16[32,1536]{1,0:T(8,128)(2,1)S(1)}, bf16[32,1536]{1,0:T(8,128)(2,1)S(1)}, u32[]{:S(2)}, u32[]{:S(2)}) collective-permute-start(bf16[32,1536]{1,0:T(8,128)(2,1)S(1)} %get-tuple-element.52), channel_id=1, source_target_pairs={{0,2},{4,6},{8,10},{12,14},{2,0},{6,4},{10,8},{14,12},{1,3},{5,7},... | collective-permute-start | bytes 294920 | tf_op jit(solution)/shard_map/ppermute | solution.py:47
  8.2 1.9 %lists.1 = (s32[16,128]{1,0:T(8,128)S(1)}, s32[2,104]{1,0:T(2,128)S(1)}, s32[2]{0:T(128)S(1)}) custom-call(s32[11,96]{1,0:T(8,128)S(1)} %pad_add_fusion.ints_ref.again_ref, s32[11,96]{1,0:T(8,128)S(1)} %pad_add_fusion.ints_ref.again_ref), custom_call_target="tpu_custom_call" | custom-call | flops 20000000000 | bytes 1000 | tf_op jit(solution)/shard_map/lists/pallas_call | solution.py:266
  10.8 1.3 %rows.1.rows_ref = bf16[96,160,128]{2,1,0:T(8,128)(2,1)S(1)} custom-call(bf16[96,20480]{1,0:T(8,128)(2,1)S(1)} %copy-done, bf16[96,32,128]{2,1,0:T(8,128)(2,1)S(1)} %get-tuple-element.31.after_ref.own_ref), custom_call_target="tpu_custom_call" | custom-call | flops 1000 | bytes 1000 | tf_op jit(solution)/shard_map/rows/pallas_call | solution.py:291
  12.1 2.1 %first.1 = (bf16[27,32,128]{2,1,0:T(8,128)(2,1)S(1)}, bf16[27,32,128]{2,1,0:T(8,128)(2,1)S(1)}, bf16[145,32,128]{2,1,0:T(8,128)(2,1)S(1)}) custom-call(s32[16,128]{1,0:T(8,128)S(1)} %get-tuple-element.28.after_ref.code_ref, s32[2,104]{1,0:T(2,128)S(1)} %get-tuple-element.29.list_ref, s32[2]{0:T(128)S(1)} %get-tuple-element.30.count_ref, ...), custom_call_target="tpu_custom_call" | custom-call | flops 1000 | bytes 1000 | tf_op jit(solution)/shard_map/first/pallas_call | solution.py:302
  14.2 2.5 %collective-permute-start.4 = (bf16[27,32,128]{2,1,0:T(8,128)(2,1)S(1)}, bf16[27,32,128]{2,1,0:T(8,128)(2,1)S(1)}, u32[]{:S(2)}, u32[]{:S(2)}) collective-permute-start(bf16[27,32,128]{2,1,0:T(8,128)(2,1)S(1)} %get-tuple-element.38), channel_id=1, source_target_pairs={{0,2},{2,0},{1,3},{3,1},{4,6},{6,4},{5,7},{7,5},{8,10},{10,8},{9,1... | collective-permute-start | bytes 663560 | tf_op jit(solution)/shard_map/ppermute | solution.py:316
  16.8 7.8 %next.1 = (bf16[27,32,128]{2,1,0:T(8,128)(2,1)S(1)}, bf16[27,32,128]{2,1,0:T(8,128)(2,1)S(1)}, bf16[27,32,128]{2,1,0:T(8,128)(2,1)S(1)}, bf16[27,32,128]{2,1,0:T...) custom-call(s32[16,128]{1,0:T(8,128)S(1)} %get-tuple-element.28.afte, ...), custom_call_target="tpu_custom_call" | custom-call | flops 20000000000 | bytes 1000 | tf_op jit(solution)/shard_map/next/pallas_call | solution.py:339
  24.6 1.7 %collective-permute-start.5 = (bf16[27,32,128]{2,1,0:T(8,128)(2,1)S(1)}, bf16[27,32,128]{2,1,0:T(8,128)(2,1)S(1)}, u32[]{:S(2)}, u32[]{:S(2)}) collective-permute-start(bf16[27,32,128]{2,1,0:T(8,128)(2,1)S(1)} %add_0.2), channel_id=1, source_target_pairs={{0,4},{4,0},{8,12},{12,8},{1,5},{5,1},{9,13},{13,9},{2,6},{6,2},{1... | collective-permute-start | bytes 663560 | tf_op jit(solution)/shard_map/ppermute | solution.py:319
  27.1 1.7 %collective-permute-start.8 = (bf16[27,32,128]{2,1,0:T(8,128)(2,1)S(1)}, bf16[27,32,128]{2,1,0:T(8,128)(2,1)S(1)}, u32[]{:S(2)}, u32[]{:S(2)}) collective-permute-start(bf16[27,32,128]{2,1,0:T(8,128)(2,1)S(1)} %get-tuple-element.41), channel_id=1, source_target_pairs={{0,2},{2,0},{1,3},{3,1},{4,6},{6,4},{5,7},{7,5},{8,10},{10,8},{9,1... | collective-permute-start | bytes 663560 | tf_op jit(solution)/shard_map/ppermute | solution.py:316
  28.9 2.0 %collective-permute-start.9 = (bf16[27,32,128]{2,1,0:T(8,128)(2,1)S(1)}, bf16[27,32,128]{2,1,0:T(8,128)(2,1)S(1)}, u32[]{:S(2)}, u32[]{:S(2)}) collective-permute-start(bf16[27,32,128]{2,1,0:T(8,128)(2,1)S(1)} %add_0.3), channel_id=1, source_target_pairs={{0,4},{4,0},{8,12},{12,8},{1,5},{5,1},{9,13},{13,9},{2,6},{6,2},{1... | collective-permute-start | bytes 663560 | tf_op jit(solution)/shard_map/ppermute | solution.py:319
  30.9 2.1 %collective-permute-done.5.rest_0_ = bf16[27,32,128]{2,1,0:T(8,128)(2,1)S(1)} collective-permute-done((bf16[27,32,128]{2,1,0:T(8,128)(2,1)S(1)}, bf16[27,32,128]{2,1,0:T(8,128)(2,1)S(1)}, u32[]{:S(2)}, u32[]{:S(2)}) %collective-permute-start.5) | collective-permute-done | bytes 221216 | tf_op jit(solution)/shard_map/ppermute | solution.py:319
  33.0 1.5 %collective-permute-start.11 = (bf16[27,32,128]{2,1,0:T(8,128)(2,1)S(1)}, bf16[27,32,128]{2,1,0:T(8,128)(2,1)S(1)}, u32[]{:S(2)}, u32[]{:S(2)}) collective-permute-start(bf16[27,32,128]{2,1,0:T(8,128)(2,1)S(1)} %get-tuple-element.44), channel_id=1, source_target_pairs={{0,2},{2,0},{1,3},{3,1},{4,6},{6,4},{5,7},{7,5},{8,10},{10,8},{9,1... | collective-permute-start | bytes 663560 | tf_op jit(solution)/shard_map/ppermute | solution.py:316
  34.8 2.5 %collective-permute-start.6 = (bf16[27,32,128]{2,1,0:T(8,128)(2,1)S(1)}, bf16[27,32,128]{2,1,0:T(8,128)(2,1)S(1)}, u32[]{:S(2)}, u32[]{:S(2)}) collective-permute-start(bf16[27,32,128]{2,1,0:T(8,128)(2,1)S(1)} %add_1.2), channel_id=1, source_target_pairs={{0,8},{4,0},{8,12},{12,4},{1,9},{5,1},{9,13},{13,5},{2,10},{6,2},{... | collective-permute-start | bytes 663560 | tf_op jit(solution)/shard_map/ppermute | solution.py:319
  37.3 2.1 %collective-permute-done.8.came_ref = bf16[27,32,128]{2,1,0:T(8,128)(2,1)S(1)} collective-permute-done((bf16[27,32,128]{2,1,0:T(8,128)(2,1)S(1)}, bf16[27,32,128]{2,1,0:T(8,128)(2,1)S(1)}, u32[]{:S(2)}, u32[]{:S(2)}) %collective-permute-start.8) | collective-permute-done | bytes 221216 | tf_op jit(solution)/shard_map/ppermute | solution.py:316
  39.4 0.7 %collective-permute-start.13 = (bf16[27,32,128]{2,1,0:T(8,128)(2,1)S(1)}, bf16[27,32,128]{2,1,0:T(8,128)(2,1)S(1)}, u32[]{:S(2)}, u32[]{:S(2)}) collective-permute-start(bf16[27,32,128]{2,1,0:T(8,128)(2,1)S(1)} %get-tuple-element.47), channel_id=1, source_target_pairs={{0,2},{2,0},{1,3},{3,1},{4,6},{6,4},{5,7},{7,5},{8,10},{10,8},{9,1... | collective-permute-start | bytes 663560 | tf_op jit(solution)/shard_map/ppermute | solution.py:316
  40.2 1.9 %collective-permute-start.10 = (bf16[27,32,128]{2,1,0:T(8,128)(2,1)S(1)}, bf16[27,32,128]{2,1,0:T(8,128)(2,1)S(1)}, u32[]{:S(2)}, u32[]{:S(2)}) collective-permute-start(bf16[27,32,128]{2,1,0:T(8,128)(2,1)S(1)} %add_1.3), channel_id=1, source_target_pairs={{0,8},{4,0},{8,12},{12,4},{1,9},{5,1},{9,13},{13,5},{2,10},{6,2},{... | collective-permute-start | bytes 663560 | tf_op jit(solution)/shard_map/ppermute | solution.py:319
  42.1 2.0 %collective-permute-done.11.came_ref = bf16[27,32,128]{2,1,0:T(8,128)(2,1)S(1)} collective-permute-done((bf16[27,32,128]{2,1,0:T(8,128)(2,1)S(1)}, bf16[27,32,128]{2,1,0:T(8,128)(2,1)S(1)}, u32[]{:S(2)}, u32[]{:S(2)}) %collective-permute-start.11) | collective-permute-done | bytes 221216 | tf_op jit(solution)/shard_map/ppermute | solution.py:316
  44.1 0.7 %collective-permute-start.15 = (bf16[54,32,128]{2,1,0:T(8,128)(2,1)S(1)}, bf16[54,32,128]{2,1,0:T(8,128)(2,1)S(1)}, u32[]{:S(2)}, u32[]{:S(2)}) collective-permute-start(bf16[54,32,128]{2,1,0:T(8,128)(2,1)S(1)} %get-tuple-element.50), channel_id=1, source_target_pairs={{0,2},{2,0},{1,3},{3,1},{4,6},{6,4},{5,7},{7,5},{8,10},{10,8},{9,1... | collective-permute-start | bytes 1327112 | tf_op jit(solution)/shard_map/ppermute | solution.py:316
  45.0 1.8 %collective-permute-start.12 = (bf16[27,32,128]{2,1,0:T(8,128)(2,1)S(1)}, bf16[27,32,128]{2,1,0:T(8,128)(2,1)S(1)}, u32[]{:S(2)}, u32[]{:S(2)}) collective-permute-start(bf16[27,32,128]{2,1,0:T(8,128)(2,1)S(1)} %add_2.2), channel_id=1, source_target_pairs={{0,4},{4,12},{8,0},{12,8},{1,5},{5,13},{9,1},{13,9},{2,6},{6,14},{... | collective-permute-start | bytes 663560 | tf_op jit(solution)/shard_map/ppermute | solution.py:319
  46.7 2.1 %collective-permute-done.13.came_ref = bf16[27,32,128]{2,1,0:T(8,128)(2,1)S(1)} collective-permute-done((bf16[27,32,128]{2,1,0:T(8,128)(2,1)S(1)}, bf16[27,32,128]{2,1,0:T(8,128)(2,1)S(1)}, u32[]{:S(2)}, u32[]{:S(2)}) %collective-permute-start.13) | collective-permute-done | bytes 221216 | tf_op jit(solution)/shard_map/ppermute | solution.py:316
  49.0 1.5 %collective-permute-start.14 = (bf16[27,32,128]{2,1,0:T(8,128)(2,1)S(1)}, bf16[27,32,128]{2,1,0:T(8,128)(2,1)S(1)}, u32[]{:S(2)}, u32[]{:S(2)}) collective-permute-start(bf16[27,32,128]{2,1,0:T(8,128)(2,1)S(1)} %add_2.3), channel_id=1, source_target_pairs={{0,4},{4,12},{8,0},{12,8},{1,5},{5,13},{9,1},{13,9},{2,6},{6,14},{... | collective-permute-start | bytes 663560 | tf_op jit(solution)/shard_map/ppermute | solution.py:319
  50.6 3.9 %collective-permute-done.12.rest_1_ = bf16[27,32,128]{2,1,0:T(8,128)(2,1)S(1)} collective-permute-done((bf16[27,32,128]{2,1,0:T(8,128)(2,1)S(1)}, bf16[27,32,128]{2,1,0:T(8,128)(2,1)S(1)}, u32[]{:S(2)}, u32[]{:S(2)}) %collective-permute-start.12) | collective-permute-done | bytes 221216 | tf_op jit(solution)/shard_map/ppermute | solution.py:319
  54.4 2.8 %collective-permute-done.14.rest_2_ = bf16[27,32,128]{2,1,0:T(8,128)(2,1)S(1)} collective-permute-done((bf16[27,32,128]{2,1,0:T(8,128)(2,1)S(1)}, bf16[27,32,128]{2,1,0:T(8,128)(2,1)S(1)}, u32[]{:S(2)}, u32[]{:S(2)}) %collective-permute-start.14) | collective-permute-done | bytes 221216 | tf_op jit(solution)/shard_map/ppermute | solution.py:319
  57.2 1.3 %last.1 = f32[12,32,576]{2,1,0:T(8,128)} custom-call(f32[54,32,128]{2,1,0:T(8,128)S(1)} %gather.1.rest_0_, bf16[27,32,128]{2,1,0:T(8,128)(2,1)S(1)} %collective-permute-done.12.rest_1_, bf16[27,32,128]{2,1,0:T(8,128)(2,1)S(1)} %collective-permute-done.14.rest_2_, bf16[54,32,128]{2,1,0:T(8,128)(2,1)S(1)} %collective-permute-done.15.rest_3_), custom_call_target="tpu_custom_call" | custom-call | flops 1000 | bytes 1000 | tf_op jit(solution)/shard_map/last/pallas_call | solution.py:376
  (27 shorter events, 4.2 us)
Async XLA Ops:
  0.0 10.1 %collective-permute-start = (bf16[32,6144]{1,0:T(8,128)(2,1)}, bf16[32,6144]{1,0:T(8,128)(2,1)S(1)}, u32[]{:S(2)}, u32[]{:S(2)}) collective-permute-start(bf16[32,6144]{1,0:T(8,128)(2,1)} %cells_ref.1), channel_id=1, source_target_pairs={{0,1},{1,0},{2,3},{3,2},{4,5},{5,4},{6,7},{7,6},{8,9},{9,8},{10,11... | collective-permute-start | bytes 1179656 | tf_op jit(solution)/shard_map/ppermute | solution.py:261
  1.4 10.7 %collective-permute-start.2 = (bf16[32,1536]{1,0:T(8,128)(2,1)S(1)}, bf16[32,1536]{1,0:T(8,128)(2,1)S(1)}, u32[]{:S(2)}, u32[]{:S(2)}) collective-permute-start(bf16[32,1536]{1,0:T(8,128)(2,1)S(1)} %get-tuple-element.51), channel_id=1, source_target_pairs={{2,4},{6,8},{10,12},{4,2},{8,6},{12,10},{3,5},{7,9},{11,13},{5,3},... | collective-permute-start | bytes 294920 | tf_op jit(solution)/shard_map/ppermute | solution.py:47
  2.1 10.0 %collective-permute-start.1 = (bf16[32,1536]{1,0:T(8,128)(2,1)S(1)}, bf16[32,1536]{1,0:T(8,128)(2,1)S(1)}, u32[]{:S(2)}, u32[]{:S(2)}) collective-permute-start(bf16[32,1536]{1,0:T(8,128)(2,1)S(1)} %get-tuple-element.52), channel_id=1, source_target_pairs={{0,2},{4,6},{8,10},{12,14},{2,0},{6,4},{10,8},{14,12},{1,3},{5,7},... | collective-permute-start | bytes 294920 | tf_op jit(solution)/shard_map/ppermute | solution.py:47
  8.2 1.9 %copy-start.1 = (bf16[32,6144]{1,0:T(8,128)(2,1)S(1)}, bf16[32,6144]{1,0:T(8,128)(2,1)}, u32[]{:S(2)}) copy-start(bf16[32,6144]{1,0:T(8,128)(2,1)} %cells_ref.1) | copy-start | bytes 1179652
  8.2 2.6 %copy-start = (bf16[96,20480]{1,0:T(8,128)(2,1)S(1)}, bf16[96,20480]{1,0:T(8,128)(2,1)}, u32[]{:S(2)}) copy-start(bf16[96,20480]{1,0:T(8,128)(2,1)} %jac_ref.1) | copy-start | bytes 11796484
  14.2 10.3 %collective-permute-start.4 = (bf16[27,32,128]{2,1,0:T(8,128)(2,1)S(1)}, bf16[27,32,128]{2,1,0:T(8,128)(2,1)S(1)}, u32[]{:S(2)}, u32[]{:S(2)}) collective-permute-start(bf16[27,32,128]{2,1,0:T(8,128)(2,1)S(1)} %get-tuple-element.38), channel_id=1, source_target_pairs={{0,2},{2,0},{1,3},{3,1},{4,6},{6,4},{5,7},{7,5},{8,10},{10,8},{9,1... | collective-permute-start | bytes 663560 | tf_op jit(solution)/shard_map/ppermute | solution.py:316
  16.7 10.4 %collective-permute-start.7 = (bf16[27,32,128]{2,1,0:T(8,128)(2,1)S(1)}, bf16[27,32,128]{2,1,0:T(8,128)(2,1)S(1)}, u32[]{:S(2)}, u32[]{:S(2)}) collective-permute-start(bf16[27,32,128]{2,1,0:T(8,128)(2,1)S(1)} %get-tuple-element.40), channel_id=1, source_target_pairs={{0,2},{2,0},{1,3},{3,1},{4,6},{6,4},{5,7},{7,5},{8,10},{10,8},{9,1... | collective-permute-start | bytes 663560 | tf_op jit(solution)/shard_map/ppermute | solution.py:316
  24.6 8.4 %collective-permute-start.5 = (bf16[27,32,128]{2,1,0:T(8,128)(2,1)S(1)}, bf16[27,32,128]{2,1,0:T(8,128)(2,1)S(1)}, u32[]{:S(2)}, u32[]{:S(2)}) collective-permute-start(bf16[27,32,128]{2,1,0:T(8,128)(2,1)S(1)} %add_0.2), channel_id=1, source_target_pairs={{0,4},{4,0},{8,12},{12,8},{1,5},{5,1},{9,13},{13,9},{2,6},{6,2},{1... | collective-permute-start | bytes 663560 | tf_op jit(solution)/shard_map/ppermute | solution.py:319
  26.3 8.4 %collective-permute-start.3 = (bf16[27,32,128]{2,1,0:T(8,128)(2,1)S(1)}, bf16[27,32,128]{2,1,0:T(8,128)(2,1)S(1)}, u32[]{:S(2)}, u32[]{:S(2)}) collective-permute-start(bf16[27,32,128]{2,1,0:T(8,128)(2,1)S(1)} %get-tuple-element.36), channel_id=1, source_target_pairs={{0,2},{2,0},{1,3},{3,1},{4,6},{6,4},{5,7},{7,5},{8,10},{10,8},{9,1... | collective-permute-start | bytes 663560 | tf_op jit(solution)/shard_map/ppermute | solution.py:316
  27.1 12.3 %collective-permute-start.8 = (bf16[27,32,128]{2,1,0:T(8,128)(2,1)S(1)}, bf16[27,32,128]{2,1,0:T(8,128)(2,1)S(1)}, u32[]{:S(2)}, u32[]{:S(2)}) collective-permute-start(bf16[27,32,128]{2,1,0:T(8,128)(2,1)S(1)} %get-tuple-element.41), channel_id=1, source_target_pairs={{0,2},{2,0},{1,3},{3,1},{4,6},{6,4},{5,7},{7,5},{8,10},{10,8},{9,1... | collective-permute-start | bytes 663560 | tf_op jit(solution)/shard_map/ppermute | solution.py:316
  28.9 11.2 %collective-permute-start.9 = (bf16[27,32,128]{2,1,0:T(8,128)(2,1)S(1)}, bf16[27,32,128]{2,1,0:T(8,128)(2,1)S(1)}, u32[]{:S(2)}, u32[]{:S(2)}) collective-permute-start(bf16[27,32,128]{2,1,0:T(8,128)(2,1)S(1)} %add_0.3), channel_id=1, source_target_pairs={{0,4},{4,0},{8,12},{12,8},{1,5},{5,1},{9,13},{13,9},{2,6},{6,2},{1... | collective-permute-start | bytes 663560 | tf_op jit(solution)/shard_map/ppermute | solution.py:319
  33.0 11.1 %collective-permute-start.11 = (bf16[27,32,128]{2,1,0:T(8,128)(2,1)S(1)}, bf16[27,32,128]{2,1,0:T(8,128)(2,1)S(1)}, u32[]{:S(2)}, u32[]{:S(2)}) collective-permute-start(bf16[27,32,128]{2,1,0:T(8,128)(2,1)S(1)} %get-tuple-element.44), channel_id=1, source_target_pairs={{0,2},{2,0},{1,3},{3,1},{4,6},{6,4},{5,7},{7,5},{8,10},{10,8},{9,1... | collective-permute-start | bytes 663560 | tf_op jit(solution)/shard_map/ppermute | solution.py:316
  34.8 9.4 %collective-permute-start.6 = (bf16[27,32,128]{2,1,0:T(8,128)(2,1)S(1)}, bf16[27,32,128]{2,1,0:T(8,128)(2,1)S(1)}, u32[]{:S(2)}, u32[]{:S(2)}) collective-permute-start(bf16[27,32,128]{2,1,0:T(8,128)(2,1)S(1)} %add_1.2), channel_id=1, source_target_pairs={{0,8},{4,0},{8,12},{12,4},{1,9},{5,1},{9,13},{13,5},{2,10},{6,2},{... | collective-permute-start | bytes 663560 | tf_op jit(solution)/shard_map/ppermute | solution.py:319
  39.4 9.5 %collective-permute-start.13 = (bf16[27,32,128]{2,1,0:T(8,128)(2,1)S(1)}, bf16[27,32,128]{2,1,0:T(8,128)(2,1)S(1)}, u32[]{:S(2)}, u32[]{:S(2)}) collective-permute-start(bf16[27,32,128]{2,1,0:T(8,128)(2,1)S(1)} %get-tuple-element.47), channel_id=1, source_target_pairs={{0,2},{2,0},{1,3},{3,1},{4,6},{6,4},{5,7},{7,5},{8,10},{10,8},{9,1... | collective-permute-start | bytes 663560 | tf_op jit(solution)/shard_map/ppermute | solution.py:316
  40.2 8.7 %collective-permute-start.10 = (bf16[27,32,128]{2,1,0:T(8,128)(2,1)S(1)}, bf16[27,32,128]{2,1,0:T(8,128)(2,1)S(1)}, u32[]{:S(2)}, u32[]{:S(2)}) collective-permute-start(bf16[27,32,128]{2,1,0:T(8,128)(2,1)S(1)} %add_1.3), channel_id=1, source_target_pairs={{0,8},{4,0},{8,12},{12,4},{1,9},{5,1},{9,13},{13,5},{2,10},{6,2},{... | collective-permute-start | bytes 663560 | tf_op jit(solution)/shard_map/ppermute | solution.py:319
  44.1 13.0 %collective-permute-start.15 = (bf16[54,32,128]{2,1,0:T(8,128)(2,1)S(1)}, bf16[54,32,128]{2,1,0:T(8,128)(2,1)S(1)}, u32[]{:S(2)}, u32[]{:S(2)}) collective-permute-start(bf16[54,32,128]{2,1,0:T(8,128)(2,1)S(1)} %get-tuple-element.50), channel_id=1, source_target_pairs={{0,2},{2,0},{1,3},{3,1},{4,6},{6,4},{5,7},{7,5},{8,10},{10,8},{9,1... | collective-permute-start | bytes 1327112 | tf_op jit(solution)/shard_map/ppermute | solution.py:316
  45.0 9.4 %collective-permute-start.12 = (bf16[27,32,128]{2,1,0:T(8,128)(2,1)S(1)}, bf16[27,32,128]{2,1,0:T(8,128)(2,1)S(1)}, u32[]{:S(2)}, u32[]{:S(2)}) collective-permute-start(bf16[27,32,128]{2,1,0:T(8,128)(2,1)S(1)} %add_2.2), channel_id=1, source_target_pairs={{0,4},{4,12},{8,0},{12,8},{1,5},{5,13},{9,1},{13,9},{2,6},{6,14},{... | collective-permute-start | bytes 663560 | tf_op jit(solution)/shard_map/ppermute | solution.py:319
  49.0 8.2 %collective-permute-start.14 = (bf16[27,32,128]{2,1,0:T(8,128)(2,1)S(1)}, bf16[27,32,128]{2,1,0:T(8,128)(2,1)S(1)}, u32[]{:S(2)}, u32[]{:S(2)}) collective-permute-start(bf16[27,32,128]{2,1,0:T(8,128)(2,1)S(1)} %add_2.3), channel_id=1, source_target_pairs={{0,4},{4,12},{8,0},{12,8},{1,5},{5,13},{9,1},{13,9},{2,6},{6,14},{... | collective-permute-start | bytes 663560 | tf_op jit(solution)/shard_map/ppermute | solution.py:319

commit v4 on v3

--- a/solution.py
+++ b/solution.py
@@ -66,7 +66,7 @@
 def call_plan(count):
     sent = [(p, 0) for p in range(count)]
     kept = [(p, 1) for p in range(count)]
-    return [sent[:1], sent[1:] + kept]
+    return [sent[:1], [sent[1], kept[0]], [sent[2], kept[1]], [sent[3], kept[2], kept[3]]]
 
 
 def lists_kernel(elems, count, ints_ref, again_ref, code_ref, list_ref, count_ref):
@@ -83,7 +83,7 @@
                     here = (z == y) & ((me == x) if mine else (me != x))
                     for i in range(2):
                         values[i] = jnp.where(here, code[place_of(y, d), mine][i], values[i])
-            calls += values[0] << (2 * d + x)
+            calls += values[0] << (2 * (2 * d + x))
             numbers += values[1] << (3 * (2 * d + x))
 
     device = z * lax.axis_size("sub") + me
@@ -94,18 +94,19 @@
     code_ref[TARGET:TARGET + FACES + 1, :elems] = (
         again_ref[MEMBER:MEMBER + 1, :] * CS + again_ref[SLOT:SLOT + FACES + 1, :])
 
-    zero, one = 0, 0
+    lengths = 0
     for start in range(0, elems, STEP):
         owners = [ints_ref[0, e] for e in range(start, start + STEP)]
         for e, owner in zip(range(start, start + STEP), owners):
-            call = (calls >> owner) & 1
+            call = (calls >> (2 * owner)) & 3
             number = (numbers >> (3 * owner)) & 7
-            list_ref[call, jnp.where(call == 0, zero, one)] = LANES * BLOCKS * number + (2 * LANES + e)
-            zero, one = zero + 1 - call, one + call
-    for call, number in enumerate((zero, one)):
-        count_ref[call] = number
+            list_ref[call, (lengths >> (8 * call)) & 127] = LANES * BLOCKS * number + (2 * LANES + e)
+            lengths += 1 << (8 * call)
+    for call in range(len(plan)):
+        length = (lengths >> (8 * call)) & 127
+        count_ref[call] = length
         for u in range(UNROLL):
-            list_ref[call, number + u] = elems
+            list_ref[call, length + u] = elems
 
 
 def near_kernel(cells_ref, other_ref, after_ref, near_ref, weight_ref):
@@ -191,7 +192,7 @@
                 weight_ref[2 * (p + q) + h] = pair[:, h * B:(h + 1) * B].astype(jnp.bfloat16)
 
 
-def first_kernel(elems, code_ref, list_ref, count_ref, rows_ref, own_ref, weight_ref, one_ref, two_ref, *rest):
+def first_kernel(elems, code_ref, list_ref, count_ref, rows_ref, own_ref, weight_ref, two_ref, one_ref, *rest):
     outs, near_ref, total = rest[:-2], rest[-2], rest[-1]
     rim = elems // 4
     device = lax.axis_index("elem") * lax.axis_size("sub") + lax.axis_index("sub")
@@ -205,7 +206,7 @@
         out[...] = total[1 + k * PAIRS // 2:1 + (k + 1) * PAIRS // 2].astype(out.dtype)
 
 
-def next_kernel(elems, call, cuts, code_ref, list_ref, count_ref, rows_ref, near_ref, weight_ref, *rest):
+def next_kernel(elems, call, cuts, code_ref, list_ref, count_ref, rows_ref, near_ref, weight_ref, after_ref, *rest):
     outs, total = rest[:-1], rest[-1]
     accumulate(call, elems, code_ref, list_ref, count_ref, rows_ref, near_ref, weight_ref, total)
     for (t, at), out in zip(cuts, outs):
@@ -310,7 +311,7 @@
         compiler_params=params(),
         cost_estimate=cost,
         name="first",
-    )(codes, lists, counts, rows, own_near, weights, one, two)
+    )(codes, lists, counts, rows, own_near, weights, two, one)
 
     def across(block):
         return lax.ppermute(block, "sub", [(0, 1), (1, 0)])
@@ -334,34 +335,49 @@
 
     whole, halves = slice(0, PAIRS), [slice(0, PAIRS // 2), slice(PAIRS // 2, PAIRS)]
     pieces = {p: halves if p < 3 else [whole] for p in range(1, count)}
-    cuts = [(t, at) for t, (p, mine) in enumerate(plan[1]) for at in ([whole] if mine else pieces[p])]
-    came = {0: [across(block) for block in sent]}
-    outs = pl.pallas_call(
-        functools.partial(next_kernel, elems, 1, cuts),
-        in_specs=[SMEM] * 3 + [VMEM] * 3,
-        out_specs=[VMEM] * len(cuts),
-        out_shape=[
-            jax.ShapeDtypeStruct((at.stop - at.start, half, 2 * B), jnp.float32 if plan[1][t][1] else jnp.bfloat16)
-            for t, at in cuts
-        ],
-        scratch_shapes=[pltpu.VMEM((1 + len(plan[1]) * PAIRS, half, 2 * B), jnp.float32)],
-        compiler_params=params(),
-        cost_estimate=long,
-        name="next",
-    )(codes, lists, counts, rows, near, weights)
-    kept = outs[-count:]
-    sent = outs[:-count]
-    ready0 = [summed(0, at, block) for at, block in zip(halves, came[0])]
+    def tables(call, after):
+        cuts = [(t, at) for t, (p, mine) in enumerate(plan[call]) for at in ([whole] if mine else pieces[p])]
+        outs = pl.pallas_call(
+            functools.partial(next_kernel, elems, call, cuts),
+            in_specs=[SMEM] * 3 + [VMEM] * 3 + [pl.BlockSpec(memory_space=pl.ANY)],
+            out_specs=[VMEM] * len(cuts),
+            out_shape=[
+                jax.ShapeDtypeStruct(
+                    (at.stop - at.start, half, 2 * B), jnp.float32 if plan[call][t][1] else jnp.bfloat16)
+                for t, at in cuts
+            ],
+            scratch_shapes=[pltpu.VMEM((1 + len(plan[call]) * PAIRS, half, 2 * B), jnp.float32)],
+            compiler_params=params(),
+            cost_estimate=cost,
+            name="tables_%d" % call,
+        )(codes, lists, counts, rows, near, weights, after)
+        for (t, at), out in zip(cuts, outs):
+            p, mine = plan[call][t]
+            if mine:
+                kept[p] = out
+            else:
+                ready.setdefault(p, []).append(out)
+
+    came = {0: [across(sent[0])]}
+    kept, ready = {}, {}
+    tables(1, near)
+    came[0].append(across(sent[1]))
+    ready0 = [summed(0, halves[0], came[0][0])]
+    tables(2, ready0[0])
+    came[0][1] = behind(came[0][1], ready0[0])
+    ready0.append(summed(0, halves[1], came[0][1]))
     joined = [along(block, [(y, y ^ 1) for y in range(count)]) for block in ready0]
-    came[1] = [across(sent[0]), across(behind(sent[1], came[0][1]))]
+    tables(3, ready0[1])
+    came[1] = [across(behind(ready[1][0], ready0[0])), across(behind(ready[1][1], came[0][1]))]
     ready1 = [summed(1, at, block, True, more) for at, block, more in zip(halves, came[1], joined)]
     round1 = [along(block, ROUNDS[0]) for block in ready1]
-    came[2] = [across(behind(sent[2], joined[0])), across(behind(sent[3], came[1][1]))]
+    came[2] = [across(behind(ready[2][0], joined[0]))]
+    came[2].append(across(behind(ready[2][1], came[2][0])))
     came[2][0] = behind(came[2][0], round1[0])
-    came[2][1] = behind(came[2][1], *round1)
+    came[2][1] = behind(came[2][1], round1[0], round1[1])
     ready2 = [summed(2, at, block, False, more) for at, block, more in zip(halves, came[2], joined)]
     round2 = [along(block, ROUNDS[1]) for block in ready2]
-    came[3] = [across(behind(sent[4], came[2][0]))]
+    came[3] = [across(behind(ready[3][0], came[2][0]))]
 
     total = pl.pallas_call(
         gather_kernel,

time: 59.1 us -> 62.1 us (1.051); the launches traced: 58.4 us -> 62.7 us
  waiting for transfers between devices: 15.2 us -> 20.4 us
  starting transfers between devices: 25.8 us -> 23.2 us
  Pallas kernels: 15.6 us -> 17.1 us
    ppermute x6, waiting for transfers between devices: 8.73 us -> 15.5 us  [along(): return lax.ppermute(block, 'elem', pairs)]
    ppermute x2, starting transfers between devices: 6.01 us -> 3.21 us  [swap(): return lax.ppermute(block, axes, pairs + [(j, i) for i, j in pairs])]
    pallas_call x1 -> x3, Pallas kernels: 7.75 us -> 9.77 us  [tables(): pl.pallas_call(functools.partial(next_kernel, elems, call, cuts), in_spec...]
    ppermute x7, starting transfers between devices: 7.97 us -> 9.95 us  [across(): return lax.ppermute(block, 'sub', [(0, 1), (1, 0)])]
    ppermute x6, starting transfers between devices: 11.3 us -> 9.61 us  [along(): return lax.ppermute(block, 'elem', pairs)]
    ppermute x7, waiting for transfers between devices: 6.47 us -> 4.94 us  [across(): return lax.ppermute(block, 'sub', [(0, 1), (1, 0)])]
  transfers between devices with their start and end apart: 16 -> 16, of which waited for: 8 -> 4; matrix products, arithmetic and copies ran while one was open for 3% -> 3% of each run, Pallas kernels for 21% -> 23%
where the time goes in v4:
time: 62.1 us; the launch traced here: 62.7 us
  starting transfers between devices  23.2 us (37%)
  waiting for transfers between devices  20.4 us (33%)
  Pallas kernels  17.1 us (28%)
  other arithmetic  1.67 us (3%)
    ppermute x6, waiting for transfers between devices, along(): return lax.ppermute(block, 'elem', pairs)  15.5 us
    ppermute x7, starting transfers between devices, across(): return lax.ppermute(block, 'sub', [(0, 1), (1, 0)])  9.95 us
    pallas_call x3, Pallas kernels, tables(): pl.pallas_call(functools.partial(next_kernel, elems, call, cuts), in_spec...  9.77 us
    ppermute x6, starting transfers between devices, along(): return lax.ppermute(block, 'elem', pairs)  9.61 us
    ppermute x7, waiting for transfers between devices, across(): return lax.ppermute(block, 'sub', [(0, 1), (1, 0)])  4.94 us
    ppermute x2, starting transfers between devices, swap(): return lax.ppermute(block, axes, pairs + [(j, i) for i, j in pairs])  3.21 us
    pallas_call x1, Pallas kernels, dense(): pl.pallas_call(functools.partial(lists_kernel, elems, count), in_specs=[S...  1.95 us
    pallas_call x1, Pallas kernels, dense(): pl.pallas_call(functools.partial(first_kernel, elems), in_specs=[SMEM] *...  1.55 us
  transfers between devices with their start and end apart: 16, of which 4 were waited for; matrix products, arithmetic and copies ran while one was open for 3% of the time, Pallas kernels for 23%

profile of v4, /device:TPU:0, one launch (start us, length us, event | category | flops | bytes accessed | tf_op | source)
XLA Modules:
  0.0 62.7 jit_solution(17736780009987524)
XLA Ops:
  0.5 1.0 %broadcast_select_fusion = (bf16[32,1536]{1,0:T(8,128)(2,1)S(1)}, bf16[32,1536]{1,0:T(8,128)(2,1)S(1)}) fusion(pred[]{:T(512)S(6)} %eq.5, bf16[32,6144]{1,0:T(8,128)(2,1)} %cells_ref.1), kind=kLoop, calls=%fused_computation | loop fusion | flops 98304 | bytes 393217 | tf_op jit(solution)/shard_map/jit(_where)/select_n | solution.py:49
  1.4 2.6 %collective-permute-start.2 = (bf16[32,1536]{1,0:T(8,128)(2,1)S(1)}, bf16[32,1536]{1,0:T(8,128)(2,1)S(1)}, u32[]{:S(2)}, u32[]{:S(2)}) collective-permute-start(bf16[32,1536]{1,0:T(8,128)(2,1)S(1)} %get-tuple-element.55), channel_id=1, source_target_pairs={{0,2},{4,6},{8,10},{12,14},{2,0},{6,4},{10,8},{14,12},{1,3},{5,7},... | collective-permute-start | bytes 294920 | tf_op jit(solution)/shard_map/ppermute | solution.py:47
  4.6 0.7 %pad_add_fusion.ints_ref.again_ref = s32[11,96]{1,0:T(8,128)S(1)} fusion(s32[4,96]{1,0:T(4,128)} %bitcast.6, s32[5,96]{1,0:T(8,128)} %bitcast.5, s32[1,96]{1,0:T(1,128)} %bitcast.7, s32[1,96]{1,0:T(1,128)} %bitcast.8), kind=kLoop, calls=%fused_computation.2 | loop fusion | flops 3168 | bytes 8448 | tf_op jit(solution)/shard_map/concatenate | solution.py:264
  5.4 2.0 %lists.1 = (s32[16,128]{1,0:T(8,128)S(1)}, s32[4,104]{1,0:T(4,128)S(1)}, s32[4]{0:T(128)S(1)}) custom-call(s32[11,96]{1,0:T(8,128)S(1)} %pad_add_fusion.ints_ref.again_ref, s32[11,96]{1,0:T(8,128)S(1)} %pad_add_fusion.ints_ref.again_ref), custom_call_target="tpu_custom_call" | custom-call | flops 20000000000 | bytes 1000 | tf_op jit(solution)/shard_map/lists/pallas_call | solution.py:267
  7.4 0.7 %near.1 = (bf16[96,32,128]{2,1,0:T(8,128)(2,1)S(1)}, bf16[96,64,64]{2,1,0:T(8,128)(2,1)S(1)}) custom-call(bf16[32,6144]{1,0:T(8,128)(2,1)S(1)} %copy-done.1, bf16[32,6144]{1,0:T(8,128)(2,1)S(1)} %collective-permute-done.other_ref, s32[16,128]{1,0:T(8,128)S(1)} %get-tuple-element.30.after_ref.code_ref), custom_call_target="tpu_custom_call" | custom-call | flops 1000 | bytes 1000 | tf_op jit(solution)/shard_map/near/pallas_call | solution.py:280
  8.1 1.3 %rows.1.rows_ref = bf16[96,160,128]{2,1,0:T(8,128)(2,1)S(1)} custom-call(bf16[96,20480]{1,0:T(8,128)(2,1)S(1)} %copy-done, bf16[96,32,128]{2,1,0:T(8,128)(2,1)S(1)} %get-tuple-element.33.after_ref.own_ref), custom_call_target="tpu_custom_call" | custom-call | flops 1000 | bytes 1000 | tf_op jit(solution)/shard_map/rows/pallas_call | solution.py:292
  9.4 1.5 %first.1 = (bf16[27,32,128]{2,1,0:T(8,128)(2,1)S(1)}, bf16[27,32,128]{2,1,0:T(8,128)(2,1)S(1)}, bf16[145,32,128]{2,1,0:T(8,128)(2,1)S(1)}) custom-call(s32[16,128]{1,0:T(8,128)S(1)} %get-tuple-element.30.after_ref.code_ref, s32[4,104]{1,0:T(4,128)S(1)} %get-tuple-element.31.list_ref, s32[4]{0:T(128)S(1)} %get-tuple-element.32.count_ref, ...), custom_call_target="tpu_custom_call" | custom-call | flops 1000 | bytes 1000 | tf_op jit(solution)/shard_map/first/pallas_call | solution.py:303
  10.9 4.3 %collective-permute-start.4 = (bf16[27,32,128]{2,1,0:T(8,128)(2,1)S(1)}, bf16[27,32,128]{2,1,0:T(8,128)(2,1)S(1)}, u32[]{:S(2)}, u32[]{:S(2)}) collective-permute-start(bf16[27,32,128]{2,1,0:T(8,128)(2,1)S(1)} %get-tuple-element.38), channel_id=1, source_target_pairs={{0,2},{2,0},{1,3},{3,1},{4,6},{6,4},{5,7},{7,5},{8,10},{10,8},{9,1... | collective-permute-start | bytes 663560 | tf_op jit(solution)/shard_map/ppermute | solution.py:317
  15.4 2.1 %tables_1.1 = (bf16[27,32,128]{2,1,0:T(8,128)(2,1)S(1)}, bf16[27,32,128]{2,1,0:T(8,128)(2,1)S(1)}, f32[54,32,128]{2,1,0:T(8,128)S(1)}) custom-call(s32[16,128]{1,0:T(8,128)S(1)} %get-tuple-element.30.after_ref.code_ref, s32[4,104]{1,0:T(4,128)S(1)} %get-tuple-element.31.list_ref, s32[4]{0:T(128)S(1)} %get-tuple-element.32.count_ref, ...), custom_call_target="tpu_custom_call" | custom-call | flops 1000 | bytes 1000 | tf_op jit(solution)/shard_map/tables_1/pallas_call | solution.py:340
  17.5 4.1 %collective-permute-done.4.came_ref = bf16[27,32,128]{2,1,0:T(8,128)(2,1)S(1)} collective-permute-done((bf16[27,32,128]{2,1,0:T(8,128)(2,1)S(1)}, bf16[27,32,128]{2,1,0:T(8,128)(2,1)S(1)}, u32[]{:S(2)}, u32[]{:S(2)}) %collective-permute-start.4) | collective-permute-done | bytes 221216 | tf_op jit(solution)/shard_map/ppermute | solution.py:317
  21.6 2.2 %collective-permute-start.6 = (bf16[27,32,128]{2,1,0:T(8,128)(2,1)S(1)}, bf16[27,32,128]{2,1,0:T(8,128)(2,1)S(1)}, u32[]{:S(2)}, u32[]{:S(2)}) collective-permute-start(bf16[27,32,128]{2,1,0:T(8,128)(2,1)S(1)} %add_0.2.after_ref), channel_id=1, source_target_pairs={{0,4},{4,0},{8,12},{12,8},{1,5},{5,1},{9,13},{13,9},{2,6},{6,2},{1... | collective-permute-start | bytes 663560 | tf_op jit(solution)/shard_map/ppermute | solution.py:320
  23.8 2.1 %collective-permute-start.5 = (bf16[27,32,128]{2,1,0:T(8,128)(2,1)S(1)}, bf16[27,32,128]{2,1,0:T(8,128)(2,1)S(1)}, u32[]{:S(2)}, u32[]{:S(2)}) collective-permute-start(bf16[27,32,128]{2,1,0:T(8,128)(2,1)S(1)} %get-tuple-element.43), channel_id=1, source_target_pairs={{0,2},{2,0},{1,3},{3,1},{4,6},{6,4},{5,7},{7,5},{8,10},{10,8},{9,1... | collective-permute-start | bytes 663560 | tf_op jit(solution)/shard_map/ppermute | solution.py:317
  25.9 2.1 %tables_2.1 = (bf16[27,32,128]{2,1,0:T(8,128)(2,1)S(1)}, bf16[27,32,128]{2,1,0:T(8,128)(2,1)S(1)}, f32[54,32,128]{2,1,0:T(8,128)S(1)}) custom-call(s32[16,128]{1,0:T(8,128)S(1)} %get-tuple-element.30.after_ref.code_ref, s32[4,104]{1,0:T(4,128)S(1)} %get-tuple-element.31.list_ref, s32[4]{0:T(128)S(1)} %get-tuple-element.32.count_ref, ...), custom_call_target="tpu_custom_call" | custom-call | flops 1000 | bytes 1000 | tf_op jit(solution)/shard_map/tables_2/pallas_call | solution.py:340
  28.0 0.7 %collective-permute-start.8 = (bf16[27,32,128]{2,1,0:T(8,128)(2,1)S(1)}, bf16[27,32,128]{2,1,0:T(8,128)(2,1)S(1)}, u32[]{:S(2)}, u32[]{:S(2)}) collective-permute-start(bf16[27,32,128]{2,1,0:T(8,128)(2,1)S(1)} %get-tuple-element.45), channel_id=1, source_target_pairs={{0,2},{2,0},{1,3},{3,1},{4,6},{6,4},{5,7},{7,5},{8,10},{10,8},{9,1... | collective-permute-start | bytes 663560 | tf_op jit(solution)/shard_map/ppermute | solution.py:317
  28.7 1.9 %collective-permute-start.9 = (bf16[27,32,128]{2,1,0:T(8,128)(2,1)S(1)}, bf16[27,32,128]{2,1,0:T(8,128)(2,1)S(1)}, u32[]{:S(2)}, u32[]{:S(2)}) collective-permute-start(bf16[27,32,128]{2,1,0:T(8,128)(2,1)S(1)} %add_0.3.after_ref), channel_id=1, source_target_pairs={{0,4},{4,0},{8,12},{12,8},{1,5},{5,1},{9,13},{13,9},{2,6},{6,2},{1... | collective-permute-start | bytes 663560 | tf_op jit(solution)/shard_map/ppermute | solution.py:320
  30.6 0.7 %collective-permute-start.11 = (bf16[27,32,128]{2,1,0:T(8,128)(2,1)S(1)}, bf16[27,32,128]{2,1,0:T(8,128)(2,1)S(1)}, u32[]{:S(2)}, u32[]{:S(2)}) collective-permute-start(bf16[27,32,128]{2,1,0:T(8,128)(2,1)S(1)} %get-tuple-element.48), channel_id=1, source_target_pairs={{0,2},{2,0},{1,3},{3,1},{4,6},{6,4},{5,7},{7,5},{8,10},{10,8},{9,1... | collective-permute-start | bytes 663560 | tf_op jit(solution)/shard_map/ppermute | solution.py:317
  31.3 0.9 %collective-permute-done.5.came_ref = bf16[27,32,128]{2,1,0:T(8,128)(2,1)S(1)} collective-permute-done((bf16[27,32,128]{2,1,0:T(8,128)(2,1)S(1)}, bf16[27,32,128]{2,1,0:T(8,128)(2,1)S(1)}, u32[]{:S(2)}, u32[]{:S(2)}) %collective-permute-start.5) | collective-permute-done | bytes 221216 | tf_op jit(solution)/shard_map/ppermute | solution.py:317
  32.3 3.3 %collective-permute-start.7 = (bf16[27,32,128]{2,1,0:T(8,128)(2,1)S(1)}, bf16[27,32,128]{2,1,0:T(8,128)(2,1)S(1)}, u32[]{:S(2)}, u32[]{:S(2)}) collective-permute-start(bf16[27,32,128]{2,1,0:T(8,128)(2,1)S(1)} %add_1.2), channel_id=1, source_target_pairs={{0,8},{4,0},{8,12},{12,4},{1,9},{5,1},{9,13},{13,5},{2,10},{6,2},{... | collective-permute-start | bytes 663560 | tf_op jit(solution)/shard_map/ppermute | solution.py:320
  35.6 5.6 %tables_3.1 = (bf16[54,32,128]{2,1,0:T(8,128)(2,1)S(1)}, f32[54,32,128]{2,1,0:T(8,128)S(1)}, f32[54,32,128]{2,1,0:T(8,128)S(1)}) custom-call(s32[16,128]{1,0:T(8,128)S(1)} %get-tuple-element.30.after_ref.code_ref, s32[4,104]{1,0:T(4,128)S(1)} %get-tuple-element.31.list_ref, s32[4]{0:T(128)S(1)} %get-tuple-element.32.count_ref, ...), custom_call_target="tpu_custom_call" | custom-call | flops 1000 | bytes 1000 | tf_op jit(solution)/shard_map/tables_3/pallas_call | solution.py:340
  42.1 1.8 %collective-permute-start.15 = (bf16[54,32,128]{2,1,0:T(8,128)(2,1)S(1)}, bf16[54,32,128]{2,1,0:T(8,128)(2,1)S(1)}, u32[]{:S(2)}, u32[]{:S(2)}) collective-permute-start(bf16[54,32,128]{2,1,0:T(8,128)(2,1)S(1)} %get-tuple-element.54), channel_id=1, source_target_pairs={{0,2},{2,0},{1,3},{3,1},{4,6},{6,4},{5,7},{7,5},{8,10},{10,8},{9,1... | collective-permute-start | bytes 1327112 | tf_op jit(solution)/shard_map/ppermute | solution.py:317
  44.0 1.6 %collective-permute-start.12 = (bf16[27,32,128]{2,1,0:T(8,128)(2,1)S(1)}, bf16[27,32,128]{2,1,0:T(8,128)(2,1)S(1)}, u32[]{:S(2)}, u32[]{:S(2)}) collective-permute-start(bf16[27,32,128]{2,1,0:T(8,128)(2,1)S(1)} %add_2.2), channel_id=1, source_target_pairs={{0,4},{4,12},{8,0},{12,8},{1,5},{5,13},{9,1},{13,9},{2,6},{6,14},{... | collective-permute-start | bytes 663560 | tf_op jit(solution)/shard_map/ppermute | solution.py:320
  45.6 8.8 %collective-permute-done.10.rest_1_ = bf16[27,32,128]{2,1,0:T(8,128)(2,1)S(1)} collective-permute-done((bf16[27,32,128]{2,1,0:T(8,128)(2,1)S(1)}, bf16[27,32,128]{2,1,0:T(8,128)(2,1)S(1)}, u32[]{:S(2)}, u32[]{:S(2)}) %collective-permute-start.10) | collective-permute-done | bytes 221216 | tf_op jit(solution)/shard_map/ppermute | solution.py:320
  54.7 6.7 %collective-permute-done.14.rest_2_ = bf16[27,32,128]{2,1,0:T(8,128)(2,1)S(1)} collective-permute-done((bf16[27,32,128]{2,1,0:T(8,128)(2,1)S(1)}, bf16[27,32,128]{2,1,0:T(8,128)(2,1)S(1)}, u32[]{:S(2)}, u32[]{:S(2)}) %collective-permute-start.14) | collective-permute-done | bytes 221216 | tf_op jit(solution)/shard_map/ppermute | solution.py:320
  61.4 1.3 %last.1 = f32[12,32,576]{2,1,0:T(8,128)} custom-call(f32[54,32,128]{2,1,0:T(8,128)S(1)} %gather.1.rest_0_, bf16[27,32,128]{2,1,0:T(8,128)(2,1)S(1)} %collective-permute-done.12.rest_1_, bf16[27,32,128]{2,1,0:T(8,128)(2,1)S(1)} %collective-permute-done.14.rest_2_, bf16[54,32,128]{2,1,0:T(8,128)(2,1)S(1)} %collective-permute-done.15.rest_3_), custom_call_target="tpu_custom_call" | custom-call | flops 1000 | bytes 1000 | tf_op jit(solution)/shard_map/last/pallas_call | solution.py:392
  (29 shorter events, 2.6 us)
Async XLA Ops:
  0.0 7.3 %collective-permute-start = (bf16[32,6144]{1,0:T(8,128)(2,1)}, bf16[32,6144]{1,0:T(8,128)(2,1)S(1)}, u32[]{:S(2)}, u32[]{:S(2)}) collective-permute-start(bf16[32,6144]{1,0:T(8,128)(2,1)} %cells_ref.1), channel_id=1, source_target_pairs={{0,1},{1,0},{2,3},{3,2},{4,5},{5,4},{6,7},{7,6},{8,9},{9,8},{10,11... | collective-permute-start | bytes 1179656 | tf_op jit(solution)/shard_map/ppermute | solution.py:262
  1.4 7.9 %collective-permute-start.2 = (bf16[32,1536]{1,0:T(8,128)(2,1)S(1)}, bf16[32,1536]{1,0:T(8,128)(2,1)S(1)}, u32[]{:S(2)}, u32[]{:S(2)}) collective-permute-start(bf16[32,1536]{1,0:T(8,128)(2,1)S(1)} %get-tuple-element.55), channel_id=1, source_target_pairs={{0,2},{4,6},{8,10},{12,14},{2,0},{6,4},{10,8},{14,12},{1,3},{5,7},... | collective-permute-start | bytes 294920 | tf_op jit(solution)/shard_map/ppermute | solution.py:47
  4.0 5.4 %collective-permute-start.1 = (bf16[32,1536]{1,0:T(8,128)(2,1)S(1)}, bf16[32,1536]{1,0:T(8,128)(2,1)S(1)}, u32[]{:S(2)}, u32[]{:S(2)}) collective-permute-start(bf16[32,1536]{1,0:T(8,128)(2,1)S(1)} %get-tuple-element.56), channel_id=1, source_target_pairs={{2,4},{6,8},{10,12},{4,2},{8,6},{12,10},{3,5},{7,9},{11,13},{5,3},... | collective-permute-start | bytes 294920 | tf_op jit(solution)/shard_map/ppermute | solution.py:47
  5.4 2.0 %copy-start.1 = (bf16[32,6144]{1,0:T(8,128)(2,1)S(1)}, bf16[32,6144]{1,0:T(8,128)(2,1)}, u32[]{:S(2)}) copy-start(bf16[32,6144]{1,0:T(8,128)(2,1)} %cells_ref.1) | copy-start | bytes 1179652
  5.4 2.7 %copy-start = (bf16[96,20480]{1,0:T(8,128)(2,1)S(1)}, bf16[96,20480]{1,0:T(8,128)(2,1)}, u32[]{:S(2)}) copy-start(bf16[96,20480]{1,0:T(8,128)(2,1)} %jac_ref.1) | copy-start | bytes 11796484
  10.9 10.6 %collective-permute-start.4 = (bf16[27,32,128]{2,1,0:T(8,128)(2,1)S(1)}, bf16[27,32,128]{2,1,0:T(8,128)(2,1)S(1)}, u32[]{:S(2)}, u32[]{:S(2)}) collective-permute-start(bf16[27,32,128]{2,1,0:T(8,128)(2,1)S(1)} %get-tuple-element.38), channel_id=1, source_target_pairs={{0,2},{2,0},{1,3},{3,1},{4,6},{6,4},{5,7},{7,5},{8,10},{10,8},{9,1... | collective-permute-start | bytes 663560 | tf_op jit(solution)/shard_map/ppermute | solution.py:317
  15.3 12.7 %collective-permute-start.3 = (bf16[27,32,128]{2,1,0:T(8,128)(2,1)S(1)}, bf16[27,32,128]{2,1,0:T(8,128)(2,1)S(1)}, u32[]{:S(2)}, u32[]{:S(2)}) collective-permute-start(bf16[27,32,128]{2,1,0:T(8,128)(2,1)S(1)} %get-tuple-element.37), channel_id=1, source_target_pairs={{0,2},{2,0},{1,3},{3,1},{4,6},{6,4},{5,7},{7,5},{8,10},{10,8},{9,1... | collective-permute-start | bytes 663560 | tf_op jit(solution)/shard_map/ppermute | solution.py:317
  21.6 9.1 %collective-permute-start.6 = (bf16[27,32,128]{2,1,0:T(8,128)(2,1)S(1)}, bf16[27,32,128]{2,1,0:T(8,128)(2,1)S(1)}, u32[]{:S(2)}, u32[]{:S(2)}) collective-permute-start(bf16[27,32,128]{2,1,0:T(8,128)(2,1)S(1)} %add_0.2.after_ref), channel_id=1, source_target_pairs={{0,4},{4,0},{8,12},{12,8},{1,5},{5,1},{9,13},{13,9},{2,6},{6,2},{1... | collective-permute-start | bytes 663560 | tf_op jit(solution)/shard_map/ppermute | solution.py:320
  23.8 8.4 %collective-permute-start.5 = (bf16[27,32,128]{2,1,0:T(8,128)(2,1)S(1)}, bf16[27,32,128]{2,1,0:T(8,128)(2,1)S(1)}, u32[]{:S(2)}, u32[]{:S(2)}) collective-permute-start(bf16[27,32,128]{2,1,0:T(8,128)(2,1)S(1)} %get-tuple-element.43), channel_id=1, source_target_pairs={{0,2},{2,0},{1,3},{3,1},{4,6},{6,4},{5,7},{7,5},{8,10},{10,8},{9,1... | collective-permute-start | bytes 663560 | tf_op jit(solution)/shard_map/ppermute | solution.py:317
  28.0 13.2 %collective-permute-start.8 = (bf16[27,32,128]{2,1,0:T(8,128)(2,1)S(1)}, bf16[27,32,128]{2,1,0:T(8,128)(2,1)S(1)}, u32[]{:S(2)}, u32[]{:S(2)}) collective-permute-start(bf16[27,32,128]{2,1,0:T(8,128)(2,1)S(1)} %get-tuple-element.45), channel_id=1, source_target_pairs={{0,2},{2,0},{1,3},{3,1},{4,6},{6,4},{5,7},{7,5},{8,10},{10,8},{9,1... | collective-permute-start | bytes 663560 | tf_op jit(solution)/shard_map/ppermute | solution.py:317
  28.7 12.5 %collective-permute-start.9 = (bf16[27,32,128]{2,1,0:T(8,128)(2,1)S(1)}, bf16[27,32,128]{2,1,0:T(8,128)(2,1)S(1)}, u32[]{:S(2)}, u32[]{:S(2)}) collective-permute-start(bf16[27,32,128]{2,1,0:T(8,128)(2,1)S(1)} %add_0.3.after_ref), channel_id=1, source_target_pairs={{0,4},{4,0},{8,12},{12,8},{1,5},{5,1},{9,13},{13,9},{2,6},{6,2},{1... | collective-permute-start | bytes 663560 | tf_op jit(solution)/shard_map/ppermute | solution.py:320
  30.6 11.2 %collective-permute-start.11 = (bf16[27,32,128]{2,1,0:T(8,128)(2,1)S(1)}, bf16[27,32,128]{2,1,0:T(8,128)(2,1)S(1)}, u32[]{:S(2)}, u32[]{:S(2)}) collective-permute-start(bf16[27,32,128]{2,1,0:T(8,128)(2,1)S(1)} %get-tuple-element.48), channel_id=1, source_target_pairs={{0,2},{2,0},{1,3},{3,1},{4,6},{6,4},{5,7},{7,5},{8,10},{10,8},{9,1... | collective-permute-start | bytes 663560 | tf_op jit(solution)/shard_map/ppermute | solution.py:317
  32.3 9.8 %collective-permute-start.7 = (bf16[27,32,128]{2,1,0:T(8,128)(2,1)S(1)}, bf16[27,32,128]{2,1,0:T(8,128)(2,1)S(1)}, u32[]{:S(2)}, u32[]{:S(2)}) collective-permute-start(bf16[27,32,128]{2,1,0:T(8,128)(2,1)S(1)} %add_1.2), channel_id=1, source_target_pairs={{0,8},{4,0},{8,12},{12,4},{1,9},{5,1},{9,13},{13,5},{2,10},{6,2},{... | collective-permute-start | bytes 663560 | tf_op jit(solution)/shard_map/ppermute | solution.py:320
  41.3 13.1 %collective-permute-start.10 = (bf16[27,32,128]{2,1,0:T(8,128)(2,1)S(1)}, bf16[27,32,128]{2,1,0:T(8,128)(2,1)S(1)}, u32[]{:S(2)}, u32[]{:S(2)}) collective-permute-start(bf16[27,32,128]{2,1,0:T(8,128)(2,1)S(1)} %add_1.3), channel_id=1, source_target_pairs={{0,8},{4,0},{8,12},{12,4},{1,9},{5,1},{9,13},{13,5},{2,10},{6,2},{... | collective-permute-start | bytes 663560 | tf_op jit(solution)/shard_map/ppermute | solution.py:320
  41.9 12.5 %collective-permute-start.13 = (bf16[27,32,128]{2,1,0:T(8,128)(2,1)S(1)}, bf16[27,32,128]{2,1,0:T(8,128)(2,1)S(1)}, u32[]{:S(2)}, u32[]{:S(2)}) collective-permute-start(bf16[27,32,128]{2,1,0:T(8,128)(2,1)S(1)} %get-tuple-element.51), channel_id=1, source_target_pairs={{0,2},{2,0},{1,3},{3,1},{4,6},{6,4},{5,7},{7,5},{8,10},{10,8},{9,1... | collective-permute-start | bytes 663560 | tf_op jit(solution)/shard_map/ppermute | solution.py:317
  42.1 19.3 %collective-permute-start.15 = (bf16[54,32,128]{2,1,0:T(8,128)(2,1)S(1)}, bf16[54,32,128]{2,1,0:T(8,128)(2,1)S(1)}, u32[]{:S(2)}, u32[]{:S(2)}) collective-permute-start(bf16[54,32,128]{2,1,0:T(8,128)(2,1)S(1)} %get-tuple-element.54), channel_id=1, source_target_pairs={{0,2},{2,0},{1,3},{3,1},{4,6},{6,4},{5,7},{7,5},{8,10},{10,8},{9,1... | collective-permute-start | bytes 1327112 | tf_op jit(solution)/shard_map/ppermute | solution.py:317
  44.0 10.7 %collective-permute-start.12 = (bf16[27,32,128]{2,1,0:T(8,128)(2,1)S(1)}, bf16[27,32,128]{2,1,0:T(8,128)(2,1)S(1)}, u32[]{:S(2)}, u32[]{:S(2)}) collective-permute-start(bf16[27,32,128]{2,1,0:T(8,128)(2,1)S(1)} %add_2.2), channel_id=1, source_target_pairs={{0,4},{4,12},{8,0},{12,8},{1,5},{5,13},{9,1},{13,9},{2,6},{6,14},{... | collective-permute-start | bytes 663560 | tf_op jit(solution)/shard_map/ppermute | solution.py:320
  54.5 6.9 %collective-permute-start.14 = (bf16[27,32,128]{2,1,0:T(8,128)(2,1)S(1)}, bf16[27,32,128]{2,1,0:T(8,128)(2,1)S(1)}, u32[]{:S(2)}, u32[]{:S(2)}) collective-permute-start(bf16[27,32,128]{2,1,0:T(8,128)(2,1)S(1)} %add_2.3), channel_id=1, source_target_pairs={{0,4},{4,12},{8,0},{12,8},{1,5},{5,13},{9,1},{13,9},{2,6},{6,14},{... | collective-permute-start | bytes 663560 | tf_op jit(solution)/shard_map/ppermute | solution.py:320

commit v5 on v4

--- a/solution.py
+++ b/solution.py
@@ -233,21 +233,28 @@
 
 
 def last_kernel(*rest):
-    out_ref, total = rest[-2], rest[-1]
-    gather_kernel(*rest[:-2], total)
+    out_ref, total, block, done = rest[-4:]
+    gather_kernel(*rest[:-4], total)
     low = lax.broadcasted_iota(jnp.int32, (32, 128), 1) < B
+    copies = []
     for a in range(AGG_DEV):
         first = a * CS // 2
         for q in range(CS // 2):
             if a % 2 == 0:
-                out_ref[a, :, q * 128:(q + 1) * 128] = total[first + q]
+                block[a, :, q * 128:(q + 1) * 128] = total[first + q]
             else:
-                out_ref[a, :, q * 128:(q + 1) * 128] = jnp.where(
+                block[a, :, q * 128:(q + 1) * 128] = jnp.where(
                     low, pltpu.roll(total[first + q], B, 1), pltpu.roll(total[first + q + 1], B, 1))
         last = total[first + CS // 2]
         if a % 2 == 1:
             last = pltpu.roll(last, B, 1)
-        out_ref[a, :, (CS // 2) * 128:] = last[:, :B]
+        block[a, :, (CS // 2) * 128:] = last[:, :B]
+        if a % 2 == 1:
+            pair = pl.ds(a - 1, 2)
+            copies.append(pltpu.make_async_copy(block.at[pair], out_ref.at[pair], done.at[a // 2]))
+            copies[-1].start()
+    for copy in copies:
+        copy.wait()
 
 
 def dense(jacobian, prolong, face_pattern, owner, member, coarse_slot):
@@ -368,7 +375,7 @@
     ready0.append(summed(0, halves[1], came[0][1]))
     joined = [along(block, [(y, y ^ 1) for y in range(count)]) for block in ready0]
     tables(3, ready0[1])
-    came[1] = [across(behind(ready[1][0], ready0[0])), across(behind(ready[1][1], came[0][1]))]
+    came[1] = [across(behind(ready[1][0], came[0][0])), across(behind(ready[1][1], came[0][1]))]
     ready1 = [summed(1, at, block, True, more) for at, block, more in zip(halves, came[1], joined)]
     round1 = [along(block, ROUNDS[0]) for block in ready1]
     came[2] = [across(behind(ready[2][0], joined[0]))]
@@ -392,9 +399,13 @@
     coarse = pl.pallas_call(
         last_kernel,
         in_specs=[VMEM] * (1 + len(parts)),
-        out_specs=VMEM,
+        out_specs=pl.BlockSpec(memory_space=pl.ANY),
         out_shape=jax.ShapeDtypeStruct((AGG_DEV, half, CS * CB), jnp.float32),
-        scratch_shapes=[pltpu.VMEM(table, jnp.float32)],
+        scratch_shapes=[
+            pltpu.VMEM(table, jnp.float32),
+            pltpu.VMEM((AGG_DEV, half, CS * CB), jnp.float32),
+            pltpu.SemaphoreType.DMA((AGG_DEV // 2,)),
+        ],
         compiler_params=params(),
         cost_estimate=cost,
         name="last",

time: 62.1 us -> 57.1 us (0.919); the launches traced: 62.7 us -> 57 us
  waiting for transfers between devices: 20.4 us -> 13.7 us
  starting transfers between devices: 23.2 us -> 24.5 us
    ppermute x6, waiting for transfers between devices: 15.5 us -> 5.85 us  [along(): return lax.ppermute(block, 'elem', pairs)]
    ppermute x7, waiting for transfers between devices: 4.94 us -> 7.87 us  [across(): return lax.ppermute(block, 'sub', [(0, 1), (1, 0)])]
    ppermute x6, starting transfers between devices: 9.61 us -> 11 us  [along(): return lax.ppermute(block, 'elem', pairs)]
  transfers between devices with their start and end apart: 16 -> 16, of which waited for: 4 -> 6; matrix products, arithmetic and copies ran while one was open for 3% -> 3% of each run, Pallas kernels for 23% -> 25%
where the time goes in v5:
time: 57.1 us; the launch traced here: 57 us
  starting transfers between devices  24.5 us (43%)
  Pallas kernels  16.9 us (30%)
  waiting for transfers between devices  13.7 us (24%)
  other arithmetic  1.67 us (3%)
    ppermute x6, starting transfers between devices, along(): return lax.ppermute(block, 'elem', pairs)  11 us
    ppermute x7, starting transfers between devices, across(): return lax.ppermute(block, 'sub', [(0, 1), (1, 0)])  9.83 us
    pallas_call x3, Pallas kernels, tables(): pl.pallas_call(functools.partial(next_kernel, elems, call, cuts), in_spec...  9.75 us
    ppermute x7, waiting for transfers between devices, across(): return lax.ppermute(block, 'sub', [(0, 1), (1, 0)])  7.87 us
    ppermute x6, waiting for transfers between devices, along(): return lax.ppermute(block, 'elem', pairs)  5.85 us
    ppermute x2, starting transfers between devices, swap(): return lax.ppermute(block, axes, pairs + [(j, i) for i, j in pairs])  3.21 us
    pallas_call x1, Pallas kernels, dense(): pl.pallas_call(functools.partial(lists_kernel, elems, count), in_specs=[S...  1.95 us
    pallas_call x1, Pallas kernels, dense(): pl.pallas_call(functools.partial(first_kernel, elems), in_specs=[SMEM] *...  1.57 us
  transfers between devices with their start and end apart: 16, of which 6 were waited for; matrix products, arithmetic and copies ran while one was open for 3% of the time, Pallas kernels for 25%

profile of v5, /device:TPU:0, one launch (start us, length us, event | category | flops | bytes accessed | tf_op | source)
XLA Modules:
  0.0 57.0 jit_solution(11676148422568323771)
XLA Ops:
  0.5 1.0 %broadcast_select_fusion = (bf16[32,1536]{1,0:T(8,128)(2,1)S(1)}, bf16[32,1536]{1,0:T(8,128)(2,1)S(1)}) fusion(pred[]{:T(512)S(6)} %eq.5, bf16[32,6144]{1,0:T(8,128)(2,1)} %cells_ref.1), kind=kLoop, calls=%fused_computation | loop fusion | flops 98304 | bytes 393217 | tf_op jit(solution)/shard_map/jit(_where)/select_n | solution.py:49
  1.4 2.6 %collective-permute-start.2 = (bf16[32,1536]{1,0:T(8,128)(2,1)S(1)}, bf16[32,1536]{1,0:T(8,128)(2,1)S(1)}, u32[]{:S(2)}, u32[]{:S(2)}) collective-permute-start(bf16[32,1536]{1,0:T(8,128)(2,1)S(1)} %get-tuple-element.55), channel_id=1, source_target_pairs={{0,2},{4,6},{8,10},{12,14},{2,0},{6,4},{10,8},{14,12},{1,3},{5,7},... | collective-permute-start | bytes 294920 | tf_op jit(solution)/shard_map/ppermute | solution.py:47
  4.6 0.7 %pad_add_fusion.ints_ref.again_ref = s32[11,96]{1,0:T(8,128)S(1)} fusion(s32[4,96]{1,0:T(4,128)} %bitcast.6, s32[5,96]{1,0:T(8,128)} %bitcast.5, s32[1,96]{1,0:T(1,128)} %bitcast.7, s32[1,96]{1,0:T(1,128)} %bitcast.8), kind=kLoop, calls=%fused_computation.2 | loop fusion | flops 3168 | bytes 8448 | tf_op jit(solution)/shard_map/concatenate | solution.py:271
  5.4 2.0 %lists.1 = (s32[16,128]{1,0:T(8,128)S(1)}, s32[4,104]{1,0:T(4,128)S(1)}, s32[4]{0:T(128)S(1)}) custom-call(s32[11,96]{1,0:T(8,128)S(1)} %pad_add_fusion.ints_ref.again_ref, s32[11,96]{1,0:T(8,128)S(1)} %pad_add_fusion.ints_ref.again_ref), custom_call_target="tpu_custom_call" | custom-call | flops 20000000000 | bytes 1000 | tf_op jit(solution)/shard_map/lists/pallas_call | solution.py:274
  8.1 1.3 %rows.1.rows_ref = bf16[96,160,128]{2,1,0:T(8,128)(2,1)S(1)} custom-call(bf16[96,20480]{1,0:T(8,128)(2,1)S(1)} %copy-done, bf16[96,32,128]{2,1,0:T(8,128)(2,1)S(1)} %get-tuple-element.33.after_ref.own_ref), custom_call_target="tpu_custom_call" | custom-call | flops 1000 | bytes 1000 | tf_op jit(solution)/shard_map/rows/pallas_call | solution.py:299
  9.4 1.6 %first.1 = (bf16[27,32,128]{2,1,0:T(8,128)(2,1)S(1)}, bf16[27,32,128]{2,1,0:T(8,128)(2,1)S(1)}, bf16[145,32,128]{2,1,0:T(8,128)(2,1)S(1)}) custom-call(s32[16,128]{1,0:T(8,128)S(1)} %get-tuple-element.30.after_ref.code_ref, s32[4,104]{1,0:T(4,128)S(1)} %get-tuple-element.31.list_ref, s32[4]{0:T(128)S(1)} %get-tuple-element.32.count_ref, ...), custom_call_target="tpu_custom_call" | custom-call | flops 1000 | bytes 1000 | tf_op jit(solution)/shard_map/first/pallas_call | solution.py:310
  11.0 4.3 %collective-permute-start.4 = (bf16[27,32,128]{2,1,0:T(8,128)(2,1)S(1)}, bf16[27,32,128]{2,1,0:T(8,128)(2,1)S(1)}, u32[]{:S(2)}, u32[]{:S(2)}) collective-permute-start(bf16[27,32,128]{2,1,0:T(8,128)(2,1)S(1)} %get-tuple-element.38), channel_id=1, source_target_pairs={{0,2},{2,0},{1,3},{3,1},{4,6},{6,4},{5,7},{7,5},{8,10},{10,8},{9,1... | collective-permute-start | bytes 663560 | tf_op jit(solution)/shard_map/ppermute | solution.py:324
  15.4 2.1 %tables_1.1 = (bf16[27,32,128]{2,1,0:T(8,128)(2,1)S(1)}, bf16[27,32,128]{2,1,0:T(8,128)(2,1)S(1)}, f32[54,32,128]{2,1,0:T(8,128)S(1)}) custom-call(s32[16,128]{1,0:T(8,128)S(1)} %get-tuple-element.30.after_ref.code_ref, s32[4,104]{1,0:T(4,128)S(1)} %get-tuple-element.31.list_ref, s32[4]{0:T(128)S(1)} %get-tuple-element.32.count_ref, ...), custom_call_target="tpu_custom_call" | custom-call | flops 1000 | bytes 1000 | tf_op jit(solution)/shard_map/tables_1/pallas_call | solution.py:347
  17.5 4.1 %collective-permute-done.4.came_ref = bf16[27,32,128]{2,1,0:T(8,128)(2,1)S(1)} collective-permute-done((bf16[27,32,128]{2,1,0:T(8,128)(2,1)S(1)}, bf16[27,32,128]{2,1,0:T(8,128)(2,1)S(1)}, u32[]{:S(2)}, u32[]{:S(2)}) %collective-permute-start.4) | collective-permute-done | bytes 221216 | tf_op jit(solution)/shard_map/ppermute | solution.py:324
  21.6 2.3 %collective-permute-start.6 = (bf16[27,32,128]{2,1,0:T(8,128)(2,1)S(1)}, bf16[27,32,128]{2,1,0:T(8,128)(2,1)S(1)}, u32[]{:S(2)}, u32[]{:S(2)}) collective-permute-start(bf16[27,32,128]{2,1,0:T(8,128)(2,1)S(1)} %add_0.2.after_ref), channel_id=1, source_target_pairs={{0,4},{4,0},{8,12},{12,8},{1,5},{5,1},{9,13},{13,9},{2,6},{6,2},{1... | collective-permute-start | bytes 663560 | tf_op jit(solution)/shard_map/ppermute | solution.py:327
  23.9 1.3 %collective-permute-start.5 = (bf16[27,32,128]{2,1,0:T(8,128)(2,1)S(1)}, bf16[27,32,128]{2,1,0:T(8,128)(2,1)S(1)}, u32[]{:S(2)}, u32[]{:S(2)}) collective-permute-start(bf16[27,32,128]{2,1,0:T(8,128)(2,1)S(1)} %get-tuple-element.43), channel_id=1, source_target_pairs={{0,2},{2,0},{1,3},{3,1},{4,6},{6,4},{5,7},{7,5},{8,10},{10,8},{9,1... | collective-permute-start | bytes 663560 | tf_op jit(solution)/shard_map/ppermute | solution.py:324
  25.2 3.2 %tables_2.1 = (bf16[27,32,128]{2,1,0:T(8,128)(2,1)S(1)}, bf16[27,32,128]{2,1,0:T(8,128)(2,1)S(1)}, f32[54,32,128]{2,1,0:T(8,128)S(1)}) custom-call(s32[16,128]{1,0:T(8,128)S(1)} %get-tuple-element.30.after_ref.code_ref, s32[4,104]{1,0:T(4,128)S(1)} %get-tuple-element.31.list_ref, s32[4]{0:T(128)S(1)} %get-tuple-element.32.count_ref, ...), custom_call_target="tpu_custom_call" | custom-call | flops 1000 | bytes 1000 | tf_op jit(solution)/shard_map/tables_2/pallas_call | solution.py:347
  28.5 1.4 %collective-permute-start.8 = (bf16[27,32,128]{2,1,0:T(8,128)(2,1)S(1)}, bf16[27,32,128]{2,1,0:T(8,128)(2,1)S(1)}, u32[]{:S(2)}, u32[]{:S(2)}) collective-permute-start(bf16[27,32,128]{2,1,0:T(8,128)(2,1)S(1)} %get-tuple-element.45), channel_id=1, source_target_pairs={{0,2},{2,0},{1,3},{3,1},{4,6},{6,4},{5,7},{7,5},{8,10},{10,8},{9,1... | collective-permute-start | bytes 663560 | tf_op jit(solution)/shard_map/ppermute | solution.py:324
  30.0 0.7 %collective-permute-start.11 = (bf16[27,32,128]{2,1,0:T(8,128)(2,1)S(1)}, bf16[27,32,128]{2,1,0:T(8,128)(2,1)S(1)}, u32[]{:S(2)}, u32[]{:S(2)}) collective-permute-start(bf16[27,32,128]{2,1,0:T(8,128)(2,1)S(1)} %get-tuple-element.48), channel_id=1, source_target_pairs={{0,2},{2,0},{1,3},{3,1},{4,6},{6,4},{5,7},{7,5},{8,10},{10,8},{9,1... | collective-permute-start | bytes 663560 | tf_op jit(solution)/shard_map/ppermute | solution.py:324
  30.7 1.2 %collective-permute-done.5.came_ref = bf16[27,32,128]{2,1,0:T(8,128)(2,1)S(1)} collective-permute-done((bf16[27,32,128]{2,1,0:T(8,128)(2,1)S(1)}, bf16[27,32,128]{2,1,0:T(8,128)(2,1)S(1)}, u32[]{:S(2)}, u32[]{:S(2)}) %collective-permute-start.5) | collective-permute-done | bytes 221216 | tf_op jit(solution)/shard_map/ppermute | solution.py:324
  32.0 3.0 %collective-permute-start.7 = (bf16[27,32,128]{2,1,0:T(8,128)(2,1)S(1)}, bf16[27,32,128]{2,1,0:T(8,128)(2,1)S(1)}, u32[]{:S(2)}, u32[]{:S(2)}) collective-permute-start(bf16[27,32,128]{2,1,0:T(8,128)(2,1)S(1)} %add_1.2), channel_id=1, source_target_pairs={{0,8},{4,0},{8,12},{12,4},{1,9},{5,1},{9,13},{13,5},{2,10},{6,2},{... | collective-permute-start | bytes 663560 | tf_op jit(solution)/shard_map/ppermute | solution.py:327
  35.0 4.5 %tables_3.1 = (bf16[54,32,128]{2,1,0:T(8,128)(2,1)S(1)}, f32[54,32,128]{2,1,0:T(8,128)S(1)}, f32[54,32,128]{2,1,0:T(8,128)S(1)}) custom-call(s32[16,128]{1,0:T(8,128)S(1)} %get-tuple-element.30.after_ref.code_ref, s32[4,104]{1,0:T(4,128)S(1)} %get-tuple-element.31.list_ref, s32[4]{0:T(128)S(1)} %get-tuple-element.32.count_ref, ...), custom_call_target="tpu_custom_call" | custom-call | flops 1000 | bytes 1000 | tf_op jit(solution)/shard_map/tables_3/pallas_call | solution.py:347
  39.9 1.8 %collective-permute-start.13 = (bf16[27,32,128]{2,1,0:T(8,128)(2,1)S(1)}, bf16[27,32,128]{2,1,0:T(8,128)(2,1)S(1)}, u32[]{:S(2)}, u32[]{:S(2)}) collective-permute-start(bf16[27,32,128]{2,1,0:T(8,128)(2,1)S(1)} %get-tuple-element.51), channel_id=1, source_target_pairs={{0,2},{2,0},{1,3},{3,1},{4,6},{6,4},{5,7},{7,5},{8,10},{10,8},{9,1... | collective-permute-start | bytes 663560 | tf_op jit(solution)/shard_map/ppermute | solution.py:324
  42.0 3.4 %collective-permute-start.12 = (bf16[27,32,128]{2,1,0:T(8,128)(2,1)S(1)}, bf16[27,32,128]{2,1,0:T(8,128)(2,1)S(1)}, u32[]{:S(2)}, u32[]{:S(2)}) collective-permute-start(bf16[27,32,128]{2,1,0:T(8,128)(2,1)S(1)} %add_2.2), channel_id=1, source_target_pairs={{0,4},{4,12},{8,0},{12,8},{1,5},{5,13},{9,1},{13,9},{2,6},{6,14},{... | collective-permute-start | bytes 663560 | tf_op jit(solution)/shard_map/ppermute | solution.py:327
  45.6 2.6 %collective-permute-done.13.came_ref = bf16[27,32,128]{2,1,0:T(8,128)(2,1)S(1)} collective-permute-done((bf16[27,32,128]{2,1,0:T(8,128)(2,1)S(1)}, bf16[27,32,128]{2,1,0:T(8,128)(2,1)S(1)}, u32[]{:S(2)}, u32[]{:S(2)}) %collective-permute-start.13) | collective-permute-done | bytes 221216 | tf_op jit(solution)/shard_map/ppermute | solution.py:324
  48.3 1.9 %collective-permute-start.14 = (bf16[27,32,128]{2,1,0:T(8,128)(2,1)S(1)}, bf16[27,32,128]{2,1,0:T(8,128)(2,1)S(1)}, u32[]{:S(2)}, u32[]{:S(2)}) collective-permute-start(bf16[27,32,128]{2,1,0:T(8,128)(2,1)S(1)} %add_2.3), channel_id=1, source_target_pairs={{0,4},{4,12},{8,0},{12,8},{1,5},{5,13},{9,1},{13,9},{2,6},{6,14},{... | collective-permute-start | bytes 663560 | tf_op jit(solution)/shard_map/ppermute | solution.py:327
  50.3 1.6 %collective-permute-done.12.rest_1_ = bf16[27,32,128]{2,1,0:T(8,128)(2,1)S(1)} collective-permute-done((bf16[27,32,128]{2,1,0:T(8,128)(2,1)S(1)}, bf16[27,32,128]{2,1,0:T(8,128)(2,1)S(1)}, u32[]{:S(2)}, u32[]{:S(2)}) %collective-permute-start.12) | collective-permute-done | bytes 221216 | tf_op jit(solution)/shard_map/ppermute | solution.py:327
  52.0 3.9 %collective-permute-done.14.rest_2_ = bf16[27,32,128]{2,1,0:T(8,128)(2,1)S(1)} collective-permute-done((bf16[27,32,128]{2,1,0:T(8,128)(2,1)S(1)}, bf16[27,32,128]{2,1,0:T(8,128)(2,1)S(1)}, u32[]{:S(2)}, u32[]{:S(2)}) %collective-permute-start.14) | collective-permute-done | bytes 221216 | tf_op jit(solution)/shard_map/ppermute | solution.py:327
  55.9 1.1 %last.1 = f32[12,32,576]{2,1,0:T(8,128)} custom-call(f32[54,32,128]{2,1,0:T(8,128)S(1)} %gather.1.rest_0_, bf16[27,32,128]{2,1,0:T(8,128)(2,1)S(1)} %collective-permute-done.12.rest_1_, bf16[27,32,128]{2,1,0:T(8,128)(2,1)S(1)} %collective-permute-done.14.rest_2_, bf16[54,32,128]{2,1,0:T(8,128)(2,1)S(1)} %collective-permute-done.15.rest_3_), custom_call_target="tpu_custom_call" | custom-call | flops 1000 | bytes 1000 | tf_op jit(solution)/shard_map/last/pallas_call | solution.py:399
  (29 shorter events, 3.3 us)
Async XLA Ops:
  0.0 7.3 %collective-permute-start = (bf16[32,6144]{1,0:T(8,128)(2,1)}, bf16[32,6144]{1,0:T(8,128)(2,1)S(1)}, u32[]{:S(2)}, u32[]{:S(2)}) collective-permute-start(bf16[32,6144]{1,0:T(8,128)(2,1)} %cells_ref.1), channel_id=1, source_target_pairs={{0,1},{1,0},{2,3},{3,2},{4,5},{5,4},{6,7},{7,6},{8,9},{9,8},{10,11... | collective-permute-start | bytes 1179656 | tf_op jit(solution)/shard_map/ppermute | solution.py:269
  1.4 7.9 %collective-permute-start.2 = (bf16[32,1536]{1,0:T(8,128)(2,1)S(1)}, bf16[32,1536]{1,0:T(8,128)(2,1)S(1)}, u32[]{:S(2)}, u32[]{:S(2)}) collective-permute-start(bf16[32,1536]{1,0:T(8,128)(2,1)S(1)} %get-tuple-element.55), channel_id=1, source_target_pairs={{0,2},{4,6},{8,10},{12,14},{2,0},{6,4},{10,8},{14,12},{1,3},{5,7},... | collective-permute-start | bytes 294920 | tf_op jit(solution)/shard_map/ppermute | solution.py:47
  4.0 5.4 %collective-permute-start.1 = (bf16[32,1536]{1,0:T(8,128)(2,1)S(1)}, bf16[32,1536]{1,0:T(8,128)(2,1)S(1)}, u32[]{:S(2)}, u32[]{:S(2)}) collective-permute-start(bf16[32,1536]{1,0:T(8,128)(2,1)S(1)} %get-tuple-element.56), channel_id=1, source_target_pairs={{2,4},{6,8},{10,12},{4,2},{8,6},{12,10},{3,5},{7,9},{11,13},{5,3},... | collective-permute-start | bytes 294920 | tf_op jit(solution)/shard_map/ppermute | solution.py:47
  5.4 2.0 %copy-start.1 = (bf16[32,6144]{1,0:T(8,128)(2,1)S(1)}, bf16[32,6144]{1,0:T(8,128)(2,1)}, u32[]{:S(2)}) copy-start(bf16[32,6144]{1,0:T(8,128)(2,1)} %cells_ref.1) | copy-start | bytes 1179652
  5.4 2.7 %copy-start = (bf16[96,20480]{1,0:T(8,128)(2,1)S(1)}, bf16[96,20480]{1,0:T(8,128)(2,1)}, u32[]{:S(2)}) copy-start(bf16[96,20480]{1,0:T(8,128)(2,1)} %jac_ref.1) | copy-start | bytes 11796484
  11.0 10.6 %collective-permute-start.4 = (bf16[27,32,128]{2,1,0:T(8,128)(2,1)S(1)}, bf16[27,32,128]{2,1,0:T(8,128)(2,1)S(1)}, u32[]{:S(2)}, u32[]{:S(2)}) collective-permute-start(bf16[27,32,128]{2,1,0:T(8,128)(2,1)S(1)} %get-tuple-element.38), channel_id=1, source_target_pairs={{0,2},{2,0},{1,3},{3,1},{4,6},{6,4},{5,7},{7,5},{8,10},{10,8},{9,1... | collective-permute-start | bytes 663560 | tf_op jit(solution)/shard_map/ppermute | solution.py:324
  15.3 13.2 %collective-permute-start.3 = (bf16[27,32,128]{2,1,0:T(8,128)(2,1)S(1)}, bf16[27,32,128]{2,1,0:T(8,128)(2,1)S(1)}, u32[]{:S(2)}, u32[]{:S(2)}) collective-permute-start(bf16[27,32,128]{2,1,0:T(8,128)(2,1)S(1)} %get-tuple-element.37), channel_id=1, source_target_pairs={{0,2},{2,0},{1,3},{3,1},{4,6},{6,4},{5,7},{7,5},{8,10},{10,8},{9,1... | collective-permute-start | bytes 663560 | tf_op jit(solution)/shard_map/ppermute | solution.py:324
  21.6 8.4 %collective-permute-start.6 = (bf16[27,32,128]{2,1,0:T(8,128)(2,1)S(1)}, bf16[27,32,128]{2,1,0:T(8,128)(2,1)S(1)}, u32[]{:S(2)}, u32[]{:S(2)}) collective-permute-start(bf16[27,32,128]{2,1,0:T(8,128)(2,1)S(1)} %add_0.2.after_ref), channel_id=1, source_target_pairs={{0,4},{4,0},{8,12},{12,8},{1,5},{5,1},{9,13},{13,9},{2,6},{6,2},{1... | collective-permute-start | bytes 663560 | tf_op jit(solution)/shard_map/ppermute | solution.py:327
  23.9 8.0 %collective-permute-start.5 = (bf16[27,32,128]{2,1,0:T(8,128)(2,1)S(1)}, bf16[27,32,128]{2,1,0:T(8,128)(2,1)S(1)}, u32[]{:S(2)}, u32[]{:S(2)}) collective-permute-start(bf16[27,32,128]{2,1,0:T(8,128)(2,1)S(1)} %get-tuple-element.43), channel_id=1, source_target_pairs={{0,2},{2,0},{1,3},{3,1},{4,6},{6,4},{5,7},{7,5},{8,10},{10,8},{9,1... | collective-permute-start | bytes 663560 | tf_op jit(solution)/shard_map/ppermute | solution.py:324
  28.5 11.0 %collective-permute-start.8 = (bf16[27,32,128]{2,1,0:T(8,128)(2,1)S(1)}, bf16[27,32,128]{2,1,0:T(8,128)(2,1)S(1)}, u32[]{:S(2)}, u32[]{:S(2)}) collective-permute-start(bf16[27,32,128]{2,1,0:T(8,128)(2,1)S(1)} %get-tuple-element.45), channel_id=1, source_target_pairs={{0,2},{2,0},{1,3},{3,1},{4,6},{6,4},{5,7},{7,5},{8,10},{10,8},{9,1... | collective-permute-start | bytes 663560 | tf_op jit(solution)/shard_map/ppermute | solution.py:324
  29.9 9.6 %collective-permute-start.9 = (bf16[27,32,128]{2,1,0:T(8,128)(2,1)S(1)}, bf16[27,32,128]{2,1,0:T(8,128)(2,1)S(1)}, u32[]{:S(2)}, u32[]{:S(2)}) collective-permute-start(bf16[27,32,128]{2,1,0:T(8,128)(2,1)S(1)} %add_0.3.after_ref), channel_id=1, source_target_pairs={{0,4},{4,0},{8,12},{12,8},{1,5},{5,1},{9,13},{13,9},{2,6},{6,2},{1... | collective-permute-start | bytes 663560 | tf_op jit(solution)/shard_map/ppermute | solution.py:327
  30.0 9.9 %collective-permute-start.11 = (bf16[27,32,128]{2,1,0:T(8,128)(2,1)S(1)}, bf16[27,32,128]{2,1,0:T(8,128)(2,1)S(1)}, u32[]{:S(2)}, u32[]{:S(2)}) collective-permute-start(bf16[27,32,128]{2,1,0:T(8,128)(2,1)S(1)} %get-tuple-element.48), channel_id=1, source_target_pairs={{0,2},{2,0},{1,3},{3,1},{4,6},{6,4},{5,7},{7,5},{8,10},{10,8},{9,1... | collective-permute-start | bytes 663560 | tf_op jit(solution)/shard_map/ppermute | solution.py:324
  32.0 9.7 %collective-permute-start.7 = (bf16[27,32,128]{2,1,0:T(8,128)(2,1)S(1)}, bf16[27,32,128]{2,1,0:T(8,128)(2,1)S(1)}, u32[]{:S(2)}, u32[]{:S(2)}) collective-permute-start(bf16[27,32,128]{2,1,0:T(8,128)(2,1)S(1)} %add_1.2), channel_id=1, source_target_pairs={{0,8},{4,0},{8,12},{12,4},{1,9},{5,1},{9,13},{13,5},{2,10},{6,2},{... | collective-permute-start | bytes 663560 | tf_op jit(solution)/shard_map/ppermute | solution.py:327
  39.6 6.0 %collective-permute-start.10 = (bf16[27,32,128]{2,1,0:T(8,128)(2,1)S(1)}, bf16[27,32,128]{2,1,0:T(8,128)(2,1)S(1)}, u32[]{:S(2)}, u32[]{:S(2)}) collective-permute-start(bf16[27,32,128]{2,1,0:T(8,128)(2,1)S(1)} %add_1.3), channel_id=1, source_target_pairs={{0,8},{4,0},{8,12},{12,4},{1,9},{5,1},{9,13},{13,5},{2,10},{6,2},{... | collective-permute-start | bytes 663560 | tf_op jit(solution)/shard_map/ppermute | solution.py:327
  39.9 8.4 %collective-permute-start.13 = (bf16[27,32,128]{2,1,0:T(8,128)(2,1)S(1)}, bf16[27,32,128]{2,1,0:T(8,128)(2,1)S(1)}, u32[]{:S(2)}, u32[]{:S(2)}) collective-permute-start(bf16[27,32,128]{2,1,0:T(8,128)(2,1)S(1)} %get-tuple-element.51), channel_id=1, source_target_pairs={{0,2},{2,0},{1,3},{3,1},{4,6},{6,4},{5,7},{7,5},{8,10},{10,8},{9,1... | collective-permute-start | bytes 663560 | tf_op jit(solution)/shard_map/ppermute | solution.py:324
  41.7 14.2 %collective-permute-start.15 = (bf16[54,32,128]{2,1,0:T(8,128)(2,1)S(1)}, bf16[54,32,128]{2,1,0:T(8,128)(2,1)S(1)}, u32[]{:S(2)}, u32[]{:S(2)}) collective-permute-start(bf16[54,32,128]{2,1,0:T(8,128)(2,1)S(1)} %get-tuple-element.54), channel_id=1, source_target_pairs={{0,2},{2,0},{1,3},{3,1},{4,6},{6,4},{5,7},{7,5},{8,10},{10,8},{9,1... | collective-permute-start | bytes 1327112 | tf_op jit(solution)/shard_map/ppermute | solution.py:324
  42.0 10.0 %collective-permute-start.12 = (bf16[27,32,128]{2,1,0:T(8,128)(2,1)S(1)}, bf16[27,32,128]{2,1,0:T(8,128)(2,1)S(1)}, u32[]{:S(2)}, u32[]{:S(2)}) collective-permute-start(bf16[27,32,128]{2,1,0:T(8,128)(2,1)S(1)} %add_2.2), channel_id=1, source_target_pairs={{0,4},{4,12},{8,0},{12,8},{1,5},{5,13},{9,1},{13,9},{2,6},{6,14},{... | collective-permute-start | bytes 663560 | tf_op jit(solution)/shard_map/ppermute | solution.py:327
  48.3 7.6 %collective-permute-start.14 = (bf16[27,32,128]{2,1,0:T(8,128)(2,1)S(1)}, bf16[27,32,128]{2,1,0:T(8,128)(2,1)S(1)}, u32[]{:S(2)}, u32[]{:S(2)}) collective-permute-start(bf16[27,32,128]{2,1,0:T(8,128)(2,1)S(1)} %add_2.3), channel_id=1, source_target_pairs={{0,4},{4,12},{8,0},{12,8},{1,5},{5,13},{9,1},{13,9},{2,6},{6,14},{... | collective-permute-start | bytes 663560 | tf_op jit(solution)/shard_map/ppermute | solution.py:327
